TPU v7x, 32 devices: a whole 2x2x4 slice. The times are simulated.
32 devices in a mesh: gx: 2 (over x), gy: 4 (over y, core), row: 4 (over z).
Axes of the slice: x: 2, y: 2, z: 4, core: 2. Of those that a mesh axis runs over, the one named last changes fastest.
Arguments:
- tokens: bfloat16 [4, 896, 1664], P('row', 'gx', 'gy'), may hold values from -6 to 6
- segments: int32 [4, 896], P('row'), may hold values from 0 to 7, never falling along the last dimension, each value on 1 to 672 neighbouring positions
- gain_attn: float32 [1664], replicated, may hold values from 0.1 to 1.9
- w_query: bfloat16 [1664, 1664], P('gx', 'gy'), as said below
- w_key: bfloat16 [1664, 1664], P('gx', 'gy'), as said below
- w_value: bfloat16 [1664, 1664], P('gx', 'gy'), may hold values from -0.15625 to 0.15625
- w_out: bfloat16 [1664, 1664], P('gy'), may hold values from -0.15625 to 0.15625
- gain_mlp: float32 [1664], replicated, may hold values from 0.1 to 1.9
- w_up: bfloat16 [1664, 8192], P('gx', 'gy'), may hold values from -0.15625 to 0.15625
- w_down: bfloat16 [8192, 1664], P('gy', 'gx'), may hold values from -0.0625 to 0.0625
- w_merge: bfloat16 [4, 1664, 1664], P(None, 'gy', 'gx'), may hold values from -0.078125 to 0.078125
- merge_groups: int32 [4, 224, 4], P('row', 'gx'), may hold values from 0 to 447, as said below
- sources: int32 [4, 224], P('row', 'gx'), may hold values from 0 to 447, as said below
Outputs:
- layer_out: bfloat16 [4, 896, 1664], P('row', 'gx', 'gy')
- returned: bfloat16 [4, 224, 1664], P('row', 'gx', 'gy')
Inputs may be any that keep to these rules, and one draw needn't show every extreme that they name: `segments`: ids never fall along a row group's tokens; each of the 8 ids holds 1 to 672 tokens, one exactly 672. `merge_groups`: for every row group and every block of 112 merged rows (one index of gx), the four positions of all its groups name each of 0 to 447 exactly once. `sources`: for every block b of 112 merged rows, the values over all row groups at that block name each of 0 to 447 exactly once. `w_query`: a real matrix whose entries lie within -161.2 and 161.2 over the square root of 1664. `w_key`: a real matrix whose entries lie within -4 and 4 over the square root of 1664.
All inputs are finite; a program needn't handle non-finite values.
Results may differ from a plain program's by a relative error of at most 0.029.
Values may be sent and summed in bfloat16 or wider, within the bound.
No kernel may reach another device: no remote copies, remote signals or barrier semaphores. Data moves between devices by JAX's collectives and lax.ppermute only.
A program may use at most 64 MiB of HBM per device.

v0:
```python
import jax
import jax.numpy as jnp
from jax import lax
from jax.sharding import PartitionSpec as P

HD = 104


EPS = 1e-06
NEG = -1e30


def normalize(tok_rows, gain):
    tok_rows = tok_rows.astype(jnp.float32)
    row_mean = jnp.mean(tok_rows, axis=-1, keepdims=True)
    centred = tok_rows - row_mean
    row_var = jnp.mean(centred * centred, axis=-1, keepdims=True)
    return (centred * lax.rsqrt(row_var + EPS) * gain).astype(jnp.bfloat16)


def body(
    tokens,
    segments,
    gain_attn,
    w_query,
    w_key,
    w_value,
    w_out,
    gain_mlp,
    w_up,
    w_down,
    w_merge,
    merge_groups,
    sources,
):
    tok_local = tokens[0]
    row_count = tok_local.shape[0]
    seg_all = segments[0]
    col_count = w_query.shape[1]
    head_count = col_count // HD
    scale = HD ** (-0.5)
    gathered = lax.all_gather(tok_local, "gy", axis=1, tiled=True)
    normed = normalize(gathered, gain_attn)
    pieces = (
        lax.all_gather(w_query, "gx", axis=0, tiled=True),
        lax.all_gather(w_key, "gx", axis=0, tiled=True),
        lax.all_gather(w_value, "gx", axis=0, tiled=True),
    )
    feat_part = normed
    q_sum = jnp.dot(feat_part, pieces[0], preferred_element_type=jnp.float32)
    k_sum = jnp.dot(feat_part, pieces[1], preferred_element_type=jnp.float32)
    v_sum = jnp.dot(feat_part, pieces[2], preferred_element_type=jnp.float32)
    queries = q_sum.astype(jnp.bfloat16).reshape(row_count, head_count, HD)
    key_rows = k_sum.astype(jnp.bfloat16)
    value_rows = v_sum.astype(jnp.bfloat16)
    own_seg = lax.dynamic_slice_in_dim(seg_all, lax.axis_index("gx") * row_count, row_count)
    start_state = (
        jnp.full((row_count, head_count), NEG, jnp.float32),
        jnp.zeros((row_count, head_count), jnp.float32),
        jnp.zeros((row_count, head_count, HD), jnp.float32),
    )
    pieces = (
        lax.all_gather(key_rows, "gx", axis=0, tiled=True),
        lax.all_gather(value_rows, "gx", axis=0, tiled=True),
    )
    key_count = pieces[0].shape[0]
    block_len = min(row_count, key_count)
    block_total = key_count // block_len

    def one_block(step, old):
        block_keys = lax.dynamic_slice_in_dim(pieces[0], step * block_len, block_len, 0)
        block_values = lax.dynamic_slice_in_dim(pieces[1], step * block_len, block_len, 0)
        key_seg = lax.dynamic_slice_in_dim(seg_all, step * block_len, block_len)
        row_top, row_total, weighted = old
        key_heads = block_keys.reshape(block_len, head_count, HD)
        value_heads = block_values.reshape(block_len, head_count, HD)
        scores = (
            jnp.einsum("qhd,khd->qhk", queries, key_heads, preferred_element_type=jnp.float32)
            * scale
        )
        same_seg = (own_seg[:, None] == key_seg[None, :])[:, None, :]
        scores = jnp.where(same_seg, scores, NEG)
        new_top = jnp.maximum(row_top, jnp.max(scores, axis=-1))
        weights = jnp.where(same_seg, jnp.exp(scores - new_top[:, :, None]), 0.0)
        rescale = jnp.exp(row_top - new_top)
        row_total = row_total * rescale + jnp.sum(weights, axis=-1)
        weighted = weighted * rescale[:, :, None] + jnp.einsum(
            "qhk,khd->qhd",
            weights.astype(jnp.bfloat16),
            value_heads,
            preferred_element_type=jnp.float32,
        )
        return (new_top, row_total, weighted)

    row_top, row_total, weighted = lax.fori_loop(0, block_total, one_block, start_state)
    attended = (weighted / row_total[:, :, None]).reshape(row_count, col_count).astype(jnp.bfloat16)
    out_cols = lax.all_to_all(w_out, "gy", split_axis=1, concat_axis=0, tiled=True)
    attn_out = jnp.dot(
        lax.all_gather(attended, "gy", axis=1, tiled=True),
        out_cols,
        preferred_element_type=jnp.float32,
    )
    after_attn = (tok_local.astype(jnp.float32) + attn_out).astype(jnp.bfloat16)
    gathered_mlp = lax.all_gather(after_attn, "gy", axis=1, tiled=True)
    normed_mlp = normalize(gathered_mlp, gain_mlp)
    feat_part = normed_mlp
    hidden_sum = jnp.dot(
        feat_part,
        lax.all_gather(w_up, "gx", axis=0, tiled=True),
        preferred_element_type=jnp.float32,
    )
    hidden = jax.nn.gelu(hidden_sum, approximate=False).astype(jnp.bfloat16)
    partials = jnp.dot(
        hidden, lax.all_gather(w_down, "gx", axis=1, tiled=True), preferred_element_type=jnp.float32
    )
    mlp_out = lax.psum_scatter(
        partials.astype(jnp.bfloat16), "gy", scatter_dimension=1, tiled=True
    ).astype(jnp.float32)
    after_mlp = (after_attn.astype(jnp.float32) + mlp_out).astype(jnp.bfloat16)
    picked = after_mlp[merge_groups[0]]
    merge_terms = jnp.einsum(
        "mkc,kcn->mn",
        picked,
        lax.all_gather(w_merge, "gx", axis=2, tiled=True),
        preferred_element_type=jnp.float32,
    )
    merged = lax.psum_scatter(
        merge_terms.astype(jnp.bfloat16), "gy", scatter_dimension=1, tiled=True
    )
    pooled = lax.all_gather(merged[None], "row", axis=0, tiled=True)
    stacked = pooled.reshape(-1, merged.shape[1])
    returned = stacked[sources[0]]
    return (after_mlp[None], returned[None])


def solution(mesh):
    placed = (
        P("row", "gx", "gy"),
        P("row", None),
        P(),
        P("gx", "gy"),
        P("gx", "gy"),
        P("gx", "gy"),
        P("gy", None),
        P(),
        P("gx", "gy"),
        P("gy", "gx"),
        P(None, "gy", "gx"),
        P("row", "gx", None),
        P("row", "gx"),
    )
    return jax.shard_map(
        body,
        mesh=mesh,
        in_specs=placed,
        out_specs=(P("row", "gx", "gy"), P("row", "gx", "gy")),
        check_vma=False,
    )
```

profile of v0, /device:TPU:0, one launch (start us, length us, event | category | flops | bytes accessed | tf_op | source)
XLA Modules:
  0.0 599.0 jit_solution(1316885208257912423)
XLA Ops:
  10.7 0.8 constant_dynamic-slice_fusion.2
  11.5 27.0 %all-gather.30.cloned.1.call-done = bf16[2,832,416]{1,2,0:T(8,128)(2,1)} async-done(((bf16[1,832,416]{1,2,0:T(8,128)(2,1)}), bf16[2,832,416]{1,2,0:T(8,128)(2,1)}) %all-gather.30.cloned.1.call-update) | async-done | bytes 1384464 | tf_op jit(solution)/shard_map/all_gather | solution.py:46
  38.6 2.5 copy.33
  41.1 1.0 reshape.163
  42.1 24.3 %all-gather.34.cloned.1.call-done = bf16[2,832,416]{1,2,0:T(8,128)(2,1)} async-done(((bf16[1,832,416]{1,2,0:T(8,128)(2,1)}), bf16[2,832,416]{1,2,0:T(8,128)(2,1)}) %all-gather.34.cloned.1.call-update) | async-done | bytes 1384464 | tf_op jit(solution)/shard_map/all_gather | solution.py:47
  66.4 2.5 copy.36
  69.0 1.9 reshape.169
  70.8 23.5 %all-gather.32.cloned.1.call-done = bf16[2,832,416]{1,2,0:T(8,128)(2,1)} async-done(((bf16[1,832,416]{1,2,0:T(8,128)(2,1)}), bf16[2,832,416]{1,2,0:T(8,128)(2,1)}) %all-gather.32.cloned.1.call-update) | async-done | bytes 1384464 | tf_op jit(solution)/shard_map/all_gather | solution.py:45
  94.3 2.5 copy.35
  96.8 1.9 reshape.167
  98.7 17.4 %all-gather.28.cloned.1.call-done = bf16[1,448,1664]{1,2,0:T(8,128)(2,1)} async-done(((bf16[1,448,416]{1,2,0:T(8,128)(2,1)}), bf16[1,448,1664]{1,2,0:T(8,128)(2,1)}) %all-gather.28.cloned.1.call-update) | async-done | bytes 1490960 | tf_op jit(solution)/shard_map/all_gather | solution.py:42
  116.1 1.8 convert_reduce_fusion
  117.9 2.0 fusion.36
  119.9 2.5 fusion.87
  122.4 12.8 %all-gather.3 = bf16[2,448,416]{1,2,0:T(8,128)(2,1)S(1)} all-gather(bf16[1,448,416]{1,2,0:T(8,128)(2,1)S(1)} %fusion.87), channel_id=1, replica_groups=mesh['gx'=2,'gy'=4,'row'=4] {'gx'}, dimensions={0}, use_global_device_ids=true | all-gather | bytes 1118208 | tf_op jit(solution)/shard_map/all_gather | solution.py:63
  135.2 0.9 copy.34
  136.7 2.4 fusion.88
  139.1 12.0 %all-gather.6 = bf16[2,448,416]{1,2,0:T(8,128)(2,1)S(1)} all-gather(bf16[1,448,416]{1,2,0:T(8,128)(2,1)S(1)} %fusion.88), channel_id=1, replica_groups=mesh['gx'=2,'gy'=4,'row'=4] {'gx'}, dimensions={0}, use_global_device_ids=true | all-gather | bytes 1118208 | tf_op jit(solution)/shard_map/all_gather | solution.py:64
  151.1 0.9 copy.37
  152.6 3.0 convolution_convert_fusion.2
  155.6 15.7 %while.18 = (s32[]{:T(128)}, f32[448,4]{0,1:T(4,128)S(1)}, f32[448,4]{0,1:T(4,128)S(1)}, f32[448,4,104]{0,2,1:T(8,128)S(1)}, s32[448]{0:T(512)S(1)}, /*index=5*/...) while((s32[]{:T(128)}, f32[448,4]{0,1:T(4,128)S(1)}, ...), condition=%wide.region_5.6_spmd.clone, body=%wide.region_2.5_spmd.clone.sunk | while | flops 345176832 | bytes 27503832 | solution.py:95
  156.3 2.7 fusion.146
  159.0 3.1 fusion.147
  162.2 1.3 fusion.149
  164.1 2.7 fusion.146
  166.8 3.1 fusion.147
  170.0 1.3 fusion.149
  171.3 0.9 divide_convert_fusion
  172.3 2.8 copy.38
  175.0 33.1 %all_to_all.19 = bf16[416,4,416]{0,2,1:T(8,128)(2,1)S(1)} all-to-all(bf16[416,4,416]{0,2,1:T(8,128)(2,1)S(1)} %bitcast.112), channel_id=1, replica_groups=mesh['gx'=2,'gy'=4,'row'=4] {'gy'}, dimensions={1} | all-to-all | bytes 2768896 | tf_op jit(solution)/shard_map/all_to_all | solution.py:97
  208.1 1.3 copy.39
  209.4 1.6 all_to_all.17
  211.1 3.1 fusion.86
  216.0 18.8 %all-gather.20.cloned.1.call-done = bf16[448,1664]{0,1:T(8,128)(2,1)} async-done(((bf16[448,416]{0,1:T(8,128)(2,1)}), bf16[448,1664]{0,1:T(8,128)(2,1)}) %all-gather.20.cloned.1.call-update) | async-done | bytes 1490960 | tf_op jit(solution)/shard_map/all_gather | solution.py:104
  234.8 1.8 convert_reduce_fusion.1
  236.6 2.0 fusion.30
  238.6 84.1 %all-gather.22.cloned.1.call-done = bf16[1664,2048]{1,0:T(8,128)(2,1)} async-done(((bf16[832,2048]{1,0:T(8,128)(2,1)}), bf16[1664,2048]{1,0:T(8,128)(2,1)}) %all-gather.22.cloned.1.call-update) | async-done | bytes 6815760 | tf_op jit(solution)/shard_map/all_gather | solution.py:109
  322.7 87.9 %all-gather.24.cloned.1.call-done = bf16[2048,1664]{0,1:T(8,128)(2,1)} async-done(((bf16[2048,832]{0,1:T(8,128)(2,1)}), bf16[2048,1664]{0,1:T(8,128)(2,1)}) %all-gather.24.cloned.1.call-update) | async-done | bytes 6815760 | tf_op jit(solution)/shard_map/all_gather | solution.py:114
  410.5 20.5 %convolution_convert_fusion = bf16[448,1664]{0,1:T(8,128)(2,1)} fusion(bf16[2048,1664]{0,1:T(8,128)(2,1)} %all-gather.24.cloned.1.call-done, bf16[1664,2048]{1,0:T(8,128)(2,1)} %all-gather.22.cloned.1.call-done, bf16[448,1664]{0,1:T(8,128)(2,1)} %all-gather.20.cloned.1.call-done, f32[1664]{0:T(1024)S(1)} %copy-done.9, f32[448]{0:T(512)S(1)} %add_rsqrt_fusion, ...), kind=kOutput, calls=%fused_computation.58 | convolution fusion | flops 6171017216 | bytes 16623616 | tf_op jit(solution)/shard_map/dot_general | solution.py:113
  431.2 5.0 copy.42
  436.5 23.7 %reduce-scatter.3.cloned.1.call-done = bf16[448,416]{0,1:T(8,128)(2,1)} async-done(((bf16[448,1664]{0,1:T(8,128)(2,1)}), bf16[448,416]{0,1:T(8,128)(2,1)}) %reduce-scatter.3.cloned.1.call-update) | async-done | bytes 372752 | tf_op jit(solution)/shard_map/reduce_scatter | solution.py:116
  460.2 1.1 add_convert_fusion
  461.6 2.1 gather_fusion
  463.8 84.2 %all-gather.26.cloned.1.call-done = bf16[4,416,1664]{1,0,2:T(4,128)(2,1)} async-done(((bf16[4,416,832]{1,0,2:T(4,128)(2,1)}), bf16[4,416,1664]{1,0,2:T(4,128)(2,1)}) %all-gather.26.cloned.1.call-update) | async-done | bytes 5537808 | tf_op jit(solution)/shard_map/all_gather | solution.py:124
  548.0 6.1 %fusion.42 = bf16[112,1664]{0,1:T(8,128)(2,1)} fusion(bf16[4,416,1664]{1,0,2:T(4,128)(2,1)} %all-gather.26.cloned.1.call-done, bf16[112,4,416]{2,1,0:T(4,128)(2,1)S(1)} %reshape.141), kind=kOutput, calls=%fused_computation.60 | convolution fusion | flops 620419072 | bytes 6283264 | tf_op jit(solution)/shard_map/mkc,kcn->mn/dot_general | solution.py:121
  554.1 21.2 %reduce-scatter.5.cloned.1.call-done = bf16[112,416]{0,1:T(8,128)(2,1)} async-done(((bf16[112,1664]{0,1:T(8,128)(2,1)}), bf16[112,416]{0,1:T(8,128)(2,1)}) %reduce-scatter.5.cloned.1.call-update) | async-done | bytes 93200 | tf_op jit(solution)/shard_map/reduce_scatter | solution.py:127
  575.3 15.0 %all-gather.7 = bf16[4,112,416]{1,2,0:T(8,128)(2,1)S(1)} all-gather(bf16[1,112,416]{1,2,0:T(8,128)(2,1)} %bitcast.121), channel_id=3, replica_groups=mesh['gx'=2,'gy'=4,'row'=4] {'row'}, dimensions={0}, use_global_device_ids=true | all-gather | bytes 465920 | tf_op jit(solution)/shard_map/all_gather | solution.py:130
  590.5 0.8 gather_fusion.1
  (79 shorter events, 9.7 us)
Async XLA Ops:
  7.2 31.4 %all-gather.30.cloned.1.call-start = ((), (), s32[]{:S(2)}) async-start(), calls=%async_computation.11 | async-start | bytes 2236416 | tf_op jit(solution)/shard_map/all_gather | solution.py:46
  7.9 58.5 %all-gather.34.cloned.1.call-start = ((), (), s32[]{:S(2)}) async-start(), calls=%async_computation.13 | async-start | bytes 2236416 | tf_op jit(solution)/shard_map/all_gather | solution.py:47
  8.6 85.6 %all-gather.32.cloned.1.call-start = ((), (), s32[]{:S(2)}) async-start(), calls=%async_computation.12 | async-start | bytes 2236416 | tf_op jit(solution)/shard_map/all_gather | solution.py:45
  9.4 106.8 %all-gather.28.cloned.1.call-start = ((), (), s32[]{:S(2)}) async-start(), calls=%async_computation.10 | async-start | bytes 2129920 | tf_op jit(solution)/shard_map/all_gather | solution.py:42
  10.0 201.1 %all-gather.18.cloned.1.call-start = ((), (), s32[]{:S(2)}) async-start(), calls=%async_computation.3 | async-start | bytes 2129920 | tf_op jit(solution)/shard_map/all_gather | solution.py:99
  96.8 23.1 %copy-start.8 = (f32[1664]{0:T(1024)S(1)}, f32[1664]{0:T(1024)}, u32[]{:S(2)}) copy-start(f32[1664]{0:T(1024)} %param.17) | copy-start | bytes 19972
  122.4 14.3 %copy-start.1 = (bf16[1,448,1664]{1,2,0:T(8,128)(2,1)S(1)}, bf16[1,448,1664]{1,2,0:T(8,128)(2,1)}, u32[]{:S(2)}) copy-start(bf16[1,448,1664]{1,2,0:T(8,128)(2,1)} %all-gather.28.cloned.1.call-done) | copy-start | bytes 4472836
  152.6 3.0 copy-start.5
  159.0 3.2 copy-start
  166.8 3.2 copy-start
  172.2 62.6 %all-gather.20.cloned.1.call-start = ((), (), s32[]{:S(2)}) async-start(), calls=%async_computation.4 | async-start | bytes 2129920 | tf_op jit(solution)/shard_map/all_gather | solution.py:104
  208.1 3.0 copy-start.6
  214.2 108.4 %all-gather.22.cloned.1.call-start = ((), (), s32[]{:S(2)}) async-start(), calls=%async_computation.5 | async-start | bytes 10223616 | tf_op jit(solution)/shard_map/all_gather | solution.py:109
  215.0 195.5 %copy-start.9 = (f32[1664]{0:T(1024)S(1)}, f32[1664]{0:T(1024)}, u32[]{:S(2)}) copy-start(f32[1664]{0:T(1024)} %param.22) | copy-start | bytes 19972
  215.0 195.5 %all-gather.24.cloned.1.call-start = ((), (), s32[]{:S(2)}) async-start(), calls=%async_computation.6 | async-start | bytes 10223616 | tf_op jit(solution)/shard_map/all_gather | solution.py:114
  215.7 244.5 %reduce-scatter.3.cloned.1.call-start = ((), (), s32[]{:S(2)}) async-start(), calls=%async_computation.7 | async-start | bytes 2129920 | tf_op jit(solution)/shard_map/reduce_scatter | solution.py:116
  410.5 20.6 %copy-start.2 = (bf16[4,416,832]{2,1,0:T(8,128)(2,1)S(1)}, bf16[4,416,832]{2,1,0:T(8,128)(2,1)}, u32[]{:S(2)}) copy-start(bf16[4,416,832]{2,1,0:T(8,128)(2,1)} %param.25) | copy-start | bytes 8306692
  431.1 5.2 copy-start.7
  431.1 29.1 %copy-start.4 = (bf16[448,416]{0,1:T(8,128)(2,1)S(1)}, bf16[448,416]{0,1:T(8,128)(2,1)}, u32[]{:S(2)}) copy-start(bf16[448,416]{0,1:T(8,128)(2,1)} %fusion.86) | copy-start | bytes 1118212
  431.1 116.9 %all-gather.26.cloned.1.call-start = ((), (), s32[]{:S(2)}) async-start(), calls=%async_computation.8 | async-start | bytes 10223616 | tf_op jit(solution)/shard_map/all_gather | solution.py:124
  436.2 139.1 %reduce-scatter.5.cloned.1.call-start = ((), (), s32[]{:S(2)}) async-start(), calls=%async_computation.9 | async-start | bytes 532480 | tf_op jit(solution)/shard_map/reduce_scatter | solution.py:127
  461.3 92.7 %copy-start.3 = (bf16[448,416]{0,1:T(8,128)(2,1)}, bf16[448,416]{0,1:T(8,128)(2,1)S(1)}, u32[]{:S(2)}) copy-start(bf16[448,416]{0,1:T(8,128)(2,1)S(1)} %add_convert_fusion) | copy-start | bytes 1118212
  463.8 90.3 %copy-start.10 = (s32[1,112]{1,0:T(1,128)S(1)}, s32[1,112]{1,0:T(1,128)}, u32[]{:S(2)}) copy-start(s32[1,112]{1,0:T(1,128)} %param.27) | copy-start | bytes 1348
Sparse Core Ops, SparseCore 0:
  9.5 28.9 all-gather.29
  40.1 26.2 all-gather.33
  68.0 26.2 all-gather.31
  95.7 20.3 all-gather.27
  172.3 29.4 all-gather.17
  214.4 20.4 all-gather.19
  236.3 86.2 all-gather.21
  324.2 86.2 all-gather.23
  431.2 28.9 reduce-scatter.2
  461.7 86.2 all-gather.25
  554.2 21.0 reduce-scatter.4
where the time goes:
time: 607 us; the launch traced here: 599 us
  waiting for transfers between devices  416 us (69%)
  blocking collectives  72.8 us (12%)
  matrix products  45.5 us (7%)
  local copies, waits for them, and re-layouts  32.3 us (5%)
  other arithmetic  17 us (3%)
  between operations  14.6 us (2%)
    all_gather x1, waiting for transfers between devices, body(): lax.all_gather(w_down, 'gx', axis=1, tiled=True)  87.9 us
    all_gather x1, waiting for transfers between devices, body(): lax.all_gather(w_merge, 'gx', axis=2, tiled=True)  84.2 us
    all_gather x1, waiting for transfers between devices, body(): lax.all_gather(w_up, 'gx', axis=0, tiled=True)  84.1 us
    all_to_all x1, blocking collectives, body(): lax.all_to_all(w_out, 'gy', split_axis=1, concat_axis=0, tiled=True)  33.1 us
    all_gather x1, waiting for transfers between devices, body(): lax.all_gather(w_key, 'gx', axis=0, tiled=True)  27 us
    all_gather x1, waiting for transfers between devices, body(): lax.all_gather(w_value, 'gx', axis=0, tiled=True)  24.3 us
    reduce_scatter x1, waiting for transfers between devices, body(): lax.psum_scatter(partials.astype(jnp.bfloat16), 'gy', scatter_dimension=1...  23.7 us
    all_gather x1, waiting for transfers between devices, body(): lax.all_gather(w_query, 'gx', axis=0, tiled=True)  23.5 us
  transfers between devices with their start and end apart: 11, of which 10 were waited for; matrix products, arithmetic and copies ran while one was open for 5% of the time, Pallas kernels for 0%

commit v1 on v0

--- a/solution.py
+++ b/solution.py
@@ -1,6 +1,10 @@
+import functools
+
 import jax
 import jax.numpy as jnp
 from jax import lax
+from jax.experimental import pallas as pl
+from jax.experimental.pallas import tpu as pltpu
 from jax.sharding import PartitionSpec as P
 
 HD = 104
@@ -8,6 +12,10 @@
 
 EPS = 1e-06
 NEG = -1e30
+VMEM_LIMIT = 30 * 1024 * 1024
+SMALL_LIMIT = 24 * 1024 * 1024
+OUT_EARLY = 128
+LOG2_E = 1.4426950408889634
 
 
 def normalize(tok_rows, gain):
@@ -18,7 +26,7 @@
     return (centred * lax.rsqrt(row_var + EPS) * gain).astype(jnp.bfloat16)
 
 
-def body(
+def general_body(
     tokens,
     segments,
     gain_attn,
@@ -133,6 +141,530 @@
     return (after_mlp[None], returned[None])
 
 
+def swap_x(arr):
+    return lax.ppermute(arr, "gx", [(0, 1), (1, 0)])
+
+
+def swap_y(arr):
+    return lax.ppermute(arr, "gy", [(i, i ^ 2) for i in range(4)])
+
+
+def swap_core(arr):
+    return lax.ppermute(arr, "gy", [(i, i ^ 1) for i in range(4)])
+
+
+def swap_row(arr, step):
+    count = lax.axis_size("row")
+    return lax.ppermute(arr, "row", [(i, i ^ step) for i in range(count)])
+
+
+def gather_eight(own):
+    over_x = swap_x(own)
+    over_y = swap_y(own)
+    held = [own, over_y, over_x, swap_y(over_x)]
+    return held + [swap_core(part) for part in held]
+
+
+PLACES = tuple((dx, dy, dc) for dc in (0, 1) for dx in (0, 1) for dy in (0, 1))
+
+
+def position():
+    gx = lax.axis_index("gx")
+    gy = lax.axis_index("gy")
+    return gx, gy // 2, gy % 2
+
+
+def run_copies(pairs, sem):
+    copies = [pltpu.make_async_copy(src, dst, sem.at[i]) for i, (src, dst) in enumerate(pairs)]
+    for copy in copies:
+        copy.start()
+    return copies
+
+
+def token_copies(refs, tok_scr):
+    gx, y, core = position()
+    width = refs[0].shape[0]
+    pairs = []
+    for ref, (dx, dy, dc) in zip(refs, PLACES):
+        row = pl.multiple_of(((y ^ dy) * 2 + (core ^ dc)) * width, 16)
+        pairs.append((ref, tok_scr.at[gx ^ dx, pl.ds(row, width)]))
+    return pairs
+
+
+STEP = 64
+
+
+def column(row, scratch):
+    scratch[...] = jnp.broadcast_to(row, (8, row.shape[1])).T
+
+
+def side_by_side(pair, at):
+    return jnp.concatenate([pair[0, at].astype(jnp.float32), pair[1, at].astype(jnp.float32)], axis=1)
+
+
+def fold(rows):
+    return jnp.sum(rows.reshape(rows.shape[0] // 8, 8, rows.shape[1]), axis=0)
+
+
+def norm_of(pivot, first, second, feats):
+    shift = jnp.sum(first, axis=0, keepdims=True) / feats
+    variance = jnp.maximum(jnp.sum(second, axis=0, keepdims=True) / feats - shift * shift, 0.0)
+    return pivot + shift, lax.rsqrt(variance + EPS)
+
+
+def norm_tokens(pair, gain, out):
+    _, feats, count = pair.shape
+    steps = feats // STEP
+    pivots = [pair[g, :16].astype(jnp.float32)[:1] for g in range(2)]
+
+    def add_up(i, totals):
+        at = pl.ds(pl.multiple_of(i * STEP, STEP), STEP)
+        new = []
+        for g in range(2):
+            rows = pair[g, at].astype(jnp.float32) - pivots[g]
+            new.append(totals[2 * g] + fold(rows))
+            new.append(totals[2 * g + 1] + fold(rows * rows))
+        return tuple(new)
+
+    zero = jnp.zeros((8, count), jnp.float32)
+    totals = lax.fori_loop(0, steps, add_up, (zero,) * 4)
+    moments = [norm_of(pivots[g], totals[2 * g], totals[2 * g + 1], feats) for g in range(2)]
+    mean, scale = (jnp.concatenate([moments[0][i], moments[1][i]], axis=1) for i in range(2))
+
+    def write(i, carry):
+        at = pl.ds(pl.multiple_of(i * STEP, STEP), STEP)
+        rows = side_by_side(pair, at) - mean
+        out[at, :] = (rows * scale * gain[at, :1]).astype(jnp.bfloat16)
+        return carry
+
+    lax.fori_loop(0, steps, write, 0)
+
+
+def matmul(lhs, rhs):
+    return jnp.dot(lhs, rhs, preferred_element_type=jnp.float32)
+
+
+def dot_first(lhs, rhs):
+    return lax.dot_general(lhs, rhs, (((0,), (0,)), ((), ())), preferred_element_type=jnp.float32)
+
+
+def attention_kernel(*refs):
+    shards = refs[:8]
+    gain, w_query, w_key, w_value, w_got, w_got_row, w_got_key, segments = refs[8:16]
+    out, tok_scr, norm_scr, w_scr, qkv_scr, att_scr, gain_scr, seg_scr, sem = refs[-9:]
+    gx, y, core = position()
+    plane = lax.axis_index("row") % 2
+    cols = out.shape[0]
+    pairs = token_copies(shards, tok_scr)
+    own = pl.ds(pl.multiple_of(gx * cols, 16), cols)
+    for i, ref in enumerate((w_query, w_key, w_value)):
+        pairs.append((ref.at[own], w_scr.at[gx, pl.ds(i * cols, cols)]))
+    pairs.append((w_got, w_scr.at[1 - gx, pl.ds(pl.multiple_of(2 * cols * plane, 16), cols)]))
+    pairs.append((w_got_row, w_scr.at[1 - gx, pl.ds(pl.multiple_of(2 * cols * (1 - plane), 16), cols)]))
+    pairs.append((w_got_key, w_scr.at[1 - gx, pl.ds(cols, cols)]))
+    copies = run_copies(pairs, sem)
+    column(gain[...], gain_scr)
+    column(segments[...], seg_scr)
+    for copy in copies[:8]:
+        copy.wait()
+    norm_tokens(tok_scr, gain_scr, norm_scr)
+    for copy in copies[8:]:
+        copy.wait()
+    feats, total = norm_scr.shape
+    depth = feats // 2
+    qkv_scr[...] = matmul(w_scr[0], norm_scr[:depth]) + matmul(w_scr[1], norm_scr[depth:])
+    scale = HD ** (-0.5) * LOG2_E
+    for head in range(cols // HD):
+        begin = head * HD
+        keys = qkv_scr[cols + begin : cols + begin + HD].T.astype(jnp.bfloat16)
+        values = qkv_scr[2 * cols + begin : 2 * cols + begin + HD].astype(jnp.bfloat16)
+        for start in range(0, total, 256):
+            at = slice(start, min(start + 256, total))
+            scores = matmul(keys, (qkv_scr[begin : begin + HD, at] * scale).astype(jnp.bfloat16))
+            scores = jnp.where(seg_scr[:, :1] == segments[:, at], scores, NEG)
+            weights = jnp.exp2(scores - jnp.max(scores, axis=0, keepdims=True))
+            row_total = jnp.sum(weights, axis=0, keepdims=True)
+            att_scr[begin : begin + HD, at] = matmul(values, weights.astype(jnp.bfloat16)) / row_total
+    out[...] = att_scr[...].astype(jnp.bfloat16)
+
+
+def project_kernel(*refs):
+    tokens, attended, weights, gain = refs[:8], refs[8:16], refs[16:22], refs[22]
+    normed, own, tok_scr, att_scr, w_scr, aft_scr, gain_scr, sem = refs[-8:]
+    gx, y, core = position()
+    width = own.shape[0]
+    cols = attended[0].shape[0]
+    feats, total = att_scr.shape
+    pairs = []
+    for ref, (dx, dy, dc) in zip(attended, PLACES):
+        row = pl.multiple_of(((y ^ dy) * 2 + (core ^ dc)) * width + (gx ^ dx) * cols, 16)
+        pairs.append((ref, att_scr.at[pl.ds(row, cols)]))
+    bounds = list(range(0, feats, 384))[:-1] + [feats]
+    chunks = list(zip(bounds[:-1], bounds[1:]))
+    for begin, end in chunks:
+        for dc, parts in enumerate((weights[:3], weights[3:])):
+            here = (y * 2 + (core ^ dc)) * width
+            there = ((y ^ 1) * 2 + (core ^ dc)) * width
+            rows = (here, there, there + parts[1].shape[0])
+            for ref, row in zip(parts, rows):
+                at = pl.ds(pl.multiple_of(row, 16), ref.shape[0])
+                pairs.append((ref.at[:, begin:end], w_scr.at[at, begin:end]))
+        if begin == 0:
+            pairs.extend(token_copies(tokens, tok_scr))
+    copies = run_copies(pairs, sem)
+    column(gain[...], gain_scr)
+    first = second = pivot = None
+    waited = 0
+    for i, (begin, end) in enumerate(chunks):
+        needed = 8 + 6 + 8 + 6 * i
+        for copy in copies[waited:needed]:
+            copy.wait()
+        waited = needed
+        rows = dot_first(w_scr[:, begin:end], att_scr[...]) + side_by_side(tok_scr, slice(begin, end))
+        rows = rows.astype(jnp.bfloat16)
+        aft_scr[begin:end] = rows
+        rows = rows.astype(jnp.float32)
+        if pivot is None:
+            pivot = rows[:1]
+        rows = rows - pivot
+        sums = fold(rows), fold(rows * rows)
+        first, second = sums if first is None else (first + sums[0], second + sums[1])
+    mean, scale = norm_of(pivot, first, second, feats)
+    row = pl.multiple_of((y * 2 + core) * width, 16)
+    mine = aft_scr[pl.ds(row, width)].astype(jnp.float32)
+    half = total // 2
+    own[...] = jnp.where(gx == 0, mine[:, :half], mine[:, half:]).astype(jnp.bfloat16)
+
+    def write(i, carry):
+        at = pl.ds(pl.multiple_of(i * STEP, STEP), STEP)
+        rows = aft_scr[at, :].astype(jnp.float32) - mean
+        normed[at, :] = (rows * scale * gain_scr[at, :1]).astype(jnp.bfloat16)
+        return carry
+
+    lax.fori_loop(0, feats // STEP, write, 0)
+
+
+def up_kernel(normed, up_own, up_got, up_got_row, hidden, norm_scr, up_scr, sem):
+    gx, y, core = position()
+    plane = lax.axis_index("row") % 2
+    feats, units = up_scr.shape
+    depth = feats // 2
+    chunk = units // 2
+    own_rows = pl.ds(pl.multiple_of(gx * depth, 16), depth)
+    other_rows = pl.ds(pl.multiple_of((1 - gx) * depth, 16), depth)
+    pairs = [
+        (normed, norm_scr),
+        (up_own.at[:, pl.ds(pl.multiple_of(gx * units, 128), units)], up_scr.at[own_rows]),
+        (up_got, up_scr.at[other_rows, pl.ds(pl.multiple_of(plane * chunk, 128), chunk)]),
+        (up_got_row, up_scr.at[other_rows, pl.ds(pl.multiple_of((1 - plane) * chunk, 128), chunk)]),
+    ]
+    for copy in run_copies(pairs, sem):
+        copy.wait()
+    for begin in range(0, units, 256):
+        rows = dot_first(up_scr[:, begin : begin + 256], norm_scr[...])
+        rows = 0.5 * rows * (1.0 + lax.erf(rows * (0.5**0.5)))
+        hidden[begin : begin + 256] = rows.astype(jnp.bfloat16)
+
+
+def down_kernel(dc, hidden, down_own, *refs):
+    got, outs, (hid_scr, down_scr, sem) = refs[:4], refs[-7:-3], refs[-3:]
+    gx, y, core = position()
+    plane = lax.axis_index("row") % 2
+    depth = down_own.shape[0]
+    units, total = hid_scr.shape
+    chunk = units // 4
+    own_rows = pl.ds(pl.multiple_of(gx * depth, 16), depth)
+    other_rows = pl.ds(pl.multiple_of((1 - gx) * depth, 16), depth)
+    pairs = [
+        (hidden, hid_scr),
+        (down_own.at[:, pl.ds(pl.multiple_of(gx * units, 128), units)], down_scr.at[own_rows]),
+    ]
+    for i, ref in enumerate(got):
+        place = plane if i < 2 else 1 - plane
+        at = pl.ds(pl.multiple_of((2 * place + i % 2) * chunk, 128), chunk)
+        pairs.append((ref, down_scr.at[other_rows, at]))
+    for copy in run_copies(pairs, sem):
+        copy.wait()
+    half = outs[0].shape[1]
+    middle = total // 2
+    for dy in range(2):
+        for part in range(2):
+            row = ((y ^ dy) * 2 + (core ^ dc)) * (2 * half) + part * half
+            sums = matmul(down_scr[pl.ds(pl.multiple_of(row, 16), half)], hid_scr[...])
+            left, right = sums[:, :middle], sums[:, middle:]
+            for dx in range(2):
+                group, other = (dx, dy) if part == 0 else (dy, dx)
+                picked = jnp.where(gx == dx, left, right)
+                outs[2 * (1 - group) + part][other] = picked.astype(jnp.bfloat16)
+
+
+def last_sum_kernel(own, rest_x, rest_y, last_x, last_y, groups, out, picked):
+    half, count = last_x.shape
+    for i, (rest, source) in enumerate(((rest_x, last_x), (rest_y, last_y))):
+        at = slice(i * half, (i + 1) * half)
+        total = own[at].astype(jnp.float32) + rest[...].astype(jnp.float32) + source[...].astype(jnp.float32)
+        out[at] = total.astype(jnp.bfloat16)
+    for k in range(groups.shape[0]):
+        place = lax.broadcasted_iota(jnp.int32, (count, groups.shape[1]), 0)
+        chosen = jnp.where(place == groups[k : k + 1], 1.0, 0.0).astype(jnp.bfloat16)
+        picked[k] = matmul(out[...], chosen).T.astype(jnp.bfloat16)
+
+
+def merge_kernel(picked, weights, *refs):
+    got, (keep, send, res_scr) = refs[:4], refs[-3:]
+    gx, y, core = position()
+    plane = lax.axis_index("row") % 2
+    slots = weights.shape[0]
+    width = keep.shape[1]
+    own = matmul(picked[0], weights[0])
+    for k in range(1, slots):
+        own = own + matmul(picked[k], weights[k])
+    other = None
+    for i, ref in enumerate(got):
+        place = plane if i < 2 else 1 - plane
+        part = matmul(picked[2 * place + i % 2], ref[...])
+        other = part if other is None else other + part
+    res_scr[gx] = own.T
+    res_scr[1 - gx] = other.T
+    for dc, target in ((0, keep), (1, send)):
+        row = pl.multiple_of((core ^ dc) * width, 16)
+        for dy in range(2):
+            target[dy] = res_scr[y ^ dy, pl.ds(row, width)].astype(jnp.bfloat16)
+
+
+def add(*arrs):
+    total = arrs[0].astype(jnp.float32)
+    for arr in arrs[1:]:
+        total = total + arr.astype(jnp.float32)
+    return total.astype(jnp.bfloat16)
+
+
+def return_kernel(*refs):
+    tiles, sources, out = refs[:-2], refs[-2], refs[-1]
+    row = lax.axis_index("row")
+    count = sources.shape[1]
+    total = None
+    for step, tile in enumerate(tiles):
+        slot = lax.broadcasted_iota(jnp.int32, (tile.shape[1], count), 0) + (row ^ step) * tile.shape[1]
+        chosen = jnp.where(slot == sources[...], 1.0, 0.0).astype(jnp.bfloat16)
+        part = matmul(tile[...], chosen)
+        total = part if total is None else total + part
+    out[...] = total.astype(jnp.bfloat16)
+
+
+def call(kernel, operands, outs, far, scratch=(), flops=0, aliases=None, far_out=False, limit=VMEM_LIMIT):
+    moved = sum(a.size * a.dtype.itemsize for a in operands)
+    outs = tuple(jax.ShapeDtypeStruct(shape, dtype) for shape, dtype in outs)
+    return pl.pallas_call(
+        kernel,
+        out_shape=outs,
+        in_specs=[pl.BlockSpec(memory_space=pl.ANY if f else pltpu.VMEM) for f in far],
+        out_specs=tuple(pl.BlockSpec(memory_space=pl.ANY if far_out else pltpu.VMEM) for _ in outs),
+        scratch_shapes=list(scratch),
+        input_output_aliases=aliases or {},
+        compiler_params=pltpu.CompilerParams(vmem_limit_bytes=limit),
+        cost_estimate=pl.CostEstimate(flops=flops, bytes_accessed=moved, transcendentals=0),
+    )(*operands)
+
+
+def after(held, passed):
+    count = len(passed)
+    return call(
+        lambda *refs: None,
+        (*passed, *held),
+        [(a.shape, a.dtype) for a in passed],
+        (True,) * (count + len(held)),
+        aliases={i: i for i in range(count)},
+        far_out=True,
+    )
+
+
+def rows_of(arr, begin, count):
+    return lax.dynamic_slice_in_dim(arr, begin, count, 0)
+
+
+def fast_body(
+    tokens,
+    segments,
+    gain_attn,
+    w_query,
+    w_key,
+    w_value,
+    w_out,
+    gain_mlp,
+    w_up,
+    w_down,
+    w_merge,
+    merge_groups,
+    sources,
+):
+    gx = lax.axis_index("gx")
+    plane = lax.axis_index("row") % 2
+    tok = tokens[0].T
+    width, count = tok.shape
+    feats = 4 * width
+    depth = feats // 2
+    half = width // 2
+    cols = w_query.shape[1] // 2
+    total_cols = 3 * cols
+    sixteen = jnp.bfloat16
+    total = 2 * count
+    gain_attn = gain_attn.reshape(1, -1)
+    gain_mlp = gain_mlp.reshape(1, -1)
+    down = w_down.T
+    units = w_up.shape[1] // 2
+    chunk = units // 2
+    theirs = (1 - gx) * units + plane * chunk
+    their_row = (1 - gx) * cols
+    first = jnp.where(
+        plane == 0, rows_of(w_query.T, their_row, cols), rows_of(w_value.T, their_row, cols)
+    )
+
+    over_x, over_y = swap_x(tok), swap_y(tok)
+    qkv_got = swap_x(first)
+    (key_piece,) = after((over_x,), (rows_of(w_key.T, their_row, cols),))
+    qkv_got_key = swap_x(key_piece)
+    held = [tok, over_y, over_x, swap_y(over_x)]
+    tok_shards = held + [swap_core(part) for part in held]
+    down_pieces = [
+        lax.dynamic_slice_in_dim(down, theirs + i * (chunk // 2), chunk // 2, 1) for i in range(2)
+    ]
+    (up_piece,) = after((qkv_got,), (lax.dynamic_slice_in_dim(w_up, theirs, chunk, 1),))
+    early = OUT_EARLY
+    (out_early,) = after((over_y,), (w_out[:early],))
+    (out_late,) = after((over_x, over_y, qkv_got), (w_out[early:],))
+    out_over_y = [swap_y(out_early), swap_y(out_late)]
+    qkv_got_row = swap_row(qkv_got, 1)
+    up_piece, *down_pieces = after(
+        (qkv_got_row, qkv_got_key, held[3], *tok_shards[4:7], out_over_y[0]), (up_piece, *down_pieces)
+    )
+    up_got = swap_x(up_piece)
+
+    (attended,) = call(
+        attention_kernel,
+        (*tok_shards, gain_attn, w_query.T, w_key.T, w_value.T, qkv_got, qkv_got_row, qkv_got_key, segments),
+        [((cols, total), sixteen)],
+        (True,) * 8 + (False,) + (True,) * 6 + (False,),
+        [
+            pltpu.VMEM((2, feats, count), sixteen),
+            pltpu.VMEM((feats, total), sixteen),
+            pltpu.VMEM((2, total_cols, depth), sixteen),
+            pltpu.VMEM((total_cols, total), jnp.float32),
+            pltpu.VMEM((cols, total), jnp.float32),
+            pltpu.VMEM((feats, 8), jnp.float32),
+            pltpu.VMEM((total, 8), jnp.int32),
+            pltpu.SemaphoreType.DMA((14,)),
+        ],
+        2 * total * feats * total_cols + 4 * total * total * cols,
+    )
+    attended, up_got = after((), (attended, up_got))
+    over_x, over_y = swap_x(attended), swap_y(attended)
+    up_got_row = swap_row(up_got, 1)
+    slots = w_merge.shape[0]
+    merge_pieces = [rows_of(w_merge, plane * (slots // 2) + i, 1)[0] for i in range(2)]
+    *out_over_y, down_piece_a, down_piece_b, merge_a, merge_b = after(
+        (over_x, over_y), (*out_over_y, *down_pieces, *merge_pieces)
+    )
+    merge_pieces = [merge_a, merge_b]
+    down_got_a, down_got_b = swap_x(down_piece_a), swap_x(down_piece_b)
+    (diagonal,) = after((down_got_a, up_got_row), (swap_y(over_x),))
+    held = [attended, over_y, over_x, diagonal]
+    att_shards = held + [swap_core(part) for part in held]
+    out_parts = [w_out, *out_over_y]
+    out_parts = out_parts + [swap_core(part) for part in out_parts]
+    down_got_a_row = swap_row(down_got_a, 1)
+    normed, own = call(
+        project_kernel,
+        (*tok_shards, *att_shards, *out_parts, gain_mlp, down_got_a, up_got_row),
+        [((feats, total), sixteen), ((width, count), sixteen)],
+        (True,) * 22 + (False, True, True),
+        [
+            pltpu.VMEM((2, feats, count), sixteen),
+            pltpu.VMEM((feats, total), sixteen),
+            pltpu.VMEM((feats, feats), sixteen),
+            pltpu.VMEM((feats, total), sixteen),
+            pltpu.VMEM((feats, 8), jnp.float32),
+            pltpu.SemaphoreType.DMA((40,)),
+        ],
+        2 * total * feats * feats,
+    )
+    merge_got = [swap_x(part) for part in merge_pieces]
+    normed, down_got_b = after((), (normed, down_got_b))
+    (hidden,) = call(
+        up_kernel,
+        (normed, w_up, up_got, up_got_row),
+        [((units, total), sixteen)],
+        (True,) * 4,
+        [
+            pltpu.VMEM((feats, total), sixteen),
+            pltpu.VMEM((feats, units), sixteen),
+            pltpu.SemaphoreType.DMA((4,)),
+        ],
+        2 * total * feats * units,
+        limit=SMALL_LIMIT,
+    )
+    down_got_b_row = swap_row(down_got_b, 1)
+    hidden, merge_got[0] = after((), (hidden, merge_got[0]))
+    pair = ((2, half, count), sixteen)
+
+    def down_part(dc, *others):
+        return call(
+            functools.partial(down_kernel, dc),
+            (hidden, down, down_got_a, down_got_b, down_got_a_row, down_got_b_row, *others),
+            [pair] * 4,
+            (True,) * (6 + len(others)),
+            [
+                pltpu.VMEM((units, total), sixteen),
+                pltpu.VMEM((feats, units), sixteen),
+                pltpu.SemaphoreType.DMA((6,)),
+            ],
+            total * feats * units,
+            limit=SMALL_LIMIT,
+        )
+
+    send = down_part(1)
+    got = [swap_core(part) for part in send]
+    merge_got_row = [swap_row(part, 1) for part in merge_got]
+    keep = down_part(0, *send)
+    keep = after((merge_got[1], merge_got_row[0]), keep)
+    from_x = swap_x(add(keep[0], got[0]))
+    from_y = swap_y(add(keep[1], got[1]))
+    rest_x, rest_y = add(keep[2], got[2], from_x), add(keep[3], got[3], from_y)
+    last_x, last_y = swap_y(rest_x[1]), swap_x(rest_y[1])
+    merged_count = merge_groups.shape[1]
+    after_mlp, picked = call(
+        last_sum_kernel,
+        (own, rest_x[0], rest_y[0], last_x, last_y, merge_groups[0].T),
+        [((width, count), sixteen), ((slots, merged_count, width), sixteen)],
+        (False,) * 6,
+        (),
+        2 * count * width * count,
+        limit=SMALL_LIMIT,
+    )
+    keep, send = call(
+        merge_kernel,
+        (picked, w_merge, *merge_got, *merge_got_row),
+        [((2, width, merged_count), sixteen)] * 2,
+        (False,) * 6,
+        [pltpu.VMEM((2, depth, merged_count), jnp.float32)],
+        2 * count * width * feats,
+        limit=SMALL_LIMIT,
+    )
+    mine = add(keep, swap_core(send))
+    merged = add(mine[0], swap_y(mine[1]))
+    tiles = [merged] + [swap_row(merged, step) for step in range(1, lax.axis_size("row"))]
+    (returned,) = call(
+        return_kernel,
+        (*tiles, sources),
+        [((width, merged_count), sixteen)],
+        (False,) * (len(tiles) + 1),
+        (),
+        2 * count * width * merged_count,
+        limit=SMALL_LIMIT,
+    )
+    return (after_mlp.T[None], returned.T[None])
+
+
 def solution(mesh):
     placed = (
         P("row", "gx", "gy"),
@@ -149,8 +681,9 @@
         P("row", "gx", None),
         P("row", "gx"),
     )
+    small = mesh.shape["gx"] == 2 and mesh.shape["gy"] == 4 and mesh.shape["row"] in (2, 4)
     return jax.shard_map(
-        body,
+        fast_body if small else general_body,
         mesh=mesh,
         in_specs=placed,
         out_specs=(P("row", "gx", "gy"), P("row", "gx", "gy")),

time: 607 us -> 178 us (0.29); the launches traced: 599 us -> 177 us
  waiting for transfers between devices: 416 us -> 78.6 us
  blocking collectives: 72.8 us -> 0 us
  matrix products: 45.5 us -> 0 us
  Pallas kernels: 0 us -> 42.5 us
  starting transfers between devices: 0.65 us -> 40.9 us
  local copies, waits for them, and re-layouts: 32.3 us -> 12.3 us
  other arithmetic: 17 us -> 1.91 us
  between operations: 14.6 us -> 1.1 us
    all_gather x9 -> x0, waiting for transfers between devices: 367 us -> none  [the longest x1 87.9 us: body(): lax.all_gather(w_down, 'gx', axis=1, tiled=True)]
    ppermute x0 -> x45, waiting for transfers between devices: none -> 78.6 us  [the longest x11 36.2 us: swap_x(): return lax.ppermute(arr, 'gx', [(0, 1), (1, 0)])]
    dot_general x10 -> x0, matrix products: 45.5 us -> none  [the longest x1 20.5 us: body(): jnp.dot(hidden, lax.all_gather(w_down, 'gx', axis=1, tiled=True), preferr...]
    reduce_scatter x2 -> x0, waiting for transfers between devices: 44.9 us -> none  [the longest x1 23.7 us: body(): lax.psum_scatter(partials.astype(jnp.bfloat16), 'gy', scatter_dimension=1...]
    pallas_call x0 -> x19, Pallas kernels: none -> 42.5 us  [call(): pl.pallas_call(kernel, out_shape=outs, in_specs=[pl.BlockSpec(memory_spac...]
    ppermute x0 -> x45, starting transfers between devices: none -> 40.9 us  [the longest x11 14 us: swap_x(): return lax.ppermute(arr, 'gx', [(0, 1), (1, 0)])]
    all_gather x3 -> x0, blocking collectives: 39.7 us -> none  [the longest x1 15 us: body(): pooled = lax.all_gather(merged[None], 'row', axis=0, tiled=True)]
    all_to_all x1 -> x0, blocking collectives: 33.1 us -> none  [body(): lax.all_to_all(w_out, 'gy', split_axis=1, concat_axis=0, tiled=True)]
  transfers between devices with their start and end apart: 11 -> 45, of which waited for: 10 -> 20; matrix products, arithmetic and copies ran while one was open for 5% -> 5% of each run, Pallas kernels for 0% -> 23%
where the time goes in v1:
time: 178 us; the launch traced here: 177 us
  waiting for transfers between devices  78.6 us (44%)
  Pallas kernels  42.5 us (24%)
  starting transfers between devices  40.9 us (23%)
  local copies, waits for them, and re-layouts  12.3 us (7%)
  other arithmetic  1.91 us (1%)
    pallas_call x19, Pallas kernels, call(): pl.pallas_call(kernel, out_shape=outs, in_specs=[pl.BlockSpec(memory_spac...  42.5 us
    ppermute x11, waiting for transfers between devices, swap_x(): return lax.ppermute(arr, 'gx', [(0, 1), (1, 0)])  36.2 us
    ppermute x9, waiting for transfers between devices, swap_y(): return lax.ppermute(arr, 'gy', [(i, i ^ 2) for i in range(4)])  30.3 us
    ppermute x11, starting transfers between devices, swap_x(): return lax.ppermute(arr, 'gx', [(0, 1), (1, 0)])  14 us
    ppermute x9, starting transfers between devices, swap_y(): return lax.ppermute(arr, 'gy', [(i, i ^ 2) for i in range(4)])  12.5 us
    ppermute x9, starting transfers between devices, swap_row(): return lax.ppermute(arr, 'row', [(i, i ^ step) for i in range(count)])  12 us
    ppermute x9, waiting for transfers between devices, swap_row(): return lax.ppermute(arr, 'row', [(i, i ^ step) for i in range(count)])  9.27 us
    unnamed x54, local copies, waits for them, and re-layouts  4.43 us
  transfers between devices with their start and end apart: 45, of which 20 were waited for; matrix products, arithmetic and copies ran while one was open for 5% of the time, Pallas kernels for 23%

profile of v1, /device:TPU:0, one launch (start us, length us, event | category | flops | bytes accessed | tf_op | source)
XLA Modules:
  0.0 177.3 jit_solution(5765129682883939609)
XLA Ops:
  0.7 1.3 select_bitcast_fusion
  1.9 3.0 %collective-permute-start.7 = (bf16[208,832]{1,0:T(8,128)(2,1)S(1)}, bf16[208,832]{1,0:T(8,128)(2,1)S(1)}, u32[]{:S(2)}, u32[]{:S(2)}) collective-permute-start(bf16[208,832]{1,0:T(8,128)(2,1)S(1)} %select_bitcast_fusion), channel_id=1, source_target_pairs={{0,16},{16,0},{1,17},{17,1},{2,18},{18,2},{3,19},{19,3},{4,20},{20... | collective-permute-start | bytes 1038344 | tf_op jit(solution)/shard_map/ppermute | solution.py:145
  4.9 1.5 collective-permute-start
  7.0 7.4 %collective-permute-done.7.refs_12_.refs_1_.refs_3_ = bf16[208,832]{1,0:T(8,128)(2,1)S(1)} collective-permute-done((bf16[208,832]{1,0:T(8,128)(2,1)S(1)}, bf16[208,832]{1,0:T(8,128)(2,1)S(1)}, u32[]{:S(2)}, u32[]{:S(2)}) %collective-permute-start.7) | collective-permute-done | bytes 346144 | tf_op jit(solution)/shard_map/ppermute | solution.py:145
  14.4 2.1 %collective-permute-start.8 = (bf16[208,832]{1,0:T(8,128)(2,1)S(1)}, bf16[208,832]{1,0:T(8,128)(2,1)S(1)}, u32[]{:S(2)}, u32[]{:S(2)}) collective-permute-start(bf16[208,832]{1,0:T(8,128)(2,1)S(1)} %collective-permute-done.7.refs_12_.refs_1_.refs_3_), channel_id=1, source_target_pairs={{0,1},{1,0},{2,3},{3,2},{4,5},{5,4},{6,7},{7,6},{8,9},{9,8},{10,11... | collective-permute-start | bytes 1038344 | tf_op jit(solution)/shard_map/ppermute | solution.py:158
  17.4 1.8 %slice.24.refs_0_ = bf16[128,1664]{1,0:T(8,128)(2,1)} slice(bf16[416,1664]{1,0:T(8,128)(2,1)} %refs_16_.1), slice={[0:128], [0:1664]} | slice | bytes 851968 | tf_op jit(solution)/shard_map/slice | solution.py:534
  19.2 1.5 collective-permute-start.10
  20.7 2.2 %collective-permute-done.1.refs_1_.refs_2_ = bf16[416,448]{1,0:T(8,128)(2,1)} collective-permute-done((bf16[416,448]{1,0:T(8,128)(2,1)}, bf16[416,448]{1,0:T(8,128)(2,1)}, u32[]{:S(2)}, u32[]{:S(2)}) %collective-permute-start.1) | collective-permute-done | bytes 372768 | tf_op jit(solution)/shard_map/ppermute | solution.py:145
  22.9 1.8 collective-permute-start.2
  26.7 1.5 collective-permute-start.9
  28.2 1.3 constant_dynamic-slice_fusion.refs_0_
  29.7 8.0 %collective-permute-done.9.refs_14_.refs_4_ = bf16[208,832]{1,0:T(8,128)(2,1)} collective-permute-done((bf16[208,832]{1,0:T(8,128)(2,1)}, bf16[208,832]{1,0:T(8,128)(2,1)}, u32[]{:S(2)}, u32[]{:S(2)}) %collective-permute-start.9) | collective-permute-done | bytes 346144 | tf_op jit(solution)/shard_map/ppermute | solution.py:145
  39.7 1.6 collective-permute-start.11
  41.8 2.2 %slice.25.refs_0_ = bf16[288,1664]{1,0:T(8,128)(2,1)} slice(bf16[416,1664]{1,0:T(8,128)(2,1)} %refs_16_.1), slice={[128:416], [0:1664]} | slice | bytes 1916928 | tf_op jit(solution)/shard_map/slice | solution.py:535
  44.0 1.5 collective-permute-start.15
  45.6 14.4 %shard_map.141.refs_0_ = bf16[208,896]{1,0:T(8,128)(2,1)} custom-call(bf16[416,448]{1,0:T(8,128)(2,1)S(1)} %bitcast.52, bf16[416,448]{1,0:T(8,128)(2,1)} %collective-permute-done.refs_1_.refs_2_, bf16[416,448]{1,0:T(8,128)(2,1)} %collective-permute-done.1.refs_1_.refs_2_, bf16[416,448]{1,0:T(8,128)(2,1)} %collective-permute-done.2.refs_3_.refs_5_, ...), custom_call_target="tpu_custom_call" | custom-call | flops 2528641024 | bytes 6107136 | tf_op jit(solution)/shard_map/pallas_call | solution.py:458
  61.7 1.6 collective-permute-start.17
  63.3 1.5 dynamic-slice_bitcast_fusion
  64.9 3.5 %collective-permute-done.15.refs_1_ = bf16[288,1664]{1,0:T(8,128)(2,1)} collective-permute-done((bf16[288,1664]{1,0:T(8,128)(2,1)}, bf16[288,1664]{1,0:T(8,128)(2,1)}, u32[]{:S(2)}, u32[]{:S(2)}) %collective-permute-start.15) | collective-permute-done | bytes 958496 | tf_op jit(solution)/shard_map/ppermute | solution.py:149
  68.4 7.0 %collective-permute-done.12.refs_7_.refs_9_ = bf16[208,896]{1,0:T(8,128)(2,1)} collective-permute-done((bf16[208,896]{1,0:T(8,128)(2,1)}, bf16[208,896]{1,0:T(8,128)(2,1)}, u32[]{:S(2)}, u32[]{:S(2)}) %collective-permute-start.12) | collective-permute-done | bytes 372768 | tf_op jit(solution)/shard_map/ppermute | solution.py:149
  76.2 1.5 collective-permute-start.14
  77.7 9.4 %collective-permute-done.14.refs_0_ = bf16[208,896]{1,0:T(8,128)(2,1)S(1)} collective-permute-done((bf16[208,896]{1,0:T(8,128)(2,1)}, bf16[208,896]{1,0:T(8,128)(2,1)S(1)}, u32[]{:S(2)}, u32[]{:S(2)}) %collective-permute-start.14) | collective-permute-done | bytes 372768 | tf_op jit(solution)/shard_map/ppermute | solution.py:149
  88.4 1.3 collective-permute-done.19.refs_13_
  89.7 2.0 %collective-permute-start.25 = (bf16[832,256]{1,0:T(8,128)(2,1)S(1)}, bf16[832,256]{1,0:T(8,128)(2,1)S(1)}, u32[]{:S(2)}, u32[]{:S(2)}) collective-permute-start(bf16[832,256]{1,0:T(8,128)(2,1)S(1)} %get-tuple-element.45), channel_id=1, source_target_pairs={{0,16},{16,0},{1,17},{17,1},{2,18},{18,2},{3,19},{19,3},{4,20},{20... | collective-permute-start | bytes 1277960 | tf_op jit(solution)/shard_map/ppermute | solution.py:145
  92.2 1.5 collective-permute-start.29
  93.7 1.3 collective-permute-start.27
  95.1 13.1 %shard_map.149 = (bf16[1664,896]{1,0:T(8,128)(2,1)S(1)}, bf16[416,448]{1,0:T(8,128)(2,1)S(1)}) custom-call(bf16[416,448]{1,0:T(8,128)(2,1)S(1)} %bitcast.53, bf16[416,448]{1,0:T(8,128)(2,1)} %collective-permute-done.refs_1_.refs_2_, bf16[416,448]{1,0:T(8,128)(2,1)} %collective-permute-done.1.refs_1_.refs_2_, ...), custom_call_target="tpu_custom_call" | custom-call | flops 4961861632 | bytes 12786176 | tf_op jit(solution)/shard_map/pallas_call | solution.py:458
  110.1 6.0 %shard_map.151.refs_0_ = bf16[1024,896]{1,0:T(8,128)(2,1)S(1)} custom-call(bf16[1664,896]{1,0:T(8,128)(2,1)S(1)} %get-tuple-element.46.normed, bf16[832,2048]{1,0:T(8,128)(2,1)S(1)} %copy-done.13, bf16[832,512]{1,0:T(8,128)(2,1)} %get-tuple-element.40.up_got, bf16[832,512]{1,0:T(8,128)(2,1)} %collective-permute-done.17.refs_2_.refs_24_.up_got_row), custom_call_target="tpu_custom_call" | custom-call | flops 3053453312 | bytes 8093696 | tf_op jit(solution)/shard_map/pallas_call | solution.py:458
  116.1 2.2 %collective-permute-done.26.refs_1_ = bf16[416,832]{1,0:T(8,128)(2,1)S(1)} collective-permute-done((bf16[416,832]{1,0:T(8,128)(2,1)S(1)}, bf16[416,832]{1,0:T(8,128)(2,1)S(1)}, u32[]{:S(2)}, u32[]{:S(2)}) %collective-permute-start.26) | collective-permute-done | bytes 692256 | tf_op jit(solution)/shard_map/ppermute | solution.py:145
  118.3 1.3 collective-permute-start.30
  119.6 3.0 %shard_map.153 = (bf16[2,208,448]{2,1,0:T(8,128)(2,1)S(1)}, bf16[2,208,448]{2,1,0:T(8,128)(2,1)S(1)}, bf16[2,208,448]{2,1,0:T(8,128)(2,1)S(1)}, bf16[2,208,448]{2,1,0:T(8,128)(2,1)S(1)}) custom-call(bf16[1024,896]{1,0:T(8,128)(2,1)S(1)} %get-tuple-element.48.hidden, bf16[832,2048]{1,0:T(8,128)(2,1)S(1)} %bitcast.43, ...), custom_call_target="tpu_custom_call" | custom-call | flops 1526726656 | bytes 6946816 | tf_op jit(solution)/shard_map/pallas_call | solution.py:458
  123.3 2.8 %shard_map.154 = (bf16[2,208,448]{2,1,0:T(8,128)(2,1)S(1)}, bf16[2,208,448]{2,1,0:T(8,128)(2,1)S(1)}, bf16[2,208,448]{2,1,0:T(8,128)(2,1)S(1)}, bf16[2,208,448]{2,1,0:T(8,128)(2,1)S(1)}) custom-call(bf16[1024,896]{1,0:T(8,128)(2,1)S(1)} %get-tuple-element.48.hidden, bf16[832,2048]{1,0:T(8,128)(2,1)S(1)} %bitcast.44, ...), custom_call_target="tpu_custom_call" | custom-call | flops 1526726656 | bytes 8437760 | tf_op jit(solution)/shard_map/pallas_call | solution.py:458
  126.1 7.6 %collective-permute-done.29.refs_4_.refs_1_ = bf16[416,832]{1,0:T(8,128)(2,1)S(1)} collective-permute-done((bf16[416,832]{1,0:T(8,128)(2,1)S(1)}, bf16[416,832]{1,0:T(8,128)(2,1)S(1)}, u32[]{:S(2)}, u32[]{:S(2)}) %collective-permute-start.29) | collective-permute-done | bytes 692256 | tf_op jit(solution)/shard_map/ppermute | solution.py:145
  133.7 2.1 %collective-permute-done.30.refs_5_.refs_2_ = bf16[416,832]{1,0:T(8,128)(2,1)S(1)} collective-permute-done((bf16[416,832]{1,0:T(8,128)(2,1)S(1)}, bf16[416,832]{1,0:T(8,128)(2,1)S(1)}, u32[]{:S(2)}, u32[]{:S(2)}) %collective-permute-start.30) | collective-permute-done | bytes 692256 | tf_op jit(solution)/shard_map/ppermute | solution.py:158
  136.0 1.6 collective-permute-start.33
  137.7 1.6 collective-permute-start.36
  139.7 6.4 %collective-permute-done.33 = bf16[2,208,448]{2,1,0:T(8,128)(2,1)S(1)} collective-permute-done((bf16[2,208,448]{2,1,0:T(8,128)(2,1)S(1)}, bf16[2,208,448]{2,1,0:T(8,128)(2,1)S(1)}, u32[]{:S(2)}, u32[]{:S(2)}) %collective-permute-start.33) | collective-permute-done | bytes 372768 | tf_op jit(solution)/shard_map/ppermute | solution.py:145
  146.2 1.6 collective-permute-done.36
  148.2 1.6 collective-permute-start.37
  150.2 3.9 %collective-permute-done.37.last_x = bf16[208,448]{1,0:T(8,128)(2,1)S(1)} collective-permute-done((bf16[208,448]{1,0:T(8,128)(2,1)S(1)}, bf16[208,448]{1,0:T(8,128)(2,1)S(1)}, u32[]{:S(2)}, u32[]{:S(2)}) %collective-permute-start.37) | collective-permute-done | bytes 186400 | tf_op jit(solution)/shard_map/ppermute | solution.py:149
  154.1 1.6 collective-permute-done.38.last_y
  156.7 1.3 shard_map.157
  158.1 1.5 collective-permute-done.40
  160.2 4.5 %collective-permute-done.41 = bf16[416,112]{1,0:T(8,128)(2,1)S(1)} collective-permute-done((bf16[416,112]{1,0:T(8,128)(2,1)S(1)}, bf16[416,112]{1,0:T(8,128)(2,1)S(1)}, u32[]{:S(2)}, u32[]{:S(2)}) %collective-permute-start.41) | collective-permute-done | bytes 93216 | tf_op jit(solution)/shard_map/ppermute | solution.py:149
  165.3 2.6 %collective-permute-start.43 = (bf16[416,112]{1,0:T(8,128)(2,1)S(1)}, bf16[416,112]{1,0:T(8,128)(2,1)S(1)}, u32[]{:S(2)}, u32[]{:S(2)}) collective-permute-start(bf16[416,112]{1,0:T(8,128)(2,1)S(1)} %fusion.refs_0_), channel_id=1, source_target_pairs={{0,2},{1,3},{2,0},{3,1},{4,6},{5,7},{6,4},{7,5},{8,10},{9,11},{10,... | collective-permute-start | bytes 279560 | tf_op jit(solution)/shard_map/ppermute | solution.py:158
  167.9 1.3 collective-permute-start.44
  169.2 1.2 collective-permute-done.42.refs_1_
  170.4 5.9 %collective-permute-done.43.refs_2_ = bf16[416,112]{1,0:T(8,128)(2,1)S(1)} collective-permute-done((bf16[416,112]{1,0:T(8,128)(2,1)S(1)}, bf16[416,112]{1,0:T(8,128)(2,1)S(1)}, u32[]{:S(2)}, u32[]{:S(2)}) %collective-permute-start.43) | collective-permute-done | bytes 93216 | tf_op jit(solution)/shard_map/ppermute | solution.py:158
  (132 shorter events, 17.5 us)
Async XLA Ops:
  0.6 24.5 %copy-start.15 = (bf16[832,416]{0,1:T(8,128)(2,1)S(1)}, bf16[832,416]{0,1:T(8,128)(2,1)}, u32[]{:S(2)}) copy-start(bf16[832,416]{0,1:T(8,128)(2,1)} %param.17) | copy-start | bytes 2076676
  1.9 27.6 %copy-start = (bf16[2048,832]{0,1:T(8,128)(2,1)S(1)}, bf16[2048,832]{0,1:T(8,128)(2,1)}, u32[]{:S(2)}) copy-start(bf16[2048,832]{0,1:T(8,128)(2,1)} %param.22) | copy-start | bytes 10223620
  1.9 12.5 %collective-permute-start.7 = (bf16[208,832]{1,0:T(8,128)(2,1)S(1)}, bf16[208,832]{1,0:T(8,128)(2,1)S(1)}, u32[]{:S(2)}, u32[]{:S(2)}) collective-permute-start(bf16[208,832]{1,0:T(8,128)(2,1)S(1)} %select_bitcast_fusion), channel_id=1, source_target_pairs={{0,16},{16,0},{1,17},{17,1},{2,18},{18,2},{3,19},{19,3},{4,20},{20... | collective-permute-start | bytes 1038344 | tf_op jit(solution)/shard_map/ppermute | solution.py:145
  4.9 14.2 %collective-permute-start = (bf16[416,448]{1,0:T(8,128)(2,1)}, bf16[416,448]{1,0:T(8,128)(2,1)}, u32[]{:S(2)}, u32[]{:S(2)}) collective-permute-start(bf16[416,448]{1,0:T(8,128)(2,1)} %bitcast.49), channel_id=1, source_target_pairs={{0,8},{4,12},{8,0},{12,4},{1,9},{5,13},{9,1},{13,5},{2,10},{6,14},... | collective-permute-start | bytes 1118216 | tf_op jit(solution)/shard_map/ppermute | solution.py:149
  6.5 16.4 %collective-permute-start.1 = (bf16[416,448]{1,0:T(8,128)(2,1)}, bf16[416,448]{1,0:T(8,128)(2,1)}, u32[]{:S(2)}, u32[]{:S(2)}) collective-permute-start(bf16[416,448]{1,0:T(8,128)(2,1)} %bitcast.50), channel_id=1, source_target_pairs={{0,16},{16,0},{1,17},{17,1},{2,18},{18,2},{3,19},{19,3},{4,20},{20... | collective-permute-start | bytes 1118216 | tf_op jit(solution)/shard_map/ppermute | solution.py:145
  7.0 17.6 %collective-permute-start.3 = (bf16[416,448]{1,0:T(8,128)(2,1)}, bf16[416,448]{1,0:T(8,128)(2,1)S(1)}, u32[]{:S(2)}, u32[]{:S(2)}) collective-permute-start(bf16[416,448]{1,0:T(8,128)(2,1)} %bitcast.51), channel_id=1, source_target_pairs={{0,4},{4,0},{8,12},{12,8},{1,5},{5,1},{9,13},{13,9},{2,6},{6,2},{1... | collective-permute-start | bytes 1118216 | tf_op jit(solution)/shard_map/ppermute | solution.py:153
  14.4 11.5 %collective-permute-start.8 = (bf16[208,832]{1,0:T(8,128)(2,1)S(1)}, bf16[208,832]{1,0:T(8,128)(2,1)S(1)}, u32[]{:S(2)}, u32[]{:S(2)}) collective-permute-start(bf16[208,832]{1,0:T(8,128)(2,1)S(1)} %collective-permute-done.7.refs_12_.refs_1_.refs_3_), channel_id=1, source_target_pairs={{0,1},{1,0},{2,3},{3,2},{4,5},{5,4},{6,7},{7,6},{8,9},{9,8},{10,11... | collective-permute-start | bytes 1038344 | tf_op jit(solution)/shard_map/ppermute | solution.py:158
  19.2 18.8 %collective-permute-start.10 = (bf16[128,1664]{1,0:T(8,128)(2,1)}, bf16[128,1664]{1,0:T(8,128)(2,1)}, u32[]{:S(2)}, u32[]{:S(2)}) collective-permute-start(bf16[128,1664]{1,0:T(8,128)(2,1)} %shard_map.143), channel_id=1, source_target_pairs={{0,8},{4,12},{8,0},{12,4},{1,9},{5,13},{9,1},{13,5},{2,10},{6,14},... | collective-permute-start | bytes 1277960 | tf_op jit(solution)/shard_map/ppermute | solution.py:149
  22.9 15.1 %collective-permute-start.2 = (bf16[416,448]{1,0:T(8,128)(2,1)}, bf16[416,448]{1,0:T(8,128)(2,1)}, u32[]{:S(2)}, u32[]{:S(2)}) collective-permute-start(bf16[416,448]{1,0:T(8,128)(2,1)} %collective-permute-done.1.refs_1_.refs_2_), channel_id=1, source_target_pairs={{0,8},{4,12},{8,0},{12,4},{1,9},{5,13},{9,1},{13,5},{2,10},{6,14},... | collective-permute-start | bytes 1118216 | tf_op jit(solution)/shard_map/ppermute | solution.py:149
  24.6 13.4 %collective-permute-start.5 = (bf16[416,448]{1,0:T(8,128)(2,1)}, bf16[416,448]{1,0:T(8,128)(2,1)}, u32[]{:S(2)}, u32[]{:S(2)}) collective-permute-start(bf16[416,448]{1,0:T(8,128)(2,1)} %collective-permute-done.1.refs_1_.refs_2_), channel_id=1, source_target_pairs={{0,4},{4,0},{8,12},{12,8},{1,5},{5,1},{9,13},{13,9},{2,6},{6,2},{1... | collective-permute-start | bytes 1118216 | tf_op jit(solution)/shard_map/ppermute | solution.py:153
  24.6 13.3 %collective-permute-start.4 = (bf16[416,448]{1,0:T(8,128)(2,1)}, bf16[416,448]{1,0:T(8,128)(2,1)}, u32[]{:S(2)}, u32[]{:S(2)}) collective-permute-start(bf16[416,448]{1,0:T(8,128)(2,1)} %collective-permute-done.refs_1_.refs_2_), channel_id=1, source_target_pairs={{0,4},{4,0},{8,12},{12,8},{1,5},{5,1},{9,13},{13,9},{2,6},{6,2},{1... | collective-permute-start | bytes 1118216 | tf_op jit(solution)/shard_map/ppermute | solution.py:153
  26.7 11.0 %collective-permute-start.9 = (bf16[208,832]{1,0:T(8,128)(2,1)}, bf16[208,832]{1,0:T(8,128)(2,1)}, u32[]{:S(2)}, u32[]{:S(2)}) collective-permute-start(bf16[208,832]{1,0:T(8,128)(2,1)} %shard_map.140), channel_id=1, source_target_pairs={{0,16},{16,0},{1,17},{17,1},{2,18},{18,2},{3,19},{19,3},{4,20},{20... | collective-permute-start | bytes 1038344 | tf_op jit(solution)/shard_map/ppermute | solution.py:145
  39.7 20.3 %collective-permute-start.11 = (bf16[832,512]{1,0:T(8,128)(2,1)S(1)}, bf16[832,512]{1,0:T(8,128)(2,1)}, u32[]{:S(2)}, u32[]{:S(2)}) collective-permute-start(bf16[832,512]{1,0:T(8,128)(2,1)S(1)} %get-tuple-element.35), channel_id=1, source_target_pairs={{0,16},{16,0},{1,17},{17,1},{2,18},{18,2},{3,19},{19,3},{4,20},{20... | collective-permute-start | bytes 2555912 | tf_op jit(solution)/shard_map/ppermute | solution.py:145
  41.3 36.4 %collective-permute-start.22 = (bf16[416,1664]{1,0:T(8,128)(2,1)}, bf16[416,1664]{1,0:T(8,128)(2,1)}, u32[]{:S(2)}, u32[]{:S(2)}) collective-permute-start(bf16[416,1664]{1,0:T(8,128)(2,1)} %refs_16_.1), channel_id=1, source_target_pairs={{0,4},{4,0},{8,12},{12,8},{1,5},{5,1},{9,13},{13,9},{2,6},{6,2},{1... | collective-permute-start | bytes 4153352 | tf_op jit(solution)/shard_map/ppermute | solution.py:153
  41.3 4.2 %collective-permute-start.6 = (bf16[416,448]{1,0:T(8,128)(2,1)}, bf16[416,448]{1,0:T(8,128)(2,1)S(1)}, u32[]{:S(2)}, u32[]{:S(2)}) collective-permute-start(bf16[416,448]{1,0:T(8,128)(2,1)} %collective-permute-done.2.refs_3_.refs_5_), channel_id=1, source_target_pairs={{0,4},{4,0},{8,12},{12,8},{1,5},{5,1},{9,13},{13,9},{2,6},{6,2},{1... | collective-permute-start | bytes 1118216 | tf_op jit(solution)/shard_map/ppermute | solution.py:153
  44.0 24.4 %collective-permute-start.15 = (bf16[288,1664]{1,0:T(8,128)(2,1)}, bf16[288,1664]{1,0:T(8,128)(2,1)}, u32[]{:S(2)}, u32[]{:S(2)}) collective-permute-start(bf16[288,1664]{1,0:T(8,128)(2,1)} %shard_map.146), channel_id=1, source_target_pairs={{0,8},{4,12},{8,0},{12,4},{1,9},{5,13},{9,1},{13,5},{2,10},{6,14},... | collective-permute-start | bytes 2875400 | tf_op jit(solution)/shard_map/ppermute | solution.py:149
  60.0 15.4 %collective-permute-start.12 = (bf16[208,896]{1,0:T(8,128)(2,1)}, bf16[208,896]{1,0:T(8,128)(2,1)}, u32[]{:S(2)}, u32[]{:S(2)}) collective-permute-start(bf16[208,896]{1,0:T(8,128)(2,1)} %get-tuple-element.36.refs_8_), channel_id=1, source_target_pairs={{0,8},{4,12},{8,0},{12,4},{1,9},{5,13},{9,1},{13,5},{2,10},{6,14},... | collective-permute-start | bytes 1118216 | tf_op jit(solution)/shard_map/ppermute | solution.py:149
  60.9 14.5 %collective-permute-start.13 = (bf16[208,896]{1,0:T(8,128)(2,1)}, bf16[208,896]{1,0:T(8,128)(2,1)}, u32[]{:S(2)}, u32[]{:S(2)}) collective-permute-start(bf16[208,896]{1,0:T(8,128)(2,1)} %get-tuple-element.36.refs_8_), channel_id=1, source_target_pairs={{0,16},{16,0},{1,17},{17,1},{2,18},{18,2},{3,19},{19,3},{4,20},{20... | collective-permute-start | bytes 1118216 | tf_op jit(solution)/shard_map/ppermute | solution.py:145
  61.7 26.1 %collective-permute-start.17 = (bf16[832,512]{1,0:T(8,128)(2,1)}, bf16[832,512]{1,0:T(8,128)(2,1)}, u32[]{:S(2)}, u32[]{:S(2)}) collective-permute-start(bf16[832,512]{1,0:T(8,128)(2,1)} %get-tuple-element.40.up_got), channel_id=1, source_target_pairs={{0,1},{1,0},{2,3},{3,2},{4,5},{5,4},{6,7},{7,6},{8,9},{9,8},{10,11... | collective-permute-start | bytes 2555912 | tf_op jit(solution)/shard_map/ppermute | solution.py:158
  75.5 19.6 %collective-permute-start.24 = (bf16[288,1664]{1,0:T(8,128)(2,1)}, bf16[288,1664]{1,0:T(8,128)(2,1)S(1)}, u32[]{:S(2)}, u32[]{:S(2)}) collective-permute-start(bf16[288,1664]{1,0:T(8,128)(2,1)} %get-tuple-element.42.refs_18_), channel_id=1, source_target_pairs={{0,4},{4,0},{8,12},{12,8},{1,5},{5,1},{9,13},{13,9},{2,6},{6,2},{1... | collective-permute-start | bytes 2875400 | tf_op jit(solution)/shard_map/ppermute | solution.py:153
  75.6 12.2 %collective-permute-start.16 = (bf16[832,256]{1,0:T(8,128)(2,1)S(1)}, bf16[832,256]{1,0:T(8,128)(2,1)S(1)}, u32[]{:S(2)}, u32[]{:S(2)}) collective-permute-start(bf16[832,256]{1,0:T(8,128)(2,1)S(1)} %get-tuple-element.39), channel_id=1, source_target_pairs={{0,16},{16,0},{1,17},{17,1},{2,18},{18,2},{3,19},{19,3},{4,20},{20... | collective-permute-start | bytes 1277960 | tf_op jit(solution)/shard_map/ppermute | solution.py:145
  76.2 11.0 %collective-permute-start.14 = (bf16[208,896]{1,0:T(8,128)(2,1)}, bf16[208,896]{1,0:T(8,128)(2,1)S(1)}, u32[]{:S(2)}, u32[]{:S(2)}) collective-permute-start(bf16[208,896]{1,0:T(8,128)(2,1)} %collective-permute-done.13.refs_6_.refs_10_), channel_id=1, source_target_pairs={{0,8},{4,12},{8,0},{12,4},{1,9},{5,13},{9,1},{13,5},{2,10},{6,14},... | collective-permute-start | bytes 1118216 | tf_op jit(solution)/shard_map/ppermute | solution.py:149
  77.7 10.6 %collective-permute-start.18 = (bf16[208,896]{1,0:T(8,128)(2,1)}, bf16[208,896]{1,0:T(8,128)(2,1)S(1)}, u32[]{:S(2)}, u32[]{:S(2)}) collective-permute-start(bf16[208,896]{1,0:T(8,128)(2,1)} %get-tuple-element.36.refs_8_), channel_id=1, source_target_pairs={{0,4},{4,0},{8,12},{12,8},{1,5},{5,1},{9,13},{13,9},{2,6},{6,2},{1... | collective-permute-start | bytes 1118216 | tf_op jit(solution)/shard_map/ppermute | solution.py:153
  87.1 5.1 %collective-permute-start.23 = (bf16[128,1664]{1,0:T(8,128)(2,1)}, bf16[128,1664]{1,0:T(8,128)(2,1)S(1)}, u32[]{:S(2)}, u32[]{:S(2)}) collective-permute-start(bf16[128,1664]{1,0:T(8,128)(2,1)} %get-tuple-element.41.refs_17_), channel_id=1, source_target_pairs={{0,4},{4,0},{8,12},{12,8},{1,5},{5,1},{9,13},{13,9},{2,6},{6,2},{1... | collective-permute-start | bytes 1277960 | tf_op jit(solution)/shard_map/ppermute | solution.py:153
  87.8 1.9 %collective-permute-start.19 = (bf16[208,896]{1,0:T(8,128)(2,1)}, bf16[208,896]{1,0:T(8,128)(2,1)S(1)}, u32[]{:S(2)}, u32[]{:S(2)}) collective-permute-start(bf16[208,896]{1,0:T(8,128)(2,1)} %collective-permute-done.12.refs_7_.refs_9_), channel_id=1, source_target_pairs={{0,4},{4,0},{8,12},{12,8},{1,5},{5,1},{9,13},{13,9},{2,6},{6,2},{1... | collective-permute-start | bytes 1118216 | tf_op jit(solution)/shard_map/ppermute | solution.py:153
  87.8 3.9 %collective-permute-start.20 = (bf16[208,896]{1,0:T(8,128)(2,1)}, bf16[208,896]{1,0:T(8,128)(2,1)S(1)}, u32[]{:S(2)}, u32[]{:S(2)}) collective-permute-start(bf16[208,896]{1,0:T(8,128)(2,1)} %collective-permute-done.13.refs_6_.refs_10_), channel_id=1, source_target_pairs={{0,4},{4,0},{8,12},{12,8},{1,5},{5,1},{9,13},{13,9},{2,6},{6,2},{1... | collective-permute-start | bytes 1118216 | tf_op jit(solution)/shard_map/ppermute | solution.py:153
  88.3 5.4 %collective-permute-start.21 = (bf16[208,896]{1,0:T(8,128)(2,1)S(1)}, bf16[208,896]{1,0:T(8,128)(2,1)S(1)}, u32[]{:S(2)}, u32[]{:S(2)}) collective-permute-start(bf16[208,896]{1,0:T(8,128)(2,1)S(1)} %shard_map.148.refs_11_), channel_id=1, source_target_pairs={{0,4},{4,0},{8,12},{12,8},{1,5},{5,1},{9,13},{13,9},{2,6},{6,2},{1... | collective-permute-start | bytes 1118216 | tf_op jit(solution)/shard_map/ppermute | solution.py:153
  89.7 18.4 %collective-permute-start.25 = (bf16[832,256]{1,0:T(8,128)(2,1)S(1)}, bf16[832,256]{1,0:T(8,128)(2,1)S(1)}, u32[]{:S(2)}, u32[]{:S(2)}) collective-permute-start(bf16[832,256]{1,0:T(8,128)(2,1)S(1)} %get-tuple-element.45), channel_id=1, source_target_pairs={{0,16},{16,0},{1,17},{17,1},{2,18},{18,2},{3,19},{19,3},{4,20},{20... | collective-permute-start | bytes 1277960 | tf_op jit(solution)/shard_map/ppermute | solution.py:145
  91.7 26.6 %collective-permute-start.26 = (bf16[416,832]{1,0:T(8,128)(2,1)S(1)}, bf16[416,832]{1,0:T(8,128)(2,1)S(1)}, u32[]{:S(2)}, u32[]{:S(2)}) collective-permute-start(bf16[416,832]{1,0:T(8,128)(2,1)S(1)} %get-tuple-element.47), channel_id=1, source_target_pairs={{0,16},{16,0},{1,17},{17,1},{2,18},{18,2},{3,19},{19,3},{4,20},{20... | collective-permute-start | bytes 2076680 | tf_op jit(solution)/shard_map/ppermute | solution.py:145
  92.2 41.5 %collective-permute-start.29 = (bf16[416,832]{1,0:T(8,128)(2,1)S(1)}, bf16[416,832]{1,0:T(8,128)(2,1)S(1)}, u32[]{:S(2)}, u32[]{:S(2)}) collective-permute-start(bf16[416,832]{1,0:T(8,128)(2,1)S(1)} %get-tuple-element.58), channel_id=1, source_target_pairs={{0,16},{16,0},{1,17},{17,1},{2,18},{18,2},{3,19},{19,3},{4,20},{20... | collective-permute-start | bytes 2076680 | tf_op jit(solution)/shard_map/ppermute | solution.py:145
  93.7 25.9 %collective-permute-start.27 = (bf16[832,256]{1,0:T(8,128)(2,1)S(1)}, bf16[832,256]{1,0:T(8,128)(2,1)S(1)}, u32[]{:S(2)}, u32[]{:S(2)}) collective-permute-start(bf16[832,256]{1,0:T(8,128)(2,1)S(1)} %collective-permute-done.16.refs_1_.refs_23_.refs_0_), channel_id=1, source_target_pairs={{0,1},{1,0},{2,3},{3,2},{4,5},{5,4},{6,7},{7,6},{8,9},{9,8},{10,11... | collective-permute-start | bytes 1277960 | tf_op jit(solution)/shard_map/ppermute | solution.py:158
  108.2 11.5 %collective-permute-start.28 = (bf16[832,256]{1,0:T(8,128)(2,1)S(1)}, bf16[832,256]{1,0:T(8,128)(2,1)S(1)}, u32[]{:S(2)}, u32[]{:S(2)}) collective-permute-start(bf16[832,256]{1,0:T(8,128)(2,1)S(1)} %get-tuple-element.49.refs_1_), channel_id=1, source_target_pairs={{0,1},{1,0},{2,3},{3,2},{4,5},{5,4},{6,7},{7,6},{8,9},{9,8},{10,11... | collective-permute-start | bytes 1277960 | tf_op jit(solution)/shard_map/ppermute | solution.py:158
  118.3 17.6 %collective-permute-start.30 = (bf16[416,832]{1,0:T(8,128)(2,1)S(1)}, bf16[416,832]{1,0:T(8,128)(2,1)S(1)}, u32[]{:S(2)}, u32[]{:S(2)}) collective-permute-start(bf16[416,832]{1,0:T(8,128)(2,1)S(1)} %get-tuple-element.59.refs_0_), channel_id=1, source_target_pairs={{0,1},{1,0},{2,3},{3,2},{4,5},{5,4},{6,7},{7,6},{8,9},{9,8},{10,11... | collective-permute-start | bytes 2076680 | tf_op jit(solution)/shard_map/ppermute | solution.py:158
  122.6 13.2 %collective-permute-start.32 = (bf16[2,208,448]{2,1,0:T(8,128)(2,1)S(1)}, bf16[2,208,448]{2,1,0:T(8,128)(2,1)S(1)}, u32[]{:S(2)}, u32[]{:S(2)}) collective-permute-start(bf16[2,208,448]{2,1,0:T(8,128)(2,1)S(1)} %get-tuple-element.50.refs_4_), channel_id=1, source_target_pairs={{0,4},{4,0},{8,12},{12,8},{1,5},{5,1},{9,13},{13,9},{2,6},{6,2},{1... | collective-permute-start | bytes 1118216 | tf_op jit(solution)/shard_map/ppermute | solution.py:153
  122.7 14.8 %collective-permute-start.35 = (bf16[2,208,448]{2,1,0:T(8,128)(2,1)S(1)}, bf16[2,208,448]{2,1,0:T(8,128)(2,1)S(1)}, u32[]{:S(2)}, u32[]{:S(2)}) collective-permute-start(bf16[2,208,448]{2,1,0:T(8,128)(2,1)S(1)} %get-tuple-element.51.refs_5_), channel_id=1, source_target_pairs={{0,4},{4,0},{8,12},{12,8},{1,5},{5,1},{9,13},{13,9},{2,6},{6,2},{1... | collective-permute-start | bytes 1118216 | tf_op jit(solution)/shard_map/ppermute | solution.py:153
  123.2 16.5 %collective-permute-start.31 = (bf16[2,208,448]{2,1,0:T(8,128)(2,1)S(1)}, bf16[2,208,448]{2,1,0:T(8,128)(2,1)S(1)}, u32[]{:S(2)}, u32[]{:S(2)}) collective-permute-start(bf16[2,208,448]{2,1,0:T(8,128)(2,1)S(1)} %get-tuple-element.52.refs_6_), channel_id=1, source_target_pairs={{0,4},{4,0},{8,12},{12,8},{1,5},{5,1},{9,13},{13,9},{2,6},{6,2},{1... | collective-permute-start | bytes 1118216 | tf_op jit(solution)/shard_map/ppermute | solution.py:153
  133.7 6.0 %collective-permute-start.34 = (bf16[2,208,448]{2,1,0:T(8,128)(2,1)S(1)}, bf16[2,208,448]{2,1,0:T(8,128)(2,1)S(1)}, u32[]{:S(2)}, u32[]{:S(2)}) collective-permute-start(bf16[2,208,448]{2,1,0:T(8,128)(2,1)S(1)} %get-tuple-element.53.refs_7_), channel_id=1, source_target_pairs={{0,4},{4,0},{8,12},{12,8},{1,5},{5,1},{9,13},{13,9},{2,6},{6,2},{1... | collective-permute-start | bytes 1118216 | tf_op jit(solution)/shard_map/ppermute | solution.py:153
  136.0 10.2 %collective-permute-start.33 = (bf16[2,208,448]{2,1,0:T(8,128)(2,1)S(1)}, bf16[2,208,448]{2,1,0:T(8,128)(2,1)S(1)}, u32[]{:S(2)}, u32[]{:S(2)}) collective-permute-start(bf16[2,208,448]{2,1,0:T(8,128)(2,1)S(1)} %add_convert_fusion.3), channel_id=1, source_target_pairs={{0,16},{16,0},{1,17},{17,1},{2,18},{18,2},{3,19},{19,3},{4,20},{20... | collective-permute-start | bytes 1118216 | tf_op jit(solution)/shard_map/ppermute | solution.py:145
  137.7 10.1 %collective-permute-start.36 = (bf16[2,208,448]{2,1,0:T(8,128)(2,1)S(1)}, bf16[2,208,448]{2,1,0:T(8,128)(2,1)S(1)}, u32[]{:S(2)}, u32[]{:S(2)}) collective-permute-start(bf16[2,208,448]{2,1,0:T(8,128)(2,1)S(1)} %add_convert_fusion.1), channel_id=1, source_target_pairs={{0,8},{4,12},{8,0},{12,4},{1,9},{5,13},{9,1},{13,5},{2,10},{6,14},... | collective-permute-start | bytes 1118216 | tf_op jit(solution)/shard_map/ppermute | solution.py:149
  139.3 17.5 %collective-permute-start.39 = (bf16[416,832]{1,0:T(8,128)(2,1)S(1)}, bf16[416,832]{1,0:T(8,128)(2,1)S(1)}, u32[]{:S(2)}, u32[]{:S(2)}) collective-permute-start(bf16[416,832]{1,0:T(8,128)(2,1)S(1)} %collective-permute-done.29.refs_4_.refs_1_), channel_id=1, source_target_pairs={{0,1},{1,0},{2,3},{3,2},{4,5},{5,4},{6,7},{7,6},{8,9},{9,8},{10,11... | collective-permute-start | bytes 2076680 | tf_op jit(solution)/shard_map/ppermute | solution.py:158
  148.2 5.9 %collective-permute-start.37 = (bf16[208,448]{1,0:T(8,128)(2,1)S(1)}, bf16[208,448]{1,0:T(8,128)(2,1)S(1)}, u32[]{:S(2)}, u32[]{:S(2)}) collective-permute-start(bf16[208,448]{1,0:T(8,128)(2,1)S(1)} %get-tuple-element.74), channel_id=1, source_target_pairs={{0,8},{4,12},{8,0},{12,4},{1,9},{5,13},{9,1},{13,5},{2,10},{6,14},... | collective-permute-start | bytes 559112 | tf_op jit(solution)/shard_map/ppermute | solution.py:149
  149.8 5.9 %collective-permute-start.38 = (bf16[208,448]{1,0:T(8,128)(2,1)S(1)}, bf16[208,448]{1,0:T(8,128)(2,1)S(1)}, u32[]{:S(2)}, u32[]{:S(2)}) collective-permute-start(bf16[208,448]{1,0:T(8,128)(2,1)S(1)} %get-tuple-element.72), channel_id=1, source_target_pairs={{0,16},{16,0},{1,17},{17,1},{2,18},{18,2},{3,19},{19,3},{4,20},{20... | collective-permute-start | bytes 559112 | tf_op jit(solution)/shard_map/ppermute | solution.py:145
  156.7 19.6 %copy-start.19 = (s32[1,112]{1,0:T(1,128)S(1)}, s32[1,112]{1,0:T(1,128)}, u32[]{:S(2)}) copy-start(s32[1,112]{1,0:T(1,128)} %refs_4_.1) | copy-start | bytes 1348
  158.1 1.5 collective-permute-start.40
  159.7 5.1 %collective-permute-start.41 = (bf16[416,112]{1,0:T(8,128)(2,1)S(1)}, bf16[416,112]{1,0:T(8,128)(2,1)S(1)}, u32[]{:S(2)}, u32[]{:S(2)}) collective-permute-start(bf16[416,112]{1,0:T(8,128)(2,1)S(1)} %slice_bitcast_fusion.4), channel_id=1, source_target_pairs={{0,8},{4,12},{8,0},{12,4},{1,9},{5,13},{9,1},{13,5},{2,10},{6,14},... | collective-permute-start | bytes 279560 | tf_op jit(solution)/shard_map/ppermute | solution.py:149
  164.8 5.6 %collective-permute-start.42 = (bf16[416,112]{1,0:T(8,128)(2,1)S(1)}, bf16[416,112]{1,0:T(8,128)(2,1)S(1)}, u32[]{:S(2)}, u32[]{:S(2)}) collective-permute-start(bf16[416,112]{1,0:T(8,128)(2,1)S(1)} %fusion.refs_0_), channel_id=1, source_target_pairs={{0,1},{1,0},{2,3},{3,2},{4,5},{5,4},{6,7},{7,6},{8,9},{9,8},{10,11... | collective-permute-start | bytes 279560 | tf_op jit(solution)/shard_map/ppermute | solution.py:158
  165.3 11.1 %collective-permute-start.43 = (bf16[416,112]{1,0:T(8,128)(2,1)S(1)}, bf16[416,112]{1,0:T(8,128)(2,1)S(1)}, u32[]{:S(2)}, u32[]{:S(2)}) collective-permute-start(bf16[416,112]{1,0:T(8,128)(2,1)S(1)} %fusion.refs_0_), channel_id=1, source_target_pairs={{0,2},{1,3},{2,0},{3,1},{4,6},{5,7},{6,4},{7,5},{8,10},{9,11},{10,... | collective-permute-start | bytes 279560 | tf_op jit(solution)/shard_map/ppermute | solution.py:158
  167.9 8.5 %collective-permute-start.44 = (bf16[416,112]{1,0:T(8,128)(2,1)S(1)}, bf16[416,112]{1,0:T(8,128)(2,1)S(1)}, u32[]{:S(2)}, u32[]{:S(2)}) collective-permute-start(bf16[416,112]{1,0:T(8,128)(2,1)S(1)} %fusion.refs_0_), channel_id=1, source_target_pairs={{0,3},{1,2},{2,1},{3,0},{4,7},{5,6},{6,5},{7,4},{8,11},{9,10},{10,... | collective-permute-start | bytes 279560 | tf_op jit(solution)/shard_map/ppermute | solution.py:158
  (24 other events, 200.2 us)

commit v2 on v1

--- a/solution.py
+++ b/solution.py
@@ -14,7 +14,6 @@
 NEG = -1e30
 VMEM_LIMIT = 30 * 1024 * 1024
 SMALL_LIMIT = 24 * 1024 * 1024
-OUT_EARLY = 128
 LOG2_E = 1.4426950408889634
 
 
@@ -289,7 +288,7 @@
 
 
 def project_kernel(*refs):
-    tokens, attended, weights, gain = refs[:8], refs[8:16], refs[16:22], refs[22]
+    tokens, attended, weights, gain = refs[:8], refs[8:16], refs[16:20], refs[20]
     normed, own, tok_scr, att_scr, w_scr, aft_scr, gain_scr, sem = refs[-8:]
     gx, y, core = position()
     width = own.shape[0]
@@ -302,11 +301,10 @@
     bounds = list(range(0, feats, 384))[:-1] + [feats]
     chunks = list(zip(bounds[:-1], bounds[1:]))
     for begin, end in chunks:
-        for dc, parts in enumerate((weights[:3], weights[3:])):
+        for dc, parts in enumerate((weights[:2], weights[2:])):
             here = (y * 2 + (core ^ dc)) * width
             there = ((y ^ 1) * 2 + (core ^ dc)) * width
-            rows = (here, there, there + parts[1].shape[0])
-            for ref, row in zip(parts, rows):
+            for ref, row in zip(parts, (here, there)):
                 at = pl.ds(pl.multiple_of(row, 16), ref.shape[0])
                 pairs.append((ref.at[:, begin:end], w_scr.at[at, begin:end]))
         if begin == 0:
@@ -316,7 +314,7 @@
     first = second = pivot = None
     waited = 0
     for i, (begin, end) in enumerate(chunks):
-        needed = 8 + 6 + 8 + 6 * i
+        needed = 8 + 4 + 8 + 4 * i
         for copy in copies[waited:needed]:
             copy.wait()
         waited = needed
@@ -344,20 +342,26 @@
     lax.fori_loop(0, feats // STEP, write, 0)
 
 
-def up_kernel(normed, up_own, up_got, up_got_row, hidden, norm_scr, up_scr, sem):
+def chunk_places(got, piece):
+    plane = lax.axis_index("row") % 2
+    for i, ref in enumerate(got):
+        place = plane if i < 2 else 1 - plane
+        yield ref, pl.ds(pl.multiple_of((2 * place + i % 2) * piece, 128), piece)
+
+
+def up_kernel(normed, up_own, *refs):
+    got, (hidden, norm_scr, up_scr, sem) = refs[:4], refs[4:]
     gx, y, core = position()
-    plane = lax.axis_index("row") % 2
     feats, units = up_scr.shape
     depth = feats // 2
-    chunk = units // 2
     own_rows = pl.ds(pl.multiple_of(gx * depth, 16), depth)
     other_rows = pl.ds(pl.multiple_of((1 - gx) * depth, 16), depth)
     pairs = [
         (normed, norm_scr),
         (up_own.at[:, pl.ds(pl.multiple_of(gx * units, 128), units)], up_scr.at[own_rows]),
-        (up_got, up_scr.at[other_rows, pl.ds(pl.multiple_of(plane * chunk, 128), chunk)]),
-        (up_got_row, up_scr.at[other_rows, pl.ds(pl.multiple_of((1 - plane) * chunk, 128), chunk)]),
     ]
+    for ref, at in chunk_places(got, units // 4):
+        pairs.append((ref, up_scr.at[other_rows, at]))
     for copy in run_copies(pairs, sem):
         copy.wait()
     for begin in range(0, units, 256):
@@ -369,19 +373,15 @@
 def down_kernel(dc, hidden, down_own, *refs):
     got, outs, (hid_scr, down_scr, sem) = refs[:4], refs[-7:-3], refs[-3:]
     gx, y, core = position()
-    plane = lax.axis_index("row") % 2
     depth = down_own.shape[0]
     units, total = hid_scr.shape
-    chunk = units // 4
     own_rows = pl.ds(pl.multiple_of(gx * depth, 16), depth)
     other_rows = pl.ds(pl.multiple_of((1 - gx) * depth, 16), depth)
     pairs = [
         (hidden, hid_scr),
         (down_own.at[:, pl.ds(pl.multiple_of(gx * units, 128), units)], down_scr.at[own_rows]),
     ]
-    for i, ref in enumerate(got):
-        place = plane if i < 2 else 1 - plane
-        at = pl.ds(pl.multiple_of((2 * place + i % 2) * chunk, 128), chunk)
+    for ref, at in chunk_places(got, units // 4):
         pairs.append((ref, down_scr.at[other_rows, at]))
     for copy in run_copies(pairs, sem):
         copy.wait()
@@ -522,29 +522,29 @@
 
     over_x, over_y = swap_x(tok), swap_y(tok)
     qkv_got = swap_x(first)
-    (key_piece,) = after((over_x,), (rows_of(w_key.T, their_row, cols),))
+    (key_piece,) = after((qkv_got,), (rows_of(w_key.T, their_row, cols),))
     qkv_got_key = swap_x(key_piece)
     held = [tok, over_y, over_x, swap_y(over_x)]
     tok_shards = held + [swap_core(part) for part in held]
-    down_pieces = [
-        lax.dynamic_slice_in_dim(down, theirs + i * (chunk // 2), chunk // 2, 1) for i in range(2)
-    ]
-    (up_piece,) = after((qkv_got,), (lax.dynamic_slice_in_dim(w_up, theirs, chunk, 1),))
-    early = OUT_EARLY
-    (out_early,) = after((over_y,), (w_out[:early],))
-    (out_late,) = after((over_x, over_y, qkv_got), (w_out[early:],))
-    out_over_y = [swap_y(out_early), swap_y(out_late)]
+    piece = chunk // 2
+    down_a, down_b = (lax.dynamic_slice_in_dim(down, theirs + i * piece, piece, 1) for i in range(2))
+    up_a, up_b = (lax.dynamic_slice_in_dim(w_up, theirs + i * piece, piece, 1) for i in range(2))
+    (up_a,) = after((qkv_got, over_x), (up_a,))
+    up_got_a = swap_x(up_a)
     qkv_got_row = swap_row(qkv_got, 1)
-    up_piece, *down_pieces = after(
-        (qkv_got_row, qkv_got_key, held[3], *tok_shards[4:7], out_over_y[0]), (up_piece, *down_pieces)
-    )
-    up_got = swap_x(up_piece)
+    (out_piece,) = after((held[3],), (w_out,))
+    out_over_y = [swap_y(out_piece)]
+    up_b, down_a, down_b = after(
+        (qkv_got_row, qkv_got_key, held[3], *tok_shards[4:7], out_piece), (up_b, down_a, down_b)
+    )
+    up_got_b, down_got_a = swap_x(up_b), swap_x(down_a)
+    up_got_a_row = swap_row(up_got_a, 1)
 
     (attended,) = call(
         attention_kernel,
-        (*tok_shards, gain_attn, w_query.T, w_key.T, w_value.T, qkv_got, qkv_got_row, qkv_got_key, segments),
+        (*tok_shards, gain_attn, w_query.T, w_key.T, w_value.T, qkv_got, qkv_got_row, qkv_got_key, segments, up_got_a),
         [((cols, total), sixteen)],
-        (True,) * 8 + (False,) + (True,) * 6 + (False,),
+        (True,) * 8 + (False,) + (True,) * 6 + (False, True),
         [
             pltpu.VMEM((2, feats, count), sixteen),
             pltpu.VMEM((feats, total), sixteen),
@@ -557,54 +557,49 @@
         ],
         2 * total * feats * total_cols + 4 * total * total * cols,
     )
-    attended, up_got = after((), (attended, up_got))
+    attended, up_got_b, down_got_a = after((up_got_a_row,), (attended, up_got_b, down_got_a))
     over_x, over_y = swap_x(attended), swap_y(attended)
-    up_got_row = swap_row(up_got, 1)
+    up_got_b_row, down_got_a_row = swap_row(up_got_b, 1), swap_row(down_got_a, 1)
     slots = w_merge.shape[0]
     merge_pieces = [rows_of(w_merge, plane * (slots // 2) + i, 1)[0] for i in range(2)]
-    *out_over_y, down_piece_a, down_piece_b, merge_a, merge_b = after(
-        (over_x, over_y), (*out_over_y, *down_pieces, *merge_pieces)
-    )
-    merge_pieces = [merge_a, merge_b]
-    down_got_a, down_got_b = swap_x(down_piece_a), swap_x(down_piece_b)
-    (diagonal,) = after((down_got_a, up_got_row), (swap_y(over_x),))
+    *out_over_y, down_b = after((over_x, over_y, up_got_b_row), (*out_over_y, down_b))
+    down_got_b = swap_x(down_b)
+    diagonal, *merge_pieces = after((down_got_a_row, down_got_b), (swap_y(over_x), *merge_pieces))
     held = [attended, over_y, over_x, diagonal]
     att_shards = held + [swap_core(part) for part in held]
     out_parts = [w_out, *out_over_y]
     out_parts = out_parts + [swap_core(part) for part in out_parts]
-    down_got_a_row = swap_row(down_got_a, 1)
+    down_got_b_row = swap_row(down_got_b, 1)
     normed, own = call(
         project_kernel,
-        (*tok_shards, *att_shards, *out_parts, gain_mlp, down_got_a, up_got_row),
+        (*tok_shards, *att_shards, *out_parts, gain_mlp, down_got_b, down_got_a_row),
         [((feats, total), sixteen), ((width, count), sixteen)],
-        (True,) * 22 + (False, True, True),
+        (True,) * 20 + (False, True, True),
         [
             pltpu.VMEM((2, feats, count), sixteen),
             pltpu.VMEM((feats, total), sixteen),
             pltpu.VMEM((feats, feats), sixteen),
             pltpu.VMEM((feats, total), sixteen),
             pltpu.VMEM((feats, 8), jnp.float32),
-            pltpu.SemaphoreType.DMA((40,)),
+            pltpu.SemaphoreType.DMA((32,)),
         ],
         2 * total * feats * feats,
     )
     merge_got = [swap_x(part) for part in merge_pieces]
-    normed, down_got_b = after((), (normed, down_got_b))
+    normed, merge_got[0] = after((), (normed, merge_got[0]))
     (hidden,) = call(
         up_kernel,
-        (normed, w_up, up_got, up_got_row),
+        (normed, w_up, up_got_a, up_got_b, up_got_a_row, up_got_b_row),
         [((units, total), sixteen)],
-        (True,) * 4,
+        (True,) * 6,
         [
             pltpu.VMEM((feats, total), sixteen),
             pltpu.VMEM((feats, units), sixteen),
-            pltpu.SemaphoreType.DMA((4,)),
+            pltpu.SemaphoreType.DMA((6,)),
         ],
         2 * total * feats * units,
         limit=SMALL_LIMIT,
     )
-    down_got_b_row = swap_row(down_got_b, 1)
-    hidden, merge_got[0] = after((), (hidden, merge_got[0]))
     pair = ((2, half, count), sixteen)
 
     def down_part(dc, *others):

time: 178 us -> 169 us (0.949)
  waiting for transfers between devices: 78.6 us -> 74.1 us
  starting transfers between devices: 40.9 us -> 38 us
    ppermute x9 -> x8, waiting for transfers between devices: 30.3 us -> 19 us  [swap_y(): return lax.ppermute(arr, 'gy', [(i, i ^ 2) for i in range(4)])]
    ppermute x9 -> x10, waiting for transfers between devices: 9.27 us -> 19.7 us  [swap_row(): return lax.ppermute(arr, 'row', [(i, i ^ step) for i in range(count)])]
    slice x2 -> x0, local copies, waits for them, and re-layouts: 3.99 us -> none  [the longest x1 2.2 us: fast_body(): out_late, = after((over_x, over_y, qkv_got), (w_out[early:],))]
    ppermute x9 -> x8, starting transfers between devices: 12.5 us -> 8.8 us  [swap_y(): return lax.ppermute(arr, 'gy', [(i, i ^ 2) for i in range(4)])]
    ppermute x11 -> x12, waiting for transfers between devices: 36.2 us -> 32.6 us  [swap_x(): return lax.ppermute(arr, 'gx', [(0, 1), (1, 0)])]
    ppermute x11 -> x12, starting transfers between devices: 14 us -> 14.9 us  [swap_x(): return lax.ppermute(arr, 'gx', [(0, 1), (1, 0)])]
    unnamed x54 -> x73, local copies, waits for them, and re-layouts: 4.43 us -> 5.21 us
    pallas_call x19 -> x17, Pallas kernels: 42.5 us -> 42.8 us  [call(): pl.pallas_call(kernel, out_shape=outs, in_specs=[pl.BlockSpec(memory_spac...]
  transfers between devices with their start and end apart: 45 -> 45, of which waited for: 20 -> 22; matrix products, arithmetic and copies ran while one was open for 5% -> 6% of each run, Pallas kernels for 23% -> 24%
where the time goes in v2:
time: 169 us
  waiting for transfers between devices  74.1 us (44%)
  Pallas kernels  42.8 us (25%)
  starting transfers between devices  38 us (22%)
  local copies, waits for them, and re-layouts  10.7 us (6%)
  other arithmetic  1.85 us (1%)
    pallas_call x17, Pallas kernels, call(): pl.pallas_call(kernel, out_shape=outs, in_specs=[pl.BlockSpec(memory_spac...  42.8 us
    ppermute x12, waiting for transfers between devices, swap_x(): return lax.ppermute(arr, 'gx', [(0, 1), (1, 0)])  32.6 us
    ppermute x10, waiting for transfers between devices, swap_row(): return lax.ppermute(arr, 'row', [(i, i ^ step) for i in range(count)])  19.7 us
    ppermute x8, waiting for transfers between devices, swap_y(): return lax.ppermute(arr, 'gy', [(i, i ^ 2) for i in range(4)])  19 us
    ppermute x12, starting transfers between devices, swap_x(): return lax.ppermute(arr, 'gx', [(0, 1), (1, 0)])  14.9 us
    ppermute x10, starting transfers between devices, swap_row(): return lax.ppermute(arr, 'row', [(i, i ^ step) for i in range(count)])  11.8 us
    ppermute x8, starting transfers between devices, swap_y(): return lax.ppermute(arr, 'gy', [(i, i ^ 2) for i in range(4)])  8.8 us
    unnamed x73, local copies, waits for them, and re-layouts  5.21 us
  transfers between devices with their start and end apart: 45, of which 22 were waited for; matrix products, arithmetic and copies ran while one was open for 6% of the time, Pallas kernels for 24%

profile of v2, /device:TPU:0, one launch (start us, length us, event | category | flops | bytes accessed | tf_op | source)
XLA Modules:
  0.0 168.6 jit_solution(6416294251302622714)
XLA Ops:
  0.6 3.0 %collective-permute-start.1 = (bf16[416,448]{1,0:T(8,128)(2,1)}, bf16[416,448]{1,0:T(8,128)(2,1)}, u32[]{:S(2)}, u32[]{:S(2)}) collective-permute-start(bf16[416,448]{1,0:T(8,128)(2,1)} %bitcast.49), channel_id=1, source_target_pairs={{0,16},{16,0},{1,17},{17,1},{2,18},{18,2},{3,19},{19,3},{4,20},{20... | collective-permute-start | bytes 1118216 | tf_op jit(solution)/shard_map/ppermute | solution.py:144
  3.6 1.2 select_bitcast_fusion
  4.9 9.7 %collective-permute-done.1.refs_2_ = bf16[416,448]{1,0:T(8,128)(2,1)} collective-permute-done((bf16[416,448]{1,0:T(8,128)(2,1)}, bf16[416,448]{1,0:T(8,128)(2,1)}, u32[]{:S(2)}, u32[]{:S(2)}) %collective-permute-start.1) | collective-permute-done | bytes 372768 | tf_op jit(solution)/shard_map/ppermute | solution.py:144
  14.6 2.1 %collective-permute-start.2 = (bf16[416,448]{1,0:T(8,128)(2,1)}, bf16[416,448]{1,0:T(8,128)(2,1)}, u32[]{:S(2)}, u32[]{:S(2)}) collective-permute-start(bf16[416,448]{1,0:T(8,128)(2,1)} %collective-permute-done.1.refs_2_), channel_id=1, source_target_pairs={{0,8},{4,12},{8,0},{12,4},{1,9},{5,13},{9,1},{13,5},{2,10},{6,14},... | collective-permute-start | bytes 1118216 | tf_op jit(solution)/shard_map/ppermute | solution.py:148
  16.7 1.8 %dynamic-slice_bitcast_fusion.4.refs_0_ = bf16[208,832]{1,0:T(8,128)(2,1)} fusion(bf16[832,416]{0,1:T(8,128)(2,1)} %param.17, s32[]{:T(128)S(6)} %select_n.39), kind=kLoop, calls=%fused_computation.9 | loop fusion | bytes 692228 | tf_op jit(solution)/shard_map/dynamic_slice | solution.py:483
  18.5 3.2 %collective-permute-done.7.refs_1_.refs_12_ = bf16[208,832]{1,0:T(8,128)(2,1)S(1)} collective-permute-done((bf16[208,832]{1,0:T(8,128)(2,1)S(1)}, bf16[208,832]{1,0:T(8,128)(2,1)S(1)}, u32[]{:S(2)}, u32[]{:S(2)}) %collective-permute-start.7) | collective-permute-done | bytes 346144 | tf_op jit(solution)/shard_map/ppermute | solution.py:144
  22.4 1.7 %collective-permute-start.9 = (bf16[208,832]{1,0:T(8,128)(2,1)}, bf16[208,832]{1,0:T(8,128)(2,1)}, u32[]{:S(2)}, u32[]{:S(2)}) collective-permute-start(bf16[208,832]{1,0:T(8,128)(2,1)} %shard_map.140), channel_id=1, source_target_pairs={{0,16},{16,0},{1,17},{17,1},{2,18},{18,2},{3,19},{19,3},{4,20},{20... | collective-permute-start | bytes 1038344 | tf_op jit(solution)/shard_map/ppermute | solution.py:144
  24.2 2.6 %copy.37.refs_0_ = bf16[416,1664]{1,0:T(8,128)(2,1)} copy(bf16[416,1664]{1,0:T(8,128)(2,1)} %refs_16_.1) | data formatting | bytes 2768896
  26.7 1.6 collective-permute-start.8
  28.3 1.5 collective-permute-start.18
  29.8 1.2 constant_dynamic-slice_fusion
  31.0 1.0 copy-done.7
  32.0 4.8 %collective-permute-done.refs_1_ = bf16[416,448]{1,0:T(8,128)(2,1)} collective-permute-done((bf16[416,448]{1,0:T(8,128)(2,1)}, bf16[416,448]{1,0:T(8,128)(2,1)}, u32[]{:S(2)}, u32[]{:S(2)}) %collective-permute-start) | collective-permute-done | bytes 372768 | tf_op jit(solution)/shard_map/ppermute | solution.py:148
  36.9 2.0 %collective-permute-start.10 = (bf16[832,256]{1,0:T(8,128)(2,1)S(1)}, bf16[832,256]{1,0:T(8,128)(2,1)S(1)}, u32[]{:S(2)}, u32[]{:S(2)}) collective-permute-start(bf16[832,256]{1,0:T(8,128)(2,1)S(1)} %shard_map.141), channel_id=1, source_target_pairs={{0,16},{16,0},{1,17},{17,1},{2,18},{18,2},{3,19},{19,3},{4,20},{20... | collective-permute-start | bytes 1277960 | tf_op jit(solution)/shard_map/ppermute | solution.py:144
  41.5 2.0 %collective-permute-start.12 = (bf16[832,256]{1,0:T(8,128)(2,1)S(1)}, bf16[832,256]{1,0:T(8,128)(2,1)S(1)}, u32[]{:S(2)}, u32[]{:S(2)}) collective-permute-start(bf16[832,256]{1,0:T(8,128)(2,1)S(1)} %get-tuple-element.34), channel_id=1, source_target_pairs={{0,16},{16,0},{1,17},{17,1},{2,18},{18,2},{3,19},{19,3},{4,20},{20... | collective-permute-start | bytes 1277960 | tf_op jit(solution)/shard_map/ppermute | solution.py:144
  43.5 3.5 %collective-permute-done.10.refs_16_.refs_0_ = bf16[832,256]{1,0:T(8,128)(2,1)S(1)} collective-permute-done((bf16[832,256]{1,0:T(8,128)(2,1)S(1)}, bf16[832,256]{1,0:T(8,128)(2,1)S(1)}, u32[]{:S(2)}, u32[]{:S(2)}) %collective-permute-start.10) | collective-permute-done | bytes 426016 | tf_op jit(solution)/shard_map/ppermute | solution.py:144
  46.9 1.4 collective-permute-start.13
  48.4 14.6 %shard_map.142.refs_0_ = bf16[208,896]{1,0:T(8,128)(2,1)} custom-call(bf16[416,448]{1,0:T(8,128)(2,1)S(1)} %bitcast.52, bf16[416,448]{1,0:T(8,128)(2,1)} %collective-permute-done.refs_1_, bf16[416,448]{1,0:T(8,128)(2,1)} %collective-permute-done.1.refs_2_, bf16[416,448]{1,0:T(8,128)(2,1)} %collective-permute-done.2.refs_3_.refs_1_.refs_5_, ...), custom_call_target="tpu_custom_call" | custom-call | flops 2528641024 | bytes 6533120 | tf_op jit(solution)/shard_map/pallas_call | solution.py:458
  63.3 2.1 %collective-permute-start.19 = (bf16[832,256]{1,0:T(8,128)(2,1)S(1)}, bf16[832,256]{1,0:T(8,128)(2,1)S(1)}, u32[]{:S(2)}, u32[]{:S(2)}) collective-permute-start(bf16[832,256]{1,0:T(8,128)(2,1)S(1)} %get-tuple-element.38.refs_1_), channel_id=1, source_target_pairs={{0,1},{1,0},{2,3},{3,2},{4,5},{5,4},{6,7},{7,6},{8,9},{9,8},{10,11... | collective-permute-start | bytes 1277960 | tf_op jit(solution)/shard_map/ppermute | solution.py:157
  65.4 1.5 collective-permute-start.14
  66.9 1.5 collective-permute-start.15
  68.4 6.5 %collective-permute-done.14.refs_3_.refs_9_ = bf16[208,896]{1,0:T(8,128)(2,1)S(1)} collective-permute-done((bf16[208,896]{1,0:T(8,128)(2,1)}, bf16[208,896]{1,0:T(8,128)(2,1)S(1)}, u32[]{:S(2)}, u32[]{:S(2)}) %collective-permute-start.14) | collective-permute-done | bytes 372768 | tf_op jit(solution)/shard_map/ppermute | solution.py:148
  74.9 1.3 collective-permute-done.15.refs_2_.refs_10_
  77.4 0.9 collective-permute-start.16
  78.3 10.3 %collective-permute-done.17.refs_3_.refs_22_.refs_2_ = bf16[832,256]{1,0:T(8,128)(2,1)S(1)} collective-permute-done((bf16[832,256]{1,0:T(8,128)(2,1)S(1)}, bf16[832,256]{1,0:T(8,128)(2,1)S(1)}, u32[]{:S(2)}, u32[]{:S(2)}) %collective-permute-start.17) | collective-permute-done | bytes 426016 | tf_op jit(solution)/shard_map/ppermute | solution.py:157
  89.4 1.6 dynamic-slice_bitcast_fusion
  93.0 1.3 collective-permute-start.29
  94.8 12.7 %shard_map.148 = (bf16[1664,896]{1,0:T(8,128)(2,1)S(1)}, bf16[416,448]{1,0:T(8,128)(2,1)S(1)}) custom-call(bf16[416,448]{1,0:T(8,128)(2,1)S(1)} %bitcast.53, bf16[416,448]{1,0:T(8,128)(2,1)} %collective-permute-done.refs_1_, bf16[416,448]{1,0:T(8,128)(2,1)} %collective-permute-done.1.refs_2_, ...), custom_call_target="tpu_custom_call" | custom-call | flops 4961861632 | bytes 12360192 | tf_op jit(solution)/shard_map/pallas_call | solution.py:458
  107.6 4.1 %collective-permute-done.27.refs_1_ = bf16[416,832]{1,0:T(8,128)(2,1)S(1)} collective-permute-done((bf16[416,832]{1,0:T(8,128)(2,1)S(1)}, bf16[416,832]{1,0:T(8,128)(2,1)S(1)}, u32[]{:S(2)}, u32[]{:S(2)}) %collective-permute-start.27) | collective-permute-done | bytes 692256 | tf_op jit(solution)/shard_map/ppermute | solution.py:144
  112.2 4.9 %shard_map.150.hidden = bf16[1024,896]{1,0:T(8,128)(2,1)S(1)} custom-call(bf16[1664,896]{1,0:T(8,128)(2,1)S(1)} %get-tuple-element.45.normed, bf16[832,2048]{1,0:T(8,128)(2,1)S(1)} %copy-done.21, bf16[832,256]{1,0:T(8,128)(2,1)S(1)} %copy-done.30, bf16[832,256]{1,0:T(8,128)(2,1)S(1)} %copy-done.18, bf16[832,256]{1,0:T(8,128)(2,1)S(1)} %copy-done.14, ...), custom_call_target="tpu_custom_call" | custom-call | flops 3053453312 | bytes 8093696 | tf_op jit(solution)/shard_map/pallas_call | solution.py:458
  117.1 3.6 %shard_map.151 = (bf16[2,208,448]{2,1,0:T(8,128)(2,1)S(1)}, bf16[2,208,448]{2,1,0:T(8,128)(2,1)S(1)}, bf16[2,208,448]{2,1,0:T(8,128)(2,1)S(1)}, bf16[2,208,448]{2,1,0:T(8,128)(2,1)S(1)}) custom-call(bf16[1024,896]{1,0:T(8,128)(2,1)S(1)} %shard_map.150.hidden, bf16[832,2048]{1,0:T(8,128)(2,1)S(1)} %bitcast.43, bf16[832,256]{1,0:T(8,128)(2,1)S(1)} %copy-done.5, ...), custom_call_target="tpu_custom_call" | custom-call | flops 1526726656 | bytes 6946816 | tf_op jit(solution)/shard_map/pallas_call | solution.py:458
  121.4 3.6 %shard_map.152 = (bf16[2,208,448]{2,1,0:T(8,128)(2,1)S(1)}, bf16[2,208,448]{2,1,0:T(8,128)(2,1)S(1)}, bf16[2,208,448]{2,1,0:T(8,128)(2,1)S(1)}, bf16[2,208,448]{2,1,0:T(8,128)(2,1)S(1)}) custom-call(bf16[1024,896]{1,0:T(8,128)(2,1)S(1)} %shard_map.150.hidden, bf16[832,2048]{1,0:T(8,128)(2,1)S(1)} %bitcast.44, bf16[832,256]{1,0:T(8,128)(2,1)S(1)} %copy-done.5, ...), custom_call_target="tpu_custom_call" | custom-call | flops 1526726656 | bytes 8437760 | tf_op jit(solution)/shard_map/pallas_call | solution.py:458
  125.0 1.8 %collective-permute-done.29.refs_4_.refs_1_ = bf16[416,832]{1,0:T(8,128)(2,1)S(1)} collective-permute-done((bf16[416,832]{1,0:T(8,128)(2,1)S(1)}, bf16[416,832]{1,0:T(8,128)(2,1)S(1)}, u32[]{:S(2)}, u32[]{:S(2)}) %collective-permute-start.29) | collective-permute-done | bytes 692256 | tf_op jit(solution)/shard_map/ppermute | solution.py:144
  126.8 1.9 %collective-permute-done.30.refs_5_.refs_2_ = bf16[416,832]{1,0:T(8,128)(2,1)S(1)} collective-permute-done((bf16[416,832]{1,0:T(8,128)(2,1)S(1)}, bf16[416,832]{1,0:T(8,128)(2,1)S(1)}, u32[]{:S(2)}, u32[]{:S(2)}) %collective-permute-start.30) | collective-permute-done | bytes 692256 | tf_op jit(solution)/shard_map/ppermute | solution.py:157
  131.0 8.3 %collective-permute-done.33 = bf16[2,208,448]{2,1,0:T(8,128)(2,1)S(1)} collective-permute-done((bf16[2,208,448]{2,1,0:T(8,128)(2,1)S(1)}, bf16[2,208,448]{2,1,0:T(8,128)(2,1)S(1)}, u32[]{:S(2)}, u32[]{:S(2)}) %collective-permute-start.33) | collective-permute-done | bytes 372768 | tf_op jit(solution)/shard_map/ppermute | solution.py:144
  140.7 1.6 collective-permute-start.38
  142.2 3.8 %collective-permute-done.37.last_x = bf16[208,448]{1,0:T(8,128)(2,1)S(1)} collective-permute-done((bf16[208,448]{1,0:T(8,128)(2,1)S(1)}, bf16[208,448]{1,0:T(8,128)(2,1)S(1)}, u32[]{:S(2)}, u32[]{:S(2)}) %collective-permute-start.37) | collective-permute-done | bytes 186400 | tf_op jit(solution)/shard_map/ppermute | solution.py:148
  146.6 1.0 shard_map.154
  147.6 1.3 shard_map.155
  149.0 1.5 collective-permute-done.40
  150.5 1.6 collective-permute-start.41
  152.1 3.5 %collective-permute-done.41 = bf16[416,112]{1,0:T(8,128)(2,1)S(1)} collective-permute-done((bf16[416,112]{1,0:T(8,128)(2,1)S(1)}, bf16[416,112]{1,0:T(8,128)(2,1)S(1)}, u32[]{:S(2)}, u32[]{:S(2)}) %collective-permute-start.41) | collective-permute-done | bytes 93216 | tf_op jit(solution)/shard_map/ppermute | solution.py:148
  155.7 0.9 collective-permute-start.42
  156.6 2.6 %collective-permute-start.43 = (bf16[416,112]{1,0:T(8,128)(2,1)S(1)}, bf16[416,112]{1,0:T(8,128)(2,1)S(1)}, u32[]{:S(2)}, u32[]{:S(2)}) collective-permute-start(bf16[416,112]{1,0:T(8,128)(2,1)S(1)} %fusion.refs_0_), channel_id=1, source_target_pairs={{0,2},{1,3},{2,0},{3,1},{4,6},{5,7},{6,4},{7,5},{8,10},{9,11},{10,... | collective-permute-start | bytes 279560 | tf_op jit(solution)/shard_map/ppermute | solution.py:157
  159.2 0.9 collective-permute-start.44
  160.1 1.3 collective-permute-done.42.refs_1_
  161.4 6.2 %collective-permute-done.43.refs_2_ = bf16[416,112]{1,0:T(8,128)(2,1)S(1)} collective-permute-done((bf16[416,112]{1,0:T(8,128)(2,1)S(1)}, bf16[416,112]{1,0:T(8,128)(2,1)S(1)}, u32[]{:S(2)}, u32[]{:S(2)}) %collective-permute-start.43) | collective-permute-done | bytes 93216 | tf_op jit(solution)/shard_map/ppermute | solution.py:157
  167.6 0.9 shard_map.156
  (147 shorter events, 13.6 us)
Async XLA Ops:
  0.6 14.0 %collective-permute-start.1 = (bf16[416,448]{1,0:T(8,128)(2,1)}, bf16[416,448]{1,0:T(8,128)(2,1)}, u32[]{:S(2)}, u32[]{:S(2)}) collective-permute-start(bf16[416,448]{1,0:T(8,128)(2,1)} %bitcast.49), channel_id=1, source_target_pairs={{0,16},{16,0},{1,17},{17,1},{2,18},{18,2},{3,19},{19,3},{4,20},{20... | collective-permute-start | bytes 1118216 | tf_op jit(solution)/shard_map/ppermute | solution.py:144
  4.8 16.8 %collective-permute-start.7 = (bf16[208,832]{1,0:T(8,128)(2,1)S(1)}, bf16[208,832]{1,0:T(8,128)(2,1)S(1)}, u32[]{:S(2)}, u32[]{:S(2)}) collective-permute-start(bf16[208,832]{1,0:T(8,128)(2,1)S(1)} %select_bitcast_fusion), channel_id=1, source_target_pairs={{0,16},{16,0},{1,17},{17,1},{2,18},{18,2},{3,19},{19,3},{4,20},{20... | collective-permute-start | bytes 1038344 | tf_op jit(solution)/shard_map/ppermute | solution.py:144
  14.6 13.7 %collective-permute-start.2 = (bf16[416,448]{1,0:T(8,128)(2,1)}, bf16[416,448]{1,0:T(8,128)(2,1)}, u32[]{:S(2)}, u32[]{:S(2)}) collective-permute-start(bf16[416,448]{1,0:T(8,128)(2,1)} %collective-permute-done.1.refs_2_), channel_id=1, source_target_pairs={{0,8},{4,12},{8,0},{12,4},{1,9},{5,13},{9,1},{13,5},{2,10},{6,14},... | collective-permute-start | bytes 1118216 | tf_op jit(solution)/shard_map/ppermute | solution.py:148
  16.7 20.2 %collective-permute-start = (bf16[416,448]{1,0:T(8,128)(2,1)}, bf16[416,448]{1,0:T(8,128)(2,1)}, u32[]{:S(2)}, u32[]{:S(2)}) collective-permute-start(bf16[416,448]{1,0:T(8,128)(2,1)} %bitcast.50), channel_id=1, source_target_pairs={{0,8},{4,12},{8,0},{12,4},{1,9},{5,13},{9,1},{13,5},{2,10},{6,14},... | collective-permute-start | bytes 1118216 | tf_op jit(solution)/shard_map/ppermute | solution.py:148
  16.7 22.1 %collective-permute-start.3 = (bf16[416,448]{1,0:T(8,128)(2,1)}, bf16[416,448]{1,0:T(8,128)(2,1)}, u32[]{:S(2)}, u32[]{:S(2)}) collective-permute-start(bf16[416,448]{1,0:T(8,128)(2,1)} %bitcast.51), channel_id=1, source_target_pairs={{0,4},{4,0},{8,12},{12,8},{1,5},{5,1},{9,13},{13,9},{2,6},{6,2},{1... | collective-permute-start | bytes 1118216 | tf_op jit(solution)/shard_map/ppermute | solution.py:152
  22.4 16.4 %collective-permute-start.9 = (bf16[208,832]{1,0:T(8,128)(2,1)}, bf16[208,832]{1,0:T(8,128)(2,1)}, u32[]{:S(2)}, u32[]{:S(2)}) collective-permute-start(bf16[208,832]{1,0:T(8,128)(2,1)} %shard_map.140), channel_id=1, source_target_pairs={{0,16},{16,0},{1,17},{17,1},{2,18},{18,2},{3,19},{19,3},{4,20},{20... | collective-permute-start | bytes 1038344 | tf_op jit(solution)/shard_map/ppermute | solution.py:144
  26.7 12.7 %collective-permute-start.8 = (bf16[208,832]{1,0:T(8,128)(2,1)}, bf16[208,832]{1,0:T(8,128)(2,1)S(1)}, u32[]{:S(2)}, u32[]{:S(2)}) collective-permute-start(bf16[208,832]{1,0:T(8,128)(2,1)} %copy-done.6), channel_id=1, source_target_pairs={{0,1},{1,0},{2,3},{3,2},{4,5},{5,4},{6,7},{7,6},{8,9},{9,8},{10,11... | collective-permute-start | bytes 1038344 | tf_op jit(solution)/shard_map/ppermute | solution.py:157
  28.3 47.9 %collective-permute-start.18 = (bf16[416,1664]{1,0:T(8,128)(2,1)}, bf16[416,1664]{1,0:T(8,128)(2,1)}, u32[]{:S(2)}, u32[]{:S(2)}) collective-permute-start(bf16[416,1664]{1,0:T(8,128)(2,1)} %shard_map.143.refs_9_), channel_id=1, source_target_pairs={{0,8},{4,12},{8,0},{12,4},{1,9},{5,13},{9,1},{13,5},{2,10},{6,14},... | collective-permute-start | bytes 4153352 | tf_op jit(solution)/shard_map/ppermute | solution.py:148
  36.9 10.1 %collective-permute-start.10 = (bf16[832,256]{1,0:T(8,128)(2,1)S(1)}, bf16[832,256]{1,0:T(8,128)(2,1)S(1)}, u32[]{:S(2)}, u32[]{:S(2)}) collective-permute-start(bf16[832,256]{1,0:T(8,128)(2,1)S(1)} %shard_map.141), channel_id=1, source_target_pairs={{0,16},{16,0},{1,17},{17,1},{2,18},{18,2},{3,19},{19,3},{4,20},{20... | collective-permute-start | bytes 1277960 | tf_op jit(solution)/shard_map/ppermute | solution.py:144
  38.9 2.0 %collective-permute-start.5 = (bf16[416,448]{1,0:T(8,128)(2,1)}, bf16[416,448]{1,0:T(8,128)(2,1)S(1)}, u32[]{:S(2)}, u32[]{:S(2)}) collective-permute-start(bf16[416,448]{1,0:T(8,128)(2,1)} %collective-permute-done.1.refs_2_), channel_id=1, source_target_pairs={{0,4},{4,0},{8,12},{12,8},{1,5},{5,1},{9,13},{13,9},{2,6},{6,2},{1... | collective-permute-start | bytes 1118216 | tf_op jit(solution)/shard_map/ppermute | solution.py:152
  38.9 2.6 %collective-permute-start.4 = (bf16[416,448]{1,0:T(8,128)(2,1)}, bf16[416,448]{1,0:T(8,128)(2,1)S(1)}, u32[]{:S(2)}, u32[]{:S(2)}) collective-permute-start(bf16[416,448]{1,0:T(8,128)(2,1)} %collective-permute-done.refs_1_), channel_id=1, source_target_pairs={{0,4},{4,0},{8,12},{12,8},{1,5},{5,1},{9,13},{13,9},{2,6},{6,2},{1... | collective-permute-start | bytes 1118216 | tf_op jit(solution)/shard_map/ppermute | solution.py:152
  39.4 8.9 %collective-permute-start.6 = (bf16[416,448]{1,0:T(8,128)(2,1)}, bf16[416,448]{1,0:T(8,128)(2,1)S(1)}, u32[]{:S(2)}, u32[]{:S(2)}) collective-permute-start(bf16[416,448]{1,0:T(8,128)(2,1)} %collective-permute-done.2.refs_3_.refs_1_.refs_5_), channel_id=1, source_target_pairs={{0,4},{4,0},{8,12},{12,8},{1,5},{5,1},{9,13},{13,9},{2,6},{6,2},{1... | collective-permute-start | bytes 1118216 | tf_op jit(solution)/shard_map/ppermute | solution.py:152
  41.4 21.6 %collective-permute-start.11 = (bf16[832,256]{1,0:T(8,128)(2,1)S(1)}, bf16[832,256]{1,0:T(8,128)(2,1)S(1)}, u32[]{:S(2)}, u32[]{:S(2)}) collective-permute-start(bf16[832,256]{1,0:T(8,128)(2,1)S(1)} %get-tuple-element.33), channel_id=1, source_target_pairs={{0,16},{16,0},{1,17},{17,1},{2,18},{18,2},{3,19},{19,3},{4,20},{20... | collective-permute-start | bytes 1277960 | tf_op jit(solution)/shard_map/ppermute | solution.py:144
  41.5 21.8 %collective-permute-start.12 = (bf16[832,256]{1,0:T(8,128)(2,1)S(1)}, bf16[832,256]{1,0:T(8,128)(2,1)S(1)}, u32[]{:S(2)}, u32[]{:S(2)}) collective-permute-start(bf16[832,256]{1,0:T(8,128)(2,1)S(1)} %get-tuple-element.34), channel_id=1, source_target_pairs={{0,16},{16,0},{1,17},{17,1},{2,18},{18,2},{3,19},{19,3},{4,20},{20... | collective-permute-start | bytes 1277960 | tf_op jit(solution)/shard_map/ppermute | solution.py:144
  46.9 16.3 %collective-permute-start.13 = (bf16[832,256]{1,0:T(8,128)(2,1)S(1)}, bf16[832,256]{1,0:T(8,128)(2,1)S(1)}, u32[]{:S(2)}, u32[]{:S(2)}) collective-permute-start(bf16[832,256]{1,0:T(8,128)(2,1)S(1)} %collective-permute-done.10.refs_16_.refs_0_), channel_id=1, source_target_pairs={{0,1},{1,0},{2,3},{3,2},{4,5},{5,4},{6,7},{7,6},{8,9},{9,8},{10,11... | collective-permute-start | bytes 1277960 | tf_op jit(solution)/shard_map/ppermute | solution.py:157
  63.2 25.3 %copy-start.13 = (bf16[832,256]{1,0:T(8,128)(2,1)}, bf16[832,256]{1,0:T(8,128)(2,1)S(1)}, u32[]{:S(2)}) copy-start(bf16[832,256]{1,0:T(8,128)(2,1)S(1)} %collective-permute-done.13.refs_3_.refs_2_) | copy-start | bytes 1277956
  63.2 25.3 %copy-start.4 = (bf16[832,256]{1,0:T(8,128)(2,1)}, bf16[832,256]{1,0:T(8,128)(2,1)S(1)}, u32[]{:S(2)}) copy-start(bf16[832,256]{1,0:T(8,128)(2,1)S(1)} %get-tuple-element.36.refs_0_) | copy-start | bytes 1277956
  63.3 25.3 %copy-start.17 = (bf16[832,256]{1,0:T(8,128)(2,1)}, bf16[832,256]{1,0:T(8,128)(2,1)S(1)}, u32[]{:S(2)}) copy-start(bf16[832,256]{1,0:T(8,128)(2,1)S(1)} %get-tuple-element.38.refs_1_) | copy-start | bytes 1277956
  63.3 13.0 %collective-permute-start.19 = (bf16[832,256]{1,0:T(8,128)(2,1)S(1)}, bf16[832,256]{1,0:T(8,128)(2,1)S(1)}, u32[]{:S(2)}, u32[]{:S(2)}) collective-permute-start(bf16[832,256]{1,0:T(8,128)(2,1)S(1)} %get-tuple-element.38.refs_1_), channel_id=1, source_target_pairs={{0,1},{1,0},{2,3},{3,2},{4,5},{5,4},{6,7},{7,6},{8,9},{9,8},{10,11... | collective-permute-start | bytes 1277960 | tf_op jit(solution)/shard_map/ppermute | solution.py:157
  65.4 9.5 %collective-permute-start.14 = (bf16[208,896]{1,0:T(8,128)(2,1)}, bf16[208,896]{1,0:T(8,128)(2,1)S(1)}, u32[]{:S(2)}, u32[]{:S(2)}) collective-permute-start(bf16[208,896]{1,0:T(8,128)(2,1)} %get-tuple-element.35.refs_8_), channel_id=1, source_target_pairs={{0,8},{4,12},{8,0},{12,4},{1,9},{5,13},{9,1},{13,5},{2,10},{6,14},... | collective-permute-start | bytes 1118216 | tf_op jit(solution)/shard_map/ppermute | solution.py:148
  66.9 9.3 %collective-permute-start.15 = (bf16[208,896]{1,0:T(8,128)(2,1)}, bf16[208,896]{1,0:T(8,128)(2,1)}, u32[]{:S(2)}, u32[]{:S(2)}) collective-permute-start(bf16[208,896]{1,0:T(8,128)(2,1)} %get-tuple-element.35.refs_8_), channel_id=1, source_target_pairs={{0,16},{16,0},{1,17},{17,1},{2,18},{18,2},{3,19},{19,3},{4,20},{20... | collective-permute-start | bytes 1118216 | tf_op jit(solution)/shard_map/ppermute | solution.py:144
  68.4 23.3 %collective-permute-start.25 = (bf16[416,1664]{1,0:T(8,128)(2,1)}, bf16[416,1664]{1,0:T(8,128)(2,1)}, u32[]{:S(2)}, u32[]{:S(2)}) collective-permute-start(bf16[416,1664]{1,0:T(8,128)(2,1)} %refs_16_.1), channel_id=1, source_target_pairs={{0,4},{4,0},{8,12},{12,8},{1,5},{5,1},{9,13},{13,9},{2,6},{6,2},{1... | collective-permute-start | bytes 4153352 | tf_op jit(solution)/shard_map/ppermute | solution.py:152
  76.3 18.5 %collective-permute-start.26 = (bf16[416,1664]{1,0:T(8,128)(2,1)}, bf16[416,1664]{1,0:T(8,128)(2,1)}, u32[]{:S(2)}, u32[]{:S(2)}) collective-permute-start(bf16[416,1664]{1,0:T(8,128)(2,1)} %get-tuple-element.41.refs_17_), channel_id=1, source_target_pairs={{0,4},{4,0},{8,12},{12,8},{1,5},{5,1},{9,13},{13,9},{2,6},{6,2},{1... | collective-permute-start | bytes 4153352 | tf_op jit(solution)/shard_map/ppermute | solution.py:152
  76.4 12.2 %collective-permute-start.17 = (bf16[832,256]{1,0:T(8,128)(2,1)S(1)}, bf16[832,256]{1,0:T(8,128)(2,1)S(1)}, u32[]{:S(2)}, u32[]{:S(2)}) collective-permute-start(bf16[832,256]{1,0:T(8,128)(2,1)S(1)} %get-tuple-element.36.refs_0_), channel_id=1, source_target_pairs={{0,1},{1,0},{2,3},{3,2},{4,5},{5,4},{6,7},{7,6},{8,9},{9,8},{10,11... | collective-permute-start | bytes 1277960 | tf_op jit(solution)/shard_map/ppermute | solution.py:157
  76.9 14.8 %collective-permute-start.20 = (bf16[832,256]{1,0:T(8,128)(2,1)}, bf16[832,256]{1,0:T(8,128)(2,1)}, u32[]{:S(2)}, u32[]{:S(2)}) collective-permute-start(bf16[832,256]{1,0:T(8,128)(2,1)} %get-tuple-element.39), channel_id=1, source_target_pairs={{0,16},{16,0},{1,17},{17,1},{2,18},{18,2},{3,19},{19,3},{4,20},{20... | collective-permute-start | bytes 1277960 | tf_op jit(solution)/shard_map/ppermute | solution.py:144
  77.4 13.6 %collective-permute-start.16 = (bf16[208,896]{1,0:T(8,128)(2,1)}, bf16[208,896]{1,0:T(8,128)(2,1)}, u32[]{:S(2)}, u32[]{:S(2)}) collective-permute-start(bf16[208,896]{1,0:T(8,128)(2,1)} %collective-permute-done.15.refs_2_.refs_10_), channel_id=1, source_target_pairs={{0,8},{4,12},{8,0},{12,4},{1,9},{5,13},{9,1},{13,5},{2,10},{6,14},... | collective-permute-start | bytes 1118216 | tf_op jit(solution)/shard_map/ppermute | solution.py:148
  89.4 2.8 %collective-permute-start.21 = (bf16[208,896]{1,0:T(8,128)(2,1)}, bf16[208,896]{1,0:T(8,128)(2,1)}, u32[]{:S(2)}, u32[]{:S(2)}) collective-permute-start(bf16[208,896]{1,0:T(8,128)(2,1)} %get-tuple-element.35.refs_8_), channel_id=1, source_target_pairs={{0,4},{4,0},{8,12},{12,8},{1,5},{5,1},{9,13},{13,9},{2,6},{6,2},{1... | collective-permute-start | bytes 1118216 | tf_op jit(solution)/shard_map/ppermute | solution.py:152
  91.1 1.9 %collective-permute-start.22 = (bf16[208,896]{1,0:T(8,128)(2,1)S(1)}, bf16[208,896]{1,0:T(8,128)(2,1)S(1)}, u32[]{:S(2)}, u32[]{:S(2)}) collective-permute-start(bf16[208,896]{1,0:T(8,128)(2,1)S(1)} %copy-done.20), channel_id=1, source_target_pairs={{0,4},{4,0},{8,12},{12,8},{1,5},{5,1},{9,13},{13,9},{2,6},{6,2},{1... | collective-permute-start | bytes 1118216 | tf_op jit(solution)/shard_map/ppermute | solution.py:152
  91.6 2.6 %collective-permute-start.23 = (bf16[208,896]{1,0:T(8,128)(2,1)}, bf16[208,896]{1,0:T(8,128)(2,1)S(1)}, u32[]{:S(2)}, u32[]{:S(2)}) collective-permute-start(bf16[208,896]{1,0:T(8,128)(2,1)} %collective-permute-done.15.refs_2_.refs_10_), channel_id=1, source_target_pairs={{0,4},{4,0},{8,12},{12,8},{1,5},{5,1},{9,13},{13,9},{2,6},{6,2},{1... | collective-permute-start | bytes 1118216 | tf_op jit(solution)/shard_map/ppermute | solution.py:152
  91.7 3.0 %collective-permute-start.24 = (bf16[208,896]{1,0:T(8,128)(2,1)}, bf16[208,896]{1,0:T(8,128)(2,1)S(1)}, u32[]{:S(2)}, u32[]{:S(2)}) collective-permute-start(bf16[208,896]{1,0:T(8,128)(2,1)} %get-tuple-element.40.refs_11_), channel_id=1, source_target_pairs={{0,4},{4,0},{8,12},{12,8},{1,5},{5,1},{9,13},{13,9},{2,6},{6,2},{1... | collective-permute-start | bytes 1118216 | tf_op jit(solution)/shard_map/ppermute | solution.py:152
  92.2 19.5 %collective-permute-start.27 = (bf16[416,832]{1,0:T(8,128)(2,1)S(1)}, bf16[416,832]{1,0:T(8,128)(2,1)S(1)}, u32[]{:S(2)}, u32[]{:S(2)}) collective-permute-start(bf16[416,832]{1,0:T(8,128)(2,1)S(1)} %get-tuple-element.44), channel_id=1, source_target_pairs={{0,16},{16,0},{1,17},{17,1},{2,18},{18,2},{3,19},{19,3},{4,20},{20... | collective-permute-start | bytes 2076680 | tf_op jit(solution)/shard_map/ppermute | solution.py:144
  93.0 33.9 %collective-permute-start.29 = (bf16[416,832]{1,0:T(8,128)(2,1)S(1)}, bf16[416,832]{1,0:T(8,128)(2,1)S(1)}, u32[]{:S(2)}, u32[]{:S(2)}) collective-permute-start(bf16[416,832]{1,0:T(8,128)(2,1)S(1)} %get-tuple-element.54), channel_id=1, source_target_pairs={{0,16},{16,0},{1,17},{17,1},{2,18},{18,2},{3,19},{19,3},{4,20},{20... | collective-permute-start | bytes 2076680 | tf_op jit(solution)/shard_map/ppermute | solution.py:144
  94.3 22.8 %collective-permute-start.28 = (bf16[832,256]{1,0:T(8,128)(2,1)}, bf16[832,256]{1,0:T(8,128)(2,1)S(1)}, u32[]{:S(2)}, u32[]{:S(2)}) collective-permute-start(bf16[832,256]{1,0:T(8,128)(2,1)} %collective-permute-done.20.refs_4_.refs_21_.refs_1_), channel_id=1, source_target_pairs={{0,1},{1,0},{2,3},{3,2},{4,5},{5,4},{6,7},{7,6},{8,9},{9,8},{10,11... | collective-permute-start | bytes 1277960 | tf_op jit(solution)/shard_map/ppermute | solution.py:157
  111.7 17.0 %collective-permute-start.30 = (bf16[416,832]{1,0:T(8,128)(2,1)S(1)}, bf16[416,832]{1,0:T(8,128)(2,1)S(1)}, u32[]{:S(2)}, u32[]{:S(2)}) collective-permute-start(bf16[416,832]{1,0:T(8,128)(2,1)S(1)} %get-tuple-element.55.refs_0_), channel_id=1, source_target_pairs={{0,1},{1,0},{2,3},{3,2},{4,5},{5,4},{6,7},{7,6},{8,9},{9,8},{10,11... | collective-permute-start | bytes 2076680 | tf_op jit(solution)/shard_map/ppermute | solution.py:157
  120.7 8.0 %collective-permute-start.32 = (bf16[2,208,448]{2,1,0:T(8,128)(2,1)S(1)}, bf16[2,208,448]{2,1,0:T(8,128)(2,1)S(1)}, u32[]{:S(2)}, u32[]{:S(2)}) collective-permute-start(bf16[2,208,448]{2,1,0:T(8,128)(2,1)S(1)} %get-tuple-element.46.refs_4_), channel_id=1, source_target_pairs={{0,4},{4,0},{8,12},{12,8},{1,5},{5,1},{9,13},{13,9},{2,6},{6,2},{1... | collective-permute-start | bytes 1118216 | tf_op jit(solution)/shard_map/ppermute | solution.py:152
  120.8 8.6 %collective-permute-start.35 = (bf16[2,208,448]{2,1,0:T(8,128)(2,1)S(1)}, bf16[2,208,448]{2,1,0:T(8,128)(2,1)S(1)}, u32[]{:S(2)}, u32[]{:S(2)}) collective-permute-start(bf16[2,208,448]{2,1,0:T(8,128)(2,1)S(1)} %get-tuple-element.47.refs_5_), channel_id=1, source_target_pairs={{0,4},{4,0},{8,12},{12,8},{1,5},{5,1},{9,13},{13,9},{2,6},{6,2},{1... | collective-permute-start | bytes 1118216 | tf_op jit(solution)/shard_map/ppermute | solution.py:152
  121.3 9.7 %collective-permute-start.31 = (bf16[2,208,448]{2,1,0:T(8,128)(2,1)S(1)}, bf16[2,208,448]{2,1,0:T(8,128)(2,1)S(1)}, u32[]{:S(2)}, u32[]{:S(2)}) collective-permute-start(bf16[2,208,448]{2,1,0:T(8,128)(2,1)S(1)} %get-tuple-element.48.refs_6_), channel_id=1, source_target_pairs={{0,4},{4,0},{8,12},{12,8},{1,5},{5,1},{9,13},{13,9},{2,6},{6,2},{1... | collective-permute-start | bytes 1118216 | tf_op jit(solution)/shard_map/ppermute | solution.py:152
  126.8 4.1 %collective-permute-start.34 = (bf16[2,208,448]{2,1,0:T(8,128)(2,1)S(1)}, bf16[2,208,448]{2,1,0:T(8,128)(2,1)S(1)}, u32[]{:S(2)}, u32[]{:S(2)}) collective-permute-start(bf16[2,208,448]{2,1,0:T(8,128)(2,1)S(1)} %get-tuple-element.49.refs_7_), channel_id=1, source_target_pairs={{0,4},{4,0},{8,12},{12,8},{1,5},{5,1},{9,13},{13,9},{2,6},{6,2},{1... | collective-permute-start | bytes 1118216 | tf_op jit(solution)/shard_map/ppermute | solution.py:152
  128.8 10.4 %collective-permute-start.33 = (bf16[2,208,448]{2,1,0:T(8,128)(2,1)S(1)}, bf16[2,208,448]{2,1,0:T(8,128)(2,1)S(1)}, u32[]{:S(2)}, u32[]{:S(2)}) collective-permute-start(bf16[2,208,448]{2,1,0:T(8,128)(2,1)S(1)} %add_convert_fusion.3), channel_id=1, source_target_pairs={{0,16},{16,0},{1,17},{17,1},{2,18},{18,2},{3,19},{19,3},{4,20},{20... | collective-permute-start | bytes 1118216 | tf_op jit(solution)/shard_map/ppermute | solution.py:144
  129.5 10.1 %collective-permute-start.36 = (bf16[2,208,448]{2,1,0:T(8,128)(2,1)S(1)}, bf16[2,208,448]{2,1,0:T(8,128)(2,1)S(1)}, u32[]{:S(2)}, u32[]{:S(2)}) collective-permute-start(bf16[2,208,448]{2,1,0:T(8,128)(2,1)S(1)} %add_convert_fusion.1), channel_id=1, source_target_pairs={{0,8},{4,12},{8,0},{12,4},{1,9},{5,13},{9,1},{13,5},{2,10},{6,14},... | collective-permute-start | bytes 1118216 | tf_op jit(solution)/shard_map/ppermute | solution.py:148
  130.1 17.5 %collective-permute-start.39 = (bf16[416,832]{1,0:T(8,128)(2,1)S(1)}, bf16[416,832]{1,0:T(8,128)(2,1)S(1)}, u32[]{:S(2)}, u32[]{:S(2)}) collective-permute-start(bf16[416,832]{1,0:T(8,128)(2,1)S(1)} %collective-permute-done.29.refs_4_.refs_1_), channel_id=1, source_target_pairs={{0,1},{1,0},{2,3},{3,2},{4,5},{5,4},{6,7},{7,6},{8,9},{9,8},{10,11... | collective-permute-start | bytes 2076680 | tf_op jit(solution)/shard_map/ppermute | solution.py:157
  140.1 5.9 %collective-permute-start.37 = (bf16[208,448]{1,0:T(8,128)(2,1)S(1)}, bf16[208,448]{1,0:T(8,128)(2,1)S(1)}, u32[]{:S(2)}, u32[]{:S(2)}) collective-permute-start(bf16[208,448]{1,0:T(8,128)(2,1)S(1)} %get-tuple-element.72), channel_id=1, source_target_pairs={{0,8},{4,12},{8,0},{12,4},{1,9},{5,13},{9,1},{13,5},{2,10},{6,14},... | collective-permute-start | bytes 559112 | tf_op jit(solution)/shard_map/ppermute | solution.py:148
  140.7 5.9 %collective-permute-start.38 = (bf16[208,448]{1,0:T(8,128)(2,1)S(1)}, bf16[208,448]{1,0:T(8,128)(2,1)S(1)}, u32[]{:S(2)}, u32[]{:S(2)}) collective-permute-start(bf16[208,448]{1,0:T(8,128)(2,1)S(1)} %get-tuple-element.70), channel_id=1, source_target_pairs={{0,16},{16,0},{1,17},{17,1},{2,18},{18,2},{3,19},{19,3},{4,20},{20... | collective-permute-start | bytes 559112 | tf_op jit(solution)/shard_map/ppermute | solution.py:144
  148.9 1.5 collective-permute-start.40
  150.5 5.1 %collective-permute-start.41 = (bf16[416,112]{1,0:T(8,128)(2,1)S(1)}, bf16[416,112]{1,0:T(8,128)(2,1)S(1)}, u32[]{:S(2)}, u32[]{:S(2)}) collective-permute-start(bf16[416,112]{1,0:T(8,128)(2,1)S(1)} %slice_bitcast_fusion.4), channel_id=1, source_target_pairs={{0,8},{4,12},{8,0},{12,4},{1,9},{5,13},{9,1},{13,5},{2,10},{6,14},... | collective-permute-start | bytes 279560 | tf_op jit(solution)/shard_map/ppermute | solution.py:148
  155.7 5.7 %collective-permute-start.42 = (bf16[416,112]{1,0:T(8,128)(2,1)S(1)}, bf16[416,112]{1,0:T(8,128)(2,1)S(1)}, u32[]{:S(2)}, u32[]{:S(2)}) collective-permute-start(bf16[416,112]{1,0:T(8,128)(2,1)S(1)} %fusion.refs_0_), channel_id=1, source_target_pairs={{0,1},{1,0},{2,3},{3,2},{4,5},{5,4},{6,7},{7,6},{8,9},{9,8},{10,11... | collective-permute-start | bytes 279560 | tf_op jit(solution)/shard_map/ppermute | solution.py:157
  156.6 11.1 %collective-permute-start.43 = (bf16[416,112]{1,0:T(8,128)(2,1)S(1)}, bf16[416,112]{1,0:T(8,128)(2,1)S(1)}, u32[]{:S(2)}, u32[]{:S(2)}) collective-permute-start(bf16[416,112]{1,0:T(8,128)(2,1)S(1)} %fusion.refs_0_), channel_id=1, source_target_pairs={{0,2},{1,3},{2,0},{3,1},{4,6},{5,7},{6,4},{7,5},{8,10},{9,11},{10,... | collective-permute-start | bytes 279560 | tf_op jit(solution)/shard_map/ppermute | solution.py:157
  159.2 8.5 %collective-permute-start.44 = (bf16[416,112]{1,0:T(8,128)(2,1)S(1)}, bf16[416,112]{1,0:T(8,128)(2,1)S(1)}, u32[]{:S(2)}, u32[]{:S(2)}) collective-permute-start(bf16[416,112]{1,0:T(8,128)(2,1)S(1)} %fusion.refs_0_), channel_id=1, source_target_pairs={{0,3},{1,2},{2,1},{3,0},{4,7},{5,6},{6,5},{7,4},{8,11},{9,10},{10,... | collective-permute-start | bytes 279560 | tf_op jit(solution)/shard_map/ppermute | solution.py:157
  (33 other events, 299.9 us)

commit v3 on v2

--- a/solution.py
+++ b/solution.py
@@ -522,7 +522,7 @@
 
     over_x, over_y = swap_x(tok), swap_y(tok)
     qkv_got = swap_x(first)
-    (key_piece,) = after((qkv_got,), (rows_of(w_key.T, their_row, cols),))
+    (key_piece,) = after((qkv_got, over_y), (rows_of(w_key.T, their_row, cols),))
     qkv_got_key = swap_x(key_piece)
     held = [tok, over_y, over_x, swap_y(over_x)]
     tok_shards = held + [swap_core(part) for part in held]

time: 169 us -> 168 us (level)
  local copies, waits for them, and re-layouts: 10.7 us -> 8 us
  starting transfers between devices: 38 us -> 40.2 us
    ppermute x12, waiting for transfers between devices: 32.6 us -> 38.7 us  [swap_x(): return lax.ppermute(arr, 'gx', [(0, 1), (1, 0)])]
    ppermute x8, waiting for transfers between devices: 19 us -> 14.7 us  [swap_y(): return lax.ppermute(arr, 'gy', [(i, i ^ 2) for i in range(4)])]
    dynamic_slice x1, local copies, waits for them, and re-layouts: 1.76 us -> 0.03 us  [rows_of(): return lax.dynamic_slice_in_dim(arr, begin, count, 0)]
    unnamed x73 -> x77, local copies, waits for them, and re-layouts: 5.21 us -> 4.2 us
  transfers between devices with their start and end apart: 45 -> 45, of which waited for: 22 -> 19; matrix products, arithmetic and copies ran while one was open for 6% -> 5% of each run, Pallas kernels for 24% -> 24%
where the time goes in v3:
time: 168 us; the launch traced here: 167 us
  waiting for transfers between devices  73.2 us (44%)
  Pallas kernels  43 us (26%)
  starting transfers between devices  40.2 us (24%)
  local copies, waits for them, and re-layouts  8 us (5%)
  other arithmetic  1.84 us (1%)
    pallas_call x17, Pallas kernels, call(): pl.pallas_call(kernel, out_shape=outs, in_specs=[pl.BlockSpec(memory_spac...  43 us
    ppermute x12, waiting for transfers between devices, swap_x(): return lax.ppermute(arr, 'gx', [(0, 1), (1, 0)])  38.7 us
    ppermute x10, waiting for transfers between devices, swap_row(): return lax.ppermute(arr, 'row', [(i, i ^ step) for i in range(count)])  18.4 us
    ppermute x12, starting transfers between devices, swap_x(): return lax.ppermute(arr, 'gx', [(0, 1), (1, 0)])  14.8 us
    ppermute x8, waiting for transfers between devices, swap_y(): return lax.ppermute(arr, 'gy', [(i, i ^ 2) for i in range(4)])  14.7 us
    ppermute x10, starting transfers between devices, swap_row(): return lax.ppermute(arr, 'row', [(i, i ^ step) for i in range(count)])  12.5 us
    ppermute x8, starting transfers between devices, swap_y(): return lax.ppermute(arr, 'gy', [(i, i ^ 2) for i in range(4)])  10.5 us
    unnamed x77, local copies, waits for them, and re-layouts  4.2 us
  transfers between devices with their start and end apart: 45, of which 19 were waited for; matrix products, arithmetic and copies ran while one was open for 5% of the time, Pallas kernels for 24%

profile of v3, /device:TPU:0, one launch (start us, length us, event | category | flops | bytes accessed | tf_op | source)
XLA Modules:
  0.0 167.4 jit_solution(5699961932406902406)
XLA Ops:
  0.6 3.0 %collective-permute-start.1 = (bf16[416,448]{1,0:T(8,128)(2,1)}, bf16[416,448]{1,0:T(8,128)(2,1)}, u32[]{:S(2)}, u32[]{:S(2)}) collective-permute-start(bf16[416,448]{1,0:T(8,128)(2,1)} %bitcast.49), channel_id=1, source_target_pairs={{0,16},{16,0},{1,17},{17,1},{2,18},{18,2},{3,19},{19,3},{4,20},{20... | collective-permute-start | bytes 1118216 | tf_op jit(solution)/shard_map/ppermute | solution.py:144
  3.6 1.2 select_bitcast_fusion
  5.0 2.0 %collective-permute-start = (bf16[416,448]{1,0:T(8,128)(2,1)}, bf16[416,448]{1,0:T(8,128)(2,1)S(1)}, u32[]{:S(2)}, u32[]{:S(2)}) collective-permute-start(bf16[416,448]{1,0:T(8,128)(2,1)} %bitcast.50), channel_id=1, source_target_pairs={{0,8},{4,12},{8,0},{12,4},{1,9},{5,13},{9,1},{13,5},{2,10},{6,14},... | collective-permute-start | bytes 1118216 | tf_op jit(solution)/shard_map/ppermute | solution.py:148
  7.0 7.6 %collective-permute-done.1.refs_2_ = bf16[416,448]{1,0:T(8,128)(2,1)} collective-permute-done((bf16[416,448]{1,0:T(8,128)(2,1)}, bf16[416,448]{1,0:T(8,128)(2,1)}, u32[]{:S(2)}, u32[]{:S(2)}) %collective-permute-start.1) | collective-permute-done | bytes 372768 | tf_op jit(solution)/shard_map/ppermute | solution.py:144
  14.6 2.1 %collective-permute-start.2 = (bf16[416,448]{1,0:T(8,128)(2,1)}, bf16[416,448]{1,0:T(8,128)(2,1)}, u32[]{:S(2)}, u32[]{:S(2)}) collective-permute-start(bf16[416,448]{1,0:T(8,128)(2,1)} %collective-permute-done.1.refs_2_), channel_id=1, source_target_pairs={{0,8},{4,12},{8,0},{12,4},{1,9},{5,13},{9,1},{13,5},{2,10},{6,14},... | collective-permute-start | bytes 1118216 | tf_op jit(solution)/shard_map/ppermute | solution.py:148
  16.7 5.1 %collective-permute-done.7.refs_1_.refs_12_ = bf16[208,832]{1,0:T(8,128)(2,1)} collective-permute-done((bf16[208,832]{1,0:T(8,128)(2,1)S(1)}, bf16[208,832]{1,0:T(8,128)(2,1)}, u32[]{:S(2)}, u32[]{:S(2)}) %collective-permute-start.7) | collective-permute-done | bytes 346144 | tf_op jit(solution)/shard_map/ppermute | solution.py:144
  21.8 1.8 %collective-permute-start.8 = (bf16[208,832]{1,0:T(8,128)(2,1)}, bf16[208,832]{1,0:T(8,128)(2,1)}, u32[]{:S(2)}, u32[]{:S(2)}) collective-permute-start(bf16[208,832]{1,0:T(8,128)(2,1)} %collective-permute-done.7.refs_1_.refs_12_), channel_id=1, source_target_pairs={{0,1},{1,0},{2,3},{3,2},{4,5},{5,4},{6,7},{7,6},{8,9},{9,8},{10,11... | collective-permute-start | bytes 1038344 | tf_op jit(solution)/shard_map/ppermute | solution.py:157
  23.6 2.5 %copy.37.refs_0_ = bf16[416,1664]{1,0:T(8,128)(2,1)} copy(bf16[416,1664]{1,0:T(8,128)(2,1)} %refs_16_.1) | data formatting | bytes 2768896
  26.9 1.5 collective-permute-start.9
  28.4 1.6 collective-permute-start.18
  30.0 1.2 constant_dynamic-slice_fusion
  32.4 6.1 %collective-permute-done.9.refs_14_.refs_4_ = bf16[208,832]{1,0:T(8,128)(2,1)S(1)} collective-permute-done((bf16[208,832]{1,0:T(8,128)(2,1)S(1)}, bf16[208,832]{1,0:T(8,128)(2,1)S(1)}, u32[]{:S(2)}, u32[]{:S(2)}) %collective-permute-start.9) | collective-permute-done | bytes 346144 | tf_op jit(solution)/shard_map/ppermute | solution.py:144
  39.5 1.6 collective-permute-start.11
  41.6 6.1 %collective-permute-done.10.refs_16_.refs_0_ = bf16[832,256]{1,0:T(8,128)(2,1)S(1)} collective-permute-done((bf16[832,256]{1,0:T(8,128)(2,1)S(1)}, bf16[832,256]{1,0:T(8,128)(2,1)S(1)}, u32[]{:S(2)}, u32[]{:S(2)}) %collective-permute-start.10) | collective-permute-done | bytes 426016 | tf_op jit(solution)/shard_map/ppermute | solution.py:144
  48.0 14.7 %shard_map.142.refs_0_ = bf16[208,896]{1,0:T(8,128)(2,1)} custom-call(bf16[416,448]{1,0:T(8,128)(2,1)S(1)} %bitcast.52, bf16[416,448]{1,0:T(8,128)(2,1)S(1)} %copy-done.12, bf16[416,448]{1,0:T(8,128)(2,1)} %collective-permute-done.1.refs_2_, bf16[416,448]{1,0:T(8,128)(2,1)} %collective-permute-done.2.refs_3_.refs_1_.refs_5_, ...), custom_call_target="tpu_custom_call" | custom-call | flops 2528641024 | bytes 6533120 | tf_op jit(solution)/shard_map/pallas_call | solution.py:458
  63.6 1.1 collective-permute-start.19
  64.7 1.5 collective-permute-start.14
  66.2 1.5 collective-permute-start.15
  67.7 5.1 %collective-permute-done.14.refs_3_.refs_9_ = bf16[208,896]{1,0:T(8,128)(2,1)S(1)} collective-permute-done((bf16[208,896]{1,0:T(8,128)(2,1)}, bf16[208,896]{1,0:T(8,128)(2,1)S(1)}, u32[]{:S(2)}, u32[]{:S(2)}) %collective-permute-start.14) | collective-permute-done | bytes 372768 | tf_op jit(solution)/shard_map/ppermute | solution.py:148
  72.8 1.3 collective-permute-done.15.refs_2_.refs_10_
  74.2 1.3 collective-permute-start.17
  75.5 1.5 collective-permute-start.20
  77.5 8.9 %collective-permute-done.17.refs_3_.refs_22_.refs_2_ = bf16[832,256]{1,0:T(8,128)(2,1)S(1)} collective-permute-done((bf16[832,256]{1,0:T(8,128)(2,1)S(1)}, bf16[832,256]{1,0:T(8,128)(2,1)S(1)}, u32[]{:S(2)}, u32[]{:S(2)}) %collective-permute-start.17) | collective-permute-done | bytes 426016 | tf_op jit(solution)/shard_map/ppermute | solution.py:157
  87.3 1.6 dynamic-slice_bitcast_fusion
  90.0 1.5 collective-permute-start.27
  92.3 1.2 collective-permute-start.28
  93.6 12.8 %shard_map.148 = (bf16[1664,896]{1,0:T(8,128)(2,1)S(1)}, bf16[416,448]{1,0:T(8,128)(2,1)S(1)}) custom-call(bf16[416,448]{1,0:T(8,128)(2,1)S(1)} %bitcast.53, bf16[416,448]{1,0:T(8,128)(2,1)S(1)} %copy-done.13, bf16[416,448]{1,0:T(8,128)(2,1)} %collective-permute-done.1.refs_2_, bf16[416,448]{1,0:T(8,128)(2,1)} %collective-permute-done.2.refs_3_.refs_1_.refs_5_, ...), custom_call_target="tpu_custom_call" | custom-call | flops 4961861632 | bytes 12360192 | tf_op jit(solution)/shard_map/pallas_call | solution.py:458
  106.4 3.1 %collective-permute-done.27.refs_1_ = bf16[416,832]{1,0:T(8,128)(2,1)S(1)} collective-permute-done((bf16[416,832]{1,0:T(8,128)(2,1)S(1)}, bf16[416,832]{1,0:T(8,128)(2,1)S(1)}, u32[]{:S(2)}, u32[]{:S(2)}) %collective-permute-start.27) | collective-permute-done | bytes 692256 | tf_op jit(solution)/shard_map/ppermute | solution.py:144
  109.5 1.2 collective-permute-start.30
  110.8 5.0 %shard_map.150.hidden = bf16[1024,896]{1,0:T(8,128)(2,1)S(1)} custom-call(bf16[1664,896]{1,0:T(8,128)(2,1)S(1)} %get-tuple-element.45.normed, bf16[832,2048]{1,0:T(8,128)(2,1)S(1)} %copy-done.22, bf16[832,256]{1,0:T(8,128)(2,1)S(1)} %copy-done.32, bf16[832,256]{1,0:T(8,128)(2,1)S(1)} %copy-done.19, bf16[832,256]{1,0:T(8,128)(2,1)S(1)} %copy-done.15, ...), custom_call_target="tpu_custom_call" | custom-call | flops 3053453312 | bytes 8093696 | tf_op jit(solution)/shard_map/pallas_call | solution.py:458
  115.8 3.6 %shard_map.151 = (bf16[2,208,448]{2,1,0:T(8,128)(2,1)S(1)}, bf16[2,208,448]{2,1,0:T(8,128)(2,1)S(1)}, bf16[2,208,448]{2,1,0:T(8,128)(2,1)S(1)}, bf16[2,208,448]{2,1,0:T(8,128)(2,1)S(1)}) custom-call(bf16[1024,896]{1,0:T(8,128)(2,1)S(1)} %shard_map.150.hidden, bf16[832,2048]{1,0:T(8,128)(2,1)S(1)} %bitcast.43, bf16[832,256]{1,0:T(8,128)(2,1)S(1)} %copy-done.6, ...), custom_call_target="tpu_custom_call" | custom-call | flops 1526726656 | bytes 6946816 | tf_op jit(solution)/shard_map/pallas_call | solution.py:458
  120.1 3.6 %shard_map.152 = (bf16[2,208,448]{2,1,0:T(8,128)(2,1)S(1)}, bf16[2,208,448]{2,1,0:T(8,128)(2,1)S(1)}, bf16[2,208,448]{2,1,0:T(8,128)(2,1)S(1)}, bf16[2,208,448]{2,1,0:T(8,128)(2,1)S(1)}) custom-call(bf16[1024,896]{1,0:T(8,128)(2,1)S(1)} %shard_map.150.hidden, bf16[832,2048]{1,0:T(8,128)(2,1)S(1)} %bitcast.44, bf16[832,256]{1,0:T(8,128)(2,1)S(1)} %copy-done.6, ...), custom_call_target="tpu_custom_call" | custom-call | flops 1526726656 | bytes 8437760 | tf_op jit(solution)/shard_map/pallas_call | solution.py:458
  123.7 0.9 collective-permute-done.29.refs_4_.refs_1_
  124.7 1.9 %collective-permute-done.30.refs_5_.refs_2_ = bf16[416,832]{1,0:T(8,128)(2,1)S(1)} collective-permute-done((bf16[416,832]{1,0:T(8,128)(2,1)S(1)}, bf16[416,832]{1,0:T(8,128)(2,1)S(1)}, u32[]{:S(2)}, u32[]{:S(2)}) %collective-permute-start.30) | collective-permute-done | bytes 692256 | tf_op jit(solution)/shard_map/ppermute | solution.py:157
  126.7 1.6 collective-permute-start.33
  129.0 1.2 collective-permute-start.39
  130.2 6.9 %collective-permute-done.33 = bf16[2,208,448]{2,1,0:T(8,128)(2,1)S(1)} collective-permute-done((bf16[2,208,448]{2,1,0:T(8,128)(2,1)S(1)}, bf16[2,208,448]{2,1,0:T(8,128)(2,1)S(1)}, u32[]{:S(2)}, u32[]{:S(2)}) %collective-permute-start.33) | collective-permute-done | bytes 372768 | tf_op jit(solution)/shard_map/ppermute | solution.py:144
  137.1 1.4 collective-permute-done.36
  140.1 4.6 %collective-permute-done.37.last_x = bf16[208,448]{1,0:T(8,128)(2,1)S(1)} collective-permute-done((bf16[208,448]{1,0:T(8,128)(2,1)S(1)}, bf16[208,448]{1,0:T(8,128)(2,1)S(1)}, u32[]{:S(2)}, u32[]{:S(2)}) %collective-permute-start.37) | collective-permute-done | bytes 186400 | tf_op jit(solution)/shard_map/ppermute | solution.py:148
  145.5 1.0 shard_map.154
  146.5 1.3 shard_map.155
  147.9 1.5 collective-permute-done.40
  149.4 1.5 collective-permute-start.41
  150.9 3.6 %collective-permute-done.41 = bf16[416,112]{1,0:T(8,128)(2,1)S(1)} collective-permute-done((bf16[416,112]{1,0:T(8,128)(2,1)S(1)}, bf16[416,112]{1,0:T(8,128)(2,1)S(1)}, u32[]{:S(2)}, u32[]{:S(2)}) %collective-permute-start.41) | collective-permute-done | bytes 93216 | tf_op jit(solution)/shard_map/ppermute | solution.py:148
  154.5 1.2 collective-permute-start.42
  155.8 2.6 %collective-permute-start.43 = (bf16[416,112]{1,0:T(8,128)(2,1)S(1)}, bf16[416,112]{1,0:T(8,128)(2,1)S(1)}, u32[]{:S(2)}, u32[]{:S(2)}) collective-permute-start(bf16[416,112]{1,0:T(8,128)(2,1)S(1)} %fusion.refs_0_), channel_id=1, source_target_pairs={{0,2},{1,3},{2,0},{3,1},{4,6},{5,7},{6,4},{7,5},{8,10},{9,11},{10,... | collective-permute-start | bytes 279560 | tf_op jit(solution)/shard_map/ppermute | solution.py:157
  159.0 1.5 collective-permute-done.42.refs_1_
  160.5 6.0 %collective-permute-done.43.refs_2_ = bf16[416,112]{1,0:T(8,128)(2,1)S(1)} collective-permute-done((bf16[416,112]{1,0:T(8,128)(2,1)S(1)}, bf16[416,112]{1,0:T(8,128)(2,1)S(1)}, u32[]{:S(2)}, u32[]{:S(2)}) %collective-permute-start.43) | collective-permute-done | bytes 93216 | tf_op jit(solution)/shard_map/ppermute | solution.py:157
  (151 shorter events, 13.6 us)
Async XLA Ops:
  0.6 25.5 %copy-start.24 = (bf16[832,416]{0,1:T(8,128)(2,1)S(1)}, bf16[832,416]{0,1:T(8,128)(2,1)}, u32[]{:S(2)}) copy-start(bf16[832,416]{0,1:T(8,128)(2,1)} %param.17) | copy-start | bytes 2076676
  0.6 14.0 %collective-permute-start.1 = (bf16[416,448]{1,0:T(8,128)(2,1)}, bf16[416,448]{1,0:T(8,128)(2,1)}, u32[]{:S(2)}, u32[]{:S(2)}) collective-permute-start(bf16[416,448]{1,0:T(8,128)(2,1)} %bitcast.49), channel_id=1, source_target_pairs={{0,16},{16,0},{1,17},{17,1},{2,18},{18,2},{3,19},{19,3},{4,20},{20... | collective-permute-start | bytes 1118216 | tf_op jit(solution)/shard_map/ppermute | solution.py:144
  4.8 16.9 %collective-permute-start.7 = (bf16[208,832]{1,0:T(8,128)(2,1)S(1)}, bf16[208,832]{1,0:T(8,128)(2,1)}, u32[]{:S(2)}, u32[]{:S(2)}) collective-permute-start(bf16[208,832]{1,0:T(8,128)(2,1)S(1)} %select_bitcast_fusion), channel_id=1, source_target_pairs={{0,16},{16,0},{1,17},{17,1},{2,18},{18,2},{3,19},{19,3},{4,20},{20... | collective-permute-start | bytes 1038344 | tf_op jit(solution)/shard_map/ppermute | solution.py:144
  5.0 21.2 %collective-permute-start = (bf16[416,448]{1,0:T(8,128)(2,1)}, bf16[416,448]{1,0:T(8,128)(2,1)S(1)}, u32[]{:S(2)}, u32[]{:S(2)}) collective-permute-start(bf16[416,448]{1,0:T(8,128)(2,1)} %bitcast.50), channel_id=1, source_target_pairs={{0,8},{4,12},{8,0},{12,4},{1,9},{5,13},{9,1},{13,5},{2,10},{6,14},... | collective-permute-start | bytes 1118216 | tf_op jit(solution)/shard_map/ppermute | solution.py:148
  14.6 13.8 %collective-permute-start.2 = (bf16[416,448]{1,0:T(8,128)(2,1)}, bf16[416,448]{1,0:T(8,128)(2,1)}, u32[]{:S(2)}, u32[]{:S(2)}) collective-permute-start(bf16[416,448]{1,0:T(8,128)(2,1)} %collective-permute-done.1.refs_2_), channel_id=1, source_target_pairs={{0,8},{4,12},{8,0},{12,4},{1,9},{5,13},{9,1},{13,5},{2,10},{6,14},... | collective-permute-start | bytes 1118216 | tf_op jit(solution)/shard_map/ppermute | solution.py:148
  16.7 15.2 %collective-permute-start.3 = (bf16[416,448]{1,0:T(8,128)(2,1)}, bf16[416,448]{1,0:T(8,128)(2,1)}, u32[]{:S(2)}, u32[]{:S(2)}) collective-permute-start(bf16[416,448]{1,0:T(8,128)(2,1)} %bitcast.51), channel_id=1, source_target_pairs={{0,4},{4,0},{8,12},{12,8},{1,5},{5,1},{9,13},{13,9},{2,6},{6,2},{1... | collective-permute-start | bytes 1118216 | tf_op jit(solution)/shard_map/ppermute | solution.py:152
  21.8 10.2 %collective-permute-start.8 = (bf16[208,832]{1,0:T(8,128)(2,1)}, bf16[208,832]{1,0:T(8,128)(2,1)}, u32[]{:S(2)}, u32[]{:S(2)}) collective-permute-start(bf16[208,832]{1,0:T(8,128)(2,1)} %collective-permute-done.7.refs_1_.refs_12_), channel_id=1, source_target_pairs={{0,1},{1,0},{2,3},{3,2},{4,5},{5,4},{6,7},{7,6},{8,9},{9,8},{10,11... | collective-permute-start | bytes 1038344 | tf_op jit(solution)/shard_map/ppermute | solution.py:157
  26.9 11.6 %collective-permute-start.9 = (bf16[208,832]{1,0:T(8,128)(2,1)S(1)}, bf16[208,832]{1,0:T(8,128)(2,1)S(1)}, u32[]{:S(2)}, u32[]{:S(2)}) collective-permute-start(bf16[208,832]{1,0:T(8,128)(2,1)S(1)} %shard_map.140), channel_id=1, source_target_pairs={{0,16},{16,0},{1,17},{17,1},{2,18},{18,2},{3,19},{19,3},{4,20},{20... | collective-permute-start | bytes 1038344 | tf_op jit(solution)/shard_map/ppermute | solution.py:144
  28.4 45.6 %collective-permute-start.18 = (bf16[416,1664]{1,0:T(8,128)(2,1)S(1)}, bf16[416,1664]{1,0:T(8,128)(2,1)}, u32[]{:S(2)}, u32[]{:S(2)}) collective-permute-start(bf16[416,1664]{1,0:T(8,128)(2,1)S(1)} %shard_map.143.refs_9_), channel_id=1, source_target_pairs={{0,8},{4,12},{8,0},{12,4},{1,9},{5,13},{9,1},{13,5},{2,10},{6,14},... | collective-permute-start | bytes 4153352 | tf_op jit(solution)/shard_map/ppermute | solution.py:148
  31.2 16.4 %collective-permute-start.10 = (bf16[832,256]{1,0:T(8,128)(2,1)S(1)}, bf16[832,256]{1,0:T(8,128)(2,1)S(1)}, u32[]{:S(2)}, u32[]{:S(2)}) collective-permute-start(bf16[832,256]{1,0:T(8,128)(2,1)S(1)} %shard_map.141), channel_id=1, source_target_pairs={{0,16},{16,0},{1,17},{17,1},{2,18},{18,2},{3,19},{19,3},{4,20},{20... | collective-permute-start | bytes 1277960 | tf_op jit(solution)/shard_map/ppermute | solution.py:144
  31.9 7.6 %collective-permute-start.5 = (bf16[416,448]{1,0:T(8,128)(2,1)}, bf16[416,448]{1,0:T(8,128)(2,1)S(1)}, u32[]{:S(2)}, u32[]{:S(2)}) collective-permute-start(bf16[416,448]{1,0:T(8,128)(2,1)} %collective-permute-done.1.refs_2_), channel_id=1, source_target_pairs={{0,4},{4,0},{8,12},{12,8},{1,5},{5,1},{9,13},{13,9},{2,6},{6,2},{1... | collective-permute-start | bytes 1118216 | tf_op jit(solution)/shard_map/ppermute | solution.py:152
  31.9 7.5 %collective-permute-start.4 = (bf16[416,448]{1,0:T(8,128)(2,1)S(1)}, bf16[416,448]{1,0:T(8,128)(2,1)S(1)}, u32[]{:S(2)}, u32[]{:S(2)}) collective-permute-start(bf16[416,448]{1,0:T(8,128)(2,1)S(1)} %copy-done.12), channel_id=1, source_target_pairs={{0,4},{4,0},{8,12},{12,8},{1,5},{5,1},{9,13},{13,9},{2,6},{6,2},{1... | collective-permute-start | bytes 1118216 | tf_op jit(solution)/shard_map/ppermute | solution.py:152
  38.6 9.3 %collective-permute-start.6 = (bf16[416,448]{1,0:T(8,128)(2,1)}, bf16[416,448]{1,0:T(8,128)(2,1)S(1)}, u32[]{:S(2)}, u32[]{:S(2)}) collective-permute-start(bf16[416,448]{1,0:T(8,128)(2,1)} %collective-permute-done.2.refs_3_.refs_1_.refs_5_), channel_id=1, source_target_pairs={{0,4},{4,0},{8,12},{12,8},{1,5},{5,1},{9,13},{13,9},{2,6},{6,2},{1... | collective-permute-start | bytes 1118216 | tf_op jit(solution)/shard_map/ppermute | solution.py:152
  39.5 23.2 %copy-start.7 = (bf16[416,448]{1,0:T(8,128)(2,1)}, bf16[416,448]{1,0:T(8,128)(2,1)S(1)}, u32[]{:S(2)}) copy-start(bf16[416,448]{1,0:T(8,128)(2,1)S(1)} %collective-permute-done.5.refs_6_.refs_8_) | copy-start | bytes 1118212
  39.5 23.2 %copy-start.9 = (bf16[416,448]{1,0:T(8,128)(2,1)}, bf16[416,448]{1,0:T(8,128)(2,1)S(1)}, u32[]{:S(2)}) copy-start(bf16[416,448]{1,0:T(8,128)(2,1)S(1)} %collective-permute-done.4.refs_5_.refs_7_) | copy-start | bytes 1118212
  39.5 23.2 %collective-permute-start.11 = (bf16[832,256]{1,0:T(8,128)(2,1)S(1)}, bf16[832,256]{1,0:T(8,128)(2,1)S(1)}, u32[]{:S(2)}, u32[]{:S(2)}) collective-permute-start(bf16[832,256]{1,0:T(8,128)(2,1)S(1)} %get-tuple-element.33), channel_id=1, source_target_pairs={{0,16},{16,0},{1,17},{17,1},{2,18},{18,2},{3,19},{19,3},{4,20},{20... | collective-permute-start | bytes 1277960 | tf_op jit(solution)/shard_map/ppermute | solution.py:144
  41.1 22.5 %collective-permute-start.12 = (bf16[832,256]{1,0:T(8,128)(2,1)S(1)}, bf16[832,256]{1,0:T(8,128)(2,1)S(1)}, u32[]{:S(2)}, u32[]{:S(2)}) collective-permute-start(bf16[832,256]{1,0:T(8,128)(2,1)S(1)} %get-tuple-element.34), channel_id=1, source_target_pairs={{0,16},{16,0},{1,17},{17,1},{2,18},{18,2},{3,19},{19,3},{4,20},{20... | collective-permute-start | bytes 1277960 | tf_op jit(solution)/shard_map/ppermute | solution.py:144
  47.7 15.9 %collective-permute-start.13 = (bf16[832,256]{1,0:T(8,128)(2,1)S(1)}, bf16[832,256]{1,0:T(8,128)(2,1)S(1)}, u32[]{:S(2)}, u32[]{:S(2)}) collective-permute-start(bf16[832,256]{1,0:T(8,128)(2,1)S(1)} %collective-permute-done.10.refs_16_.refs_0_), channel_id=1, source_target_pairs={{0,1},{1,0},{2,3},{3,2},{4,5},{5,4},{6,7},{7,6},{8,9},{9,8},{10,11... | collective-permute-start | bytes 1277960 | tf_op jit(solution)/shard_map/ppermute | solution.py:157
  63.6 10.5 %collective-permute-start.19 = (bf16[832,256]{1,0:T(8,128)(2,1)S(1)}, bf16[832,256]{1,0:T(8,128)(2,1)S(1)}, u32[]{:S(2)}, u32[]{:S(2)}) collective-permute-start(bf16[832,256]{1,0:T(8,128)(2,1)S(1)} %get-tuple-element.38.refs_1_), channel_id=1, source_target_pairs={{0,1},{1,0},{2,3},{3,2},{4,5},{5,4},{6,7},{7,6},{8,9},{9,8},{10,11... | collective-permute-start | bytes 1277960 | tf_op jit(solution)/shard_map/ppermute | solution.py:157
  64.7 8.1 %collective-permute-start.14 = (bf16[208,896]{1,0:T(8,128)(2,1)}, bf16[208,896]{1,0:T(8,128)(2,1)S(1)}, u32[]{:S(2)}, u32[]{:S(2)}) collective-permute-start(bf16[208,896]{1,0:T(8,128)(2,1)} %get-tuple-element.35.refs_8_), channel_id=1, source_target_pairs={{0,8},{4,12},{8,0},{12,4},{1,9},{5,13},{9,1},{13,5},{2,10},{6,14},... | collective-permute-start | bytes 1118216 | tf_op jit(solution)/shard_map/ppermute | solution.py:148
  66.2 7.9 %collective-permute-start.15 = (bf16[208,896]{1,0:T(8,128)(2,1)}, bf16[208,896]{1,0:T(8,128)(2,1)}, u32[]{:S(2)}, u32[]{:S(2)}) collective-permute-start(bf16[208,896]{1,0:T(8,128)(2,1)} %get-tuple-element.35.refs_8_), channel_id=1, source_target_pairs={{0,16},{16,0},{1,17},{17,1},{2,18},{18,2},{3,19},{19,3},{4,20},{20... | collective-permute-start | bytes 1118216 | tf_op jit(solution)/shard_map/ppermute | solution.py:144
  67.7 21.9 %collective-permute-start.25 = (bf16[416,1664]{1,0:T(8,128)(2,1)}, bf16[416,1664]{1,0:T(8,128)(2,1)}, u32[]{:S(2)}, u32[]{:S(2)}) collective-permute-start(bf16[416,1664]{1,0:T(8,128)(2,1)} %refs_16_.1), channel_id=1, source_target_pairs={{0,4},{4,0},{8,12},{12,8},{1,5},{5,1},{9,13},{13,9},{2,6},{6,2},{1... | collective-permute-start | bytes 4153352 | tf_op jit(solution)/shard_map/ppermute | solution.py:152
  74.1 19.5 %collective-permute-start.26 = (bf16[416,1664]{1,0:T(8,128)(2,1)}, bf16[416,1664]{1,0:T(8,128)(2,1)}, u32[]{:S(2)}, u32[]{:S(2)}) collective-permute-start(bf16[416,1664]{1,0:T(8,128)(2,1)} %get-tuple-element.41.refs_17_), channel_id=1, source_target_pairs={{0,4},{4,0},{8,12},{12,8},{1,5},{5,1},{9,13},{13,9},{2,6},{6,2},{1... | collective-permute-start | bytes 4153352 | tf_op jit(solution)/shard_map/ppermute | solution.py:152
  74.2 12.2 %collective-permute-start.17 = (bf16[832,256]{1,0:T(8,128)(2,1)S(1)}, bf16[832,256]{1,0:T(8,128)(2,1)S(1)}, u32[]{:S(2)}, u32[]{:S(2)}) collective-permute-start(bf16[832,256]{1,0:T(8,128)(2,1)S(1)} %get-tuple-element.36.refs_0_), channel_id=1, source_target_pairs={{0,1},{1,0},{2,3},{3,2},{4,5},{5,4},{6,7},{7,6},{8,9},{9,8},{10,11... | collective-permute-start | bytes 1277960 | tf_op jit(solution)/shard_map/ppermute | solution.py:157
  75.5 14.0 %collective-permute-start.20 = (bf16[832,256]{1,0:T(8,128)(2,1)}, bf16[832,256]{1,0:T(8,128)(2,1)}, u32[]{:S(2)}, u32[]{:S(2)}) collective-permute-start(bf16[832,256]{1,0:T(8,128)(2,1)} %get-tuple-element.39), channel_id=1, source_target_pairs={{0,16},{16,0},{1,17},{17,1},{2,18},{18,2},{3,19},{19,3},{4,20},{20... | collective-permute-start | bytes 1277960 | tf_op jit(solution)/shard_map/ppermute | solution.py:144
  77.0 11.9 %collective-permute-start.16 = (bf16[208,896]{1,0:T(8,128)(2,1)}, bf16[208,896]{1,0:T(8,128)(2,1)}, u32[]{:S(2)}, u32[]{:S(2)}) collective-permute-start(bf16[208,896]{1,0:T(8,128)(2,1)} %collective-permute-done.15.refs_2_.refs_10_), channel_id=1, source_target_pairs={{0,8},{4,12},{8,0},{12,4},{1,9},{5,13},{9,1},{13,5},{2,10},{6,14},... | collective-permute-start | bytes 1118216 | tf_op jit(solution)/shard_map/ppermute | solution.py:148
  87.2 2.8 %collective-permute-start.21 = (bf16[208,896]{1,0:T(8,128)(2,1)}, bf16[208,896]{1,0:T(8,128)(2,1)}, u32[]{:S(2)}, u32[]{:S(2)}) collective-permute-start(bf16[208,896]{1,0:T(8,128)(2,1)} %get-tuple-element.35.refs_8_), channel_id=1, source_target_pairs={{0,4},{4,0},{8,12},{12,8},{1,5},{5,1},{9,13},{13,9},{2,6},{6,2},{1... | collective-permute-start | bytes 1118216 | tf_op jit(solution)/shard_map/ppermute | solution.py:152
  88.9 2.6 %collective-permute-start.22 = (bf16[208,896]{1,0:T(8,128)(2,1)S(1)}, bf16[208,896]{1,0:T(8,128)(2,1)S(1)}, u32[]{:S(2)}, u32[]{:S(2)}) collective-permute-start(bf16[208,896]{1,0:T(8,128)(2,1)S(1)} %copy-done.21), channel_id=1, source_target_pairs={{0,4},{4,0},{8,12},{12,8},{1,5},{5,1},{9,13},{13,9},{2,6},{6,2},{1... | collective-permute-start | bytes 1118216 | tf_op jit(solution)/shard_map/ppermute | solution.py:152
  89.5 2.8 %collective-permute-start.23 = (bf16[208,896]{1,0:T(8,128)(2,1)}, bf16[208,896]{1,0:T(8,128)(2,1)S(1)}, u32[]{:S(2)}, u32[]{:S(2)}) collective-permute-start(bf16[208,896]{1,0:T(8,128)(2,1)} %collective-permute-done.15.refs_2_.refs_10_), channel_id=1, source_target_pairs={{0,4},{4,0},{8,12},{12,8},{1,5},{5,1},{9,13},{13,9},{2,6},{6,2},{1... | collective-permute-start | bytes 1118216 | tf_op jit(solution)/shard_map/ppermute | solution.py:152
  89.6 4.0 %collective-permute-start.24 = (bf16[208,896]{1,0:T(8,128)(2,1)}, bf16[208,896]{1,0:T(8,128)(2,1)S(1)}, u32[]{:S(2)}, u32[]{:S(2)}) collective-permute-start(bf16[208,896]{1,0:T(8,128)(2,1)} %get-tuple-element.40.refs_11_), channel_id=1, source_target_pairs={{0,4},{4,0},{8,12},{12,8},{1,5},{5,1},{9,13},{13,9},{2,6},{6,2},{1... | collective-permute-start | bytes 1118216 | tf_op jit(solution)/shard_map/ppermute | solution.py:152
  90.0 19.5 %collective-permute-start.27 = (bf16[416,832]{1,0:T(8,128)(2,1)S(1)}, bf16[416,832]{1,0:T(8,128)(2,1)S(1)}, u32[]{:S(2)}, u32[]{:S(2)}) collective-permute-start(bf16[416,832]{1,0:T(8,128)(2,1)S(1)} %get-tuple-element.44), channel_id=1, source_target_pairs={{0,16},{16,0},{1,17},{17,1},{2,18},{18,2},{3,19},{19,3},{4,20},{20... | collective-permute-start | bytes 2076680 | tf_op jit(solution)/shard_map/ppermute | solution.py:144
  91.5 33.1 %collective-permute-start.29 = (bf16[416,832]{1,0:T(8,128)(2,1)S(1)}, bf16[416,832]{1,0:T(8,128)(2,1)S(1)}, u32[]{:S(2)}, u32[]{:S(2)}) collective-permute-start(bf16[416,832]{1,0:T(8,128)(2,1)S(1)} %get-tuple-element.54), channel_id=1, source_target_pairs={{0,16},{16,0},{1,17},{17,1},{2,18},{18,2},{3,19},{19,3},{4,20},{20... | collective-permute-start | bytes 2076680 | tf_op jit(solution)/shard_map/ppermute | solution.py:144
  92.3 23.5 %collective-permute-start.28 = (bf16[832,256]{1,0:T(8,128)(2,1)}, bf16[832,256]{1,0:T(8,128)(2,1)S(1)}, u32[]{:S(2)}, u32[]{:S(2)}) collective-permute-start(bf16[832,256]{1,0:T(8,128)(2,1)} %collective-permute-done.20.refs_4_.refs_21_.refs_1_), channel_id=1, source_target_pairs={{0,1},{1,0},{2,3},{3,2},{4,5},{5,4},{6,7},{7,6},{8,9},{9,8},{10,11... | collective-permute-start | bytes 1277960 | tf_op jit(solution)/shard_map/ppermute | solution.py:157
  109.5 17.0 %collective-permute-start.30 = (bf16[416,832]{1,0:T(8,128)(2,1)S(1)}, bf16[416,832]{1,0:T(8,128)(2,1)S(1)}, u32[]{:S(2)}, u32[]{:S(2)}) collective-permute-start(bf16[416,832]{1,0:T(8,128)(2,1)S(1)} %get-tuple-element.55.refs_0_), channel_id=1, source_target_pairs={{0,1},{1,0},{2,3},{3,2},{4,5},{5,4},{6,7},{7,6},{8,9},{9,8},{10,11... | collective-permute-start | bytes 2076680 | tf_op jit(solution)/shard_map/ppermute | solution.py:157
  119.5 7.1 %collective-permute-start.32 = (bf16[2,208,448]{2,1,0:T(8,128)(2,1)S(1)}, bf16[2,208,448]{2,1,0:T(8,128)(2,1)S(1)}, u32[]{:S(2)}, u32[]{:S(2)}) collective-permute-start(bf16[2,208,448]{2,1,0:T(8,128)(2,1)S(1)} %get-tuple-element.46.refs_4_), channel_id=1, source_target_pairs={{0,4},{4,0},{8,12},{12,8},{1,5},{5,1},{9,13},{13,9},{2,6},{6,2},{1... | collective-permute-start | bytes 1118216 | tf_op jit(solution)/shard_map/ppermute | solution.py:152
  119.5 8.7 %collective-permute-start.35 = (bf16[2,208,448]{2,1,0:T(8,128)(2,1)S(1)}, bf16[2,208,448]{2,1,0:T(8,128)(2,1)S(1)}, u32[]{:S(2)}, u32[]{:S(2)}) collective-permute-start(bf16[2,208,448]{2,1,0:T(8,128)(2,1)S(1)} %get-tuple-element.47.refs_5_), channel_id=1, source_target_pairs={{0,4},{4,0},{8,12},{12,8},{1,5},{5,1},{9,13},{13,9},{2,6},{6,2},{1... | collective-permute-start | bytes 1118216 | tf_op jit(solution)/shard_map/ppermute | solution.py:152
  120.0 10.1 %collective-permute-start.31 = (bf16[2,208,448]{2,1,0:T(8,128)(2,1)S(1)}, bf16[2,208,448]{2,1,0:T(8,128)(2,1)S(1)}, u32[]{:S(2)}, u32[]{:S(2)}) collective-permute-start(bf16[2,208,448]{2,1,0:T(8,128)(2,1)S(1)} %get-tuple-element.48.refs_6_), channel_id=1, source_target_pairs={{0,4},{4,0},{8,12},{12,8},{1,5},{5,1},{9,13},{13,9},{2,6},{6,2},{1... | collective-permute-start | bytes 1118216 | tf_op jit(solution)/shard_map/ppermute | solution.py:152
  124.7 5.5 %collective-permute-start.34 = (bf16[2,208,448]{2,1,0:T(8,128)(2,1)S(1)}, bf16[2,208,448]{2,1,0:T(8,128)(2,1)S(1)}, u32[]{:S(2)}, u32[]{:S(2)}) collective-permute-start(bf16[2,208,448]{2,1,0:T(8,128)(2,1)S(1)} %get-tuple-element.49.refs_7_), channel_id=1, source_target_pairs={{0,4},{4,0},{8,12},{12,8},{1,5},{5,1},{9,13},{13,9},{2,6},{6,2},{1... | collective-permute-start | bytes 1118216 | tf_op jit(solution)/shard_map/ppermute | solution.py:152
  126.7 10.4 %collective-permute-start.33 = (bf16[2,208,448]{2,1,0:T(8,128)(2,1)S(1)}, bf16[2,208,448]{2,1,0:T(8,128)(2,1)S(1)}, u32[]{:S(2)}, u32[]{:S(2)}) collective-permute-start(bf16[2,208,448]{2,1,0:T(8,128)(2,1)S(1)} %add_convert_fusion.3), channel_id=1, source_target_pairs={{0,16},{16,0},{1,17},{17,1},{2,18},{18,2},{3,19},{19,3},{4,20},{20... | collective-permute-start | bytes 1118216 | tf_op jit(solution)/shard_map/ppermute | solution.py:144
  128.3 10.1 %collective-permute-start.36 = (bf16[2,208,448]{2,1,0:T(8,128)(2,1)S(1)}, bf16[2,208,448]{2,1,0:T(8,128)(2,1)S(1)}, u32[]{:S(2)}, u32[]{:S(2)}) collective-permute-start(bf16[2,208,448]{2,1,0:T(8,128)(2,1)S(1)} %add_convert_fusion.1), channel_id=1, source_target_pairs={{0,8},{4,12},{8,0},{12,4},{1,9},{5,13},{9,1},{13,5},{2,10},{6,14},... | collective-permute-start | bytes 1118216 | tf_op jit(solution)/shard_map/ppermute | solution.py:148
  129.0 17.5 %collective-permute-start.39 = (bf16[416,832]{1,0:T(8,128)(2,1)S(1)}, bf16[416,832]{1,0:T(8,128)(2,1)S(1)}, u32[]{:S(2)}, u32[]{:S(2)}) collective-permute-start(bf16[416,832]{1,0:T(8,128)(2,1)S(1)} %collective-permute-done.29.refs_4_.refs_1_), channel_id=1, source_target_pairs={{0,1},{1,0},{2,3},{3,2},{4,5},{5,4},{6,7},{7,6},{8,9},{9,8},{10,11... | collective-permute-start | bytes 2076680 | tf_op jit(solution)/shard_map/ppermute | solution.py:157
  138.9 5.9 %collective-permute-start.37 = (bf16[208,448]{1,0:T(8,128)(2,1)S(1)}, bf16[208,448]{1,0:T(8,128)(2,1)S(1)}, u32[]{:S(2)}, u32[]{:S(2)}) collective-permute-start(bf16[208,448]{1,0:T(8,128)(2,1)S(1)} %get-tuple-element.72), channel_id=1, source_target_pairs={{0,8},{4,12},{8,0},{12,4},{1,9},{5,13},{9,1},{13,5},{2,10},{6,14},... | collective-permute-start | bytes 559112 | tf_op jit(solution)/shard_map/ppermute | solution.py:148
  139.5 5.9 %collective-permute-start.38 = (bf16[208,448]{1,0:T(8,128)(2,1)S(1)}, bf16[208,448]{1,0:T(8,128)(2,1)S(1)}, u32[]{:S(2)}, u32[]{:S(2)}) collective-permute-start(bf16[208,448]{1,0:T(8,128)(2,1)S(1)} %get-tuple-element.70), channel_id=1, source_target_pairs={{0,16},{16,0},{1,17},{17,1},{2,18},{18,2},{3,19},{19,3},{4,20},{20... | collective-permute-start | bytes 559112 | tf_op jit(solution)/shard_map/ppermute | solution.py:144
  147.8 1.5 collective-permute-start.40
  149.4 5.1 %collective-permute-start.41 = (bf16[416,112]{1,0:T(8,128)(2,1)S(1)}, bf16[416,112]{1,0:T(8,128)(2,1)S(1)}, u32[]{:S(2)}, u32[]{:S(2)}) collective-permute-start(bf16[416,112]{1,0:T(8,128)(2,1)S(1)} %slice_bitcast_fusion.4), channel_id=1, source_target_pairs={{0,8},{4,12},{8,0},{12,4},{1,9},{5,13},{9,1},{13,5},{2,10},{6,14},... | collective-permute-start | bytes 279560 | tf_op jit(solution)/shard_map/ppermute | solution.py:148
  154.5 6.0 %collective-permute-start.42 = (bf16[416,112]{1,0:T(8,128)(2,1)S(1)}, bf16[416,112]{1,0:T(8,128)(2,1)S(1)}, u32[]{:S(2)}, u32[]{:S(2)}) collective-permute-start(bf16[416,112]{1,0:T(8,128)(2,1)S(1)} %fusion.refs_0_), channel_id=1, source_target_pairs={{0,1},{1,0},{2,3},{3,2},{4,5},{5,4},{6,7},{7,6},{8,9},{9,8},{10,11... | collective-permute-start | bytes 279560 | tf_op jit(solution)/shard_map/ppermute | solution.py:157
  155.8 10.7 %collective-permute-start.43 = (bf16[416,112]{1,0:T(8,128)(2,1)S(1)}, bf16[416,112]{1,0:T(8,128)(2,1)S(1)}, u32[]{:S(2)}, u32[]{:S(2)}) collective-permute-start(bf16[416,112]{1,0:T(8,128)(2,1)S(1)} %fusion.refs_0_), channel_id=1, source_target_pairs={{0,2},{1,3},{2,0},{3,1},{4,6},{5,7},{6,4},{7,5},{8,10},{9,11},{10,... | collective-permute-start | bytes 279560 | tf_op jit(solution)/shard_map/ppermute | solution.py:157
  158.4 8.2 %collective-permute-start.44 = (bf16[416,112]{1,0:T(8,128)(2,1)S(1)}, bf16[416,112]{1,0:T(8,128)(2,1)S(1)}, u32[]{:S(2)}, u32[]{:S(2)}) collective-permute-start(bf16[416,112]{1,0:T(8,128)(2,1)S(1)} %fusion.refs_0_), channel_id=1, source_target_pairs={{0,3},{1,2},{2,1},{3,0},{4,7},{5,6},{6,5},{7,4},{8,11},{9,10},{10,... | collective-permute-start | bytes 279560 | tf_op jit(solution)/shard_map/ppermute | solution.py:157
  (35 other events, 332.3 us)
